TPU v7x, 512 devices: a whole 4x4x16 slice. The times are simulated.
512 devices in a mesh: batch: 64 (over y_hi, z, core), tensor: 8 (over y_lo, x).
Axes of the slice: x: 4, y: 4 (y_hi: 2, y_lo: 2; y = y_hi * 2 + y_lo), z: 16, core: 2. Of those that a mesh axis runs over, the one named last changes fastest.
Arguments:
- acts: bfloat16 [8192, 8192], P('batch', 'tensor')
- grads: bfloat16 [8192, 8192], P('batch', 'tensor')
- chosen: int32 [512], replicated, may hold values from 0 to 8191, as said below
- assign: int32 [64], replicated, may hold values from 0 to 63, each once
Outputs:
- scores: float32 [64, 64], P('batch')
Inputs may be any that keep to these rules, and one draw needn't show every extreme that they name: `chosen`: distinct values.
All inputs are finite; a program needn't handle non-finite values.
Results may differ from a plain program's by a relative error of at most 0.0003.
Values may be sent and summed in bfloat16 or wider, within the bound.
No kernel may reach another device: no remote copies, remote signals or barrier semaphores. Data moves between devices by JAX's collectives and lax.ppermute only.
A program may use at most 64 MiB of HBM per device.

v0:
```python
import jax
import jax.numpy as jnp
from jax import lax
from jax.sharding import PartitionSpec as P

D = 8192
NSEL = 512
TOK = 128


def passed_along(block, axis, distance):
    devices = range(lax.axis_size(axis))
    route = [((i - distance) % len(devices), i) for i in devices]
    return lax.ppermute(block, axis, route)


def on_device(acts, grads, chosen, assign):
    row_count = acts.shape[0]
    seq_count = row_count // TOK
    cycle_size = lax.axis_size("batch")
    contract_dims = (((1,), (1,)), ((), ()))
    whole = lax.all_gather(grads, "tensor", axis=1, tiled=True)
    picked = jnp.take(whole, chosen, axis=1)

    def pair_terms(held_acts, held_grads):
        feat_gram = lax.dot_general(
            acts, held_acts, contract_dims, preferred_element_type=jnp.float32
        )
        grad_gram = lax.dot_general(
            picked, held_grads, contract_dims, preferred_element_type=jnp.float32
        )
        return (feat_gram * grad_gram).reshape(seq_count, TOK, seq_count, TOK).sum(axis=(1, 3))

    initial = pair_terms(acts, picked)

    def cycle_step(carried, unused):
        held_acts, held_grads = passed_along((carried[0], carried[1]), "batch", 1)
        return ((held_acts, held_grads), pair_terms(held_acts, held_grads))

    final_state, remaining = lax.scan(cycle_step, (acts, picked), None, length=cycle_size // 2)
    partial_terms = jnp.concatenate([initial[None], remaining], axis=0)
    summed = lax.psum(partial_terms, "tensor")
    pair_grid = lax.all_gather(summed[None], "batch", axis=0, tiled=True)
    own_index = lax.axis_index("batch")
    peer_ids = jnp.arange(cycle_size, dtype=jnp.int32)
    peers_behind = (own_index - peer_ids) % cycle_size
    peers_ahead = (peer_ids - own_index) % cycle_size
    half_cycle = cycle_size // 2
    own_side = pair_grid[own_index][jnp.minimum(peers_behind, half_cycle)]
    peer_side = jnp.transpose(pair_grid[peer_ids, jnp.minimum(peers_ahead, half_cycle)], (0, 2, 1))
    values = jnp.where((peers_behind <= half_cycle)[:, None, None], own_side, peer_side)
    row_sums = jnp.transpose(values, (1, 0, 2)).reshape(seq_count, cycle_size * seq_count)
    norming = 1.0 / (float(TOK) * float(D) * float(NSEL))
    row_vals = row_sums * norming
    return jnp.zeros((seq_count, cycle_size * seq_count), jnp.float32).at[:, assign].set(row_vals)


def solution(mesh):
    placed = (P("batch", "tensor"), P("batch", "tensor"), P(), P())
    return jax.shard_map(
        on_device, mesh=mesh, in_specs=placed, out_specs=P("batch", None), check_vma=False
    )
```

profile of v0, /device:TPU:1, one launch (start us, length us, event | category | flops | bytes accessed | tf_op | source)
XLA Modules:
  0.0 639.9 jit_solution(16808361224059328361)
XLA Ops:
  12.7 46.0 %all-gather.2.cloned.1.call-done = bf16[128,8192]{0,1:T(8,128)(2,1)} async-done(((bf16[128,1024]{0,1:T(8,128)(2,1)}), bf16[128,8192]{0,1:T(8,128)(2,1)}) %all-gather.2.cloned.1.call-update) | async-done | bytes 2097168 | tf_op jit(solution)/shard_map/all_gather | solution.py:22
  63.0 470.0 %while.14 = (s32[]{:T(128)}, bf16[128,1024]{1,0:T(8,128)(2,1)S(1)}, bf16[128,512]{1,0:T(8,128)(2,1)S(1)}, f32[32,1,1]{0,2,1:T(1,128)S(1)}, bf16[128,1024]{1,0:T(...) while((s32[]{:T(128)}, bf16[128,1024]{1,0:T(8,128)(2,1)S(1)}, ...), condition=%wide.region_3.4_spmd, body=%wide.region_1.3_spmd.sunk | while | flops 50364416 | bytes 3276989 | solution.py:40
  63.0 8.8 %collective-permute-start.1 = (bf16[128,512]{1,0:T(8,128)(2,1)S(1)}, bf16[128,512]{1,0:T(8,128)(2,1)S(1)}, u32[]{:S(2)}, u32[]{:S(2)}) collective-permute-start(bf16[128,512]{1,0:T(8,128)(2,1)S(1)} %get-tuple-element.117), channel_id=1, source_target_pairs={{504,0},{0,8},{8,16},{16,24},{24,32},{32,40},{40,48},{48,56},{56,6... | collective-permute-start | bytes 393224 | tf_op jit(solution)/shard_map/while/body/eval_jaxpr/ppermute | solution.py:14
  123.2 7.3 %collective-permute-done.1 = bf16[128,512]{1,0:T(8,128)(2,1)S(1)} collective-permute-done((bf16[128,512]{1,0:T(8,128)(2,1)S(1)}, bf16[128,512]{1,0:T(8,128)(2,1)S(1)}, u32[]{:S(2)}, u32[]{:S(2)}) %collective-permute-start.1) | collective-permute-done | bytes 131104 | tf_op jit(solution)/shard_map/while/body/eval_jaxpr/ppermute | solution.py:14
  138.0 7.3 %collective-permute-done.1 = bf16[128,512]{1,0:T(8,128)(2,1)S(1)} collective-permute-done((bf16[128,512]{1,0:T(8,128)(2,1)S(1)}, bf16[128,512]{1,0:T(8,128)(2,1)S(1)}, u32[]{:S(2)}, u32[]{:S(2)}) %collective-permute-start.1) | collective-permute-done | bytes 131104 | tf_op jit(solution)/shard_map/while/body/eval_jaxpr/ppermute | solution.py:14
  152.8 7.3 %collective-permute-done.1 = bf16[128,512]{1,0:T(8,128)(2,1)S(1)} collective-permute-done((bf16[128,512]{1,0:T(8,128)(2,1)S(1)}, bf16[128,512]{1,0:T(8,128)(2,1)S(1)}, u32[]{:S(2)}, u32[]{:S(2)}) %collective-permute-start.1) | collective-permute-done | bytes 131104 | tf_op jit(solution)/shard_map/while/body/eval_jaxpr/ppermute | solution.py:14
  167.5 7.3 %collective-permute-done.1 = bf16[128,512]{1,0:T(8,128)(2,1)S(1)} collective-permute-done((bf16[128,512]{1,0:T(8,128)(2,1)S(1)}, bf16[128,512]{1,0:T(8,128)(2,1)S(1)}, u32[]{:S(2)}, u32[]{:S(2)}) %collective-permute-start.1) | collective-permute-done | bytes 131104 | tf_op jit(solution)/shard_map/while/body/eval_jaxpr/ppermute | solution.py:14
  197.1 7.3 %collective-permute-done.1 = bf16[128,512]{1,0:T(8,128)(2,1)S(1)} collective-permute-done((bf16[128,512]{1,0:T(8,128)(2,1)S(1)}, bf16[128,512]{1,0:T(8,128)(2,1)S(1)}, u32[]{:S(2)}, u32[]{:S(2)}) %collective-permute-start.1) | collective-permute-done | bytes 131104 | tf_op jit(solution)/shard_map/while/body/eval_jaxpr/ppermute | solution.py:14
  211.8 7.3 %collective-permute-done.1 = bf16[128,512]{1,0:T(8,128)(2,1)S(1)} collective-permute-done((bf16[128,512]{1,0:T(8,128)(2,1)S(1)}, bf16[128,512]{1,0:T(8,128)(2,1)S(1)}, u32[]{:S(2)}, u32[]{:S(2)}) %collective-permute-start.1) | collective-permute-done | bytes 131104 | tf_op jit(solution)/shard_map/while/body/eval_jaxpr/ppermute | solution.py:14
  226.6 7.3 %collective-permute-done.1 = bf16[128,512]{1,0:T(8,128)(2,1)S(1)} collective-permute-done((bf16[128,512]{1,0:T(8,128)(2,1)S(1)}, bf16[128,512]{1,0:T(8,128)(2,1)S(1)}, u32[]{:S(2)}, u32[]{:S(2)}) %collective-permute-start.1) | collective-permute-done | bytes 131104 | tf_op jit(solution)/shard_map/while/body/eval_jaxpr/ppermute | solution.py:14
  241.4 7.3 %collective-permute-done.1 = bf16[128,512]{1,0:T(8,128)(2,1)S(1)} collective-permute-done((bf16[128,512]{1,0:T(8,128)(2,1)S(1)}, bf16[128,512]{1,0:T(8,128)(2,1)S(1)}, u32[]{:S(2)}, u32[]{:S(2)}) %collective-permute-start.1) | collective-permute-done | bytes 131104 | tf_op jit(solution)/shard_map/while/body/eval_jaxpr/ppermute | solution.py:14
  270.9 7.3 %collective-permute-done.1 = bf16[128,512]{1,0:T(8,128)(2,1)S(1)} collective-permute-done((bf16[128,512]{1,0:T(8,128)(2,1)S(1)}, bf16[128,512]{1,0:T(8,128)(2,1)S(1)}, u32[]{:S(2)}, u32[]{:S(2)}) %collective-permute-start.1) | collective-permute-done | bytes 131104 | tf_op jit(solution)/shard_map/while/body/eval_jaxpr/ppermute | solution.py:14
  285.7 7.3 %collective-permute-done.1 = bf16[128,512]{1,0:T(8,128)(2,1)S(1)} collective-permute-done((bf16[128,512]{1,0:T(8,128)(2,1)S(1)}, bf16[128,512]{1,0:T(8,128)(2,1)S(1)}, u32[]{:S(2)}, u32[]{:S(2)}) %collective-permute-start.1) | collective-permute-done | bytes 131104 | tf_op jit(solution)/shard_map/while/body/eval_jaxpr/ppermute | solution.py:14
  300.5 7.3 %collective-permute-done.1 = bf16[128,512]{1,0:T(8,128)(2,1)S(1)} collective-permute-done((bf16[128,512]{1,0:T(8,128)(2,1)S(1)}, bf16[128,512]{1,0:T(8,128)(2,1)S(1)}, u32[]{:S(2)}, u32[]{:S(2)}) %collective-permute-start.1) | collective-permute-done | bytes 131104 | tf_op jit(solution)/shard_map/while/body/eval_jaxpr/ppermute | solution.py:14
  315.2 7.3 %collective-permute-done.1 = bf16[128,512]{1,0:T(8,128)(2,1)S(1)} collective-permute-done((bf16[128,512]{1,0:T(8,128)(2,1)S(1)}, bf16[128,512]{1,0:T(8,128)(2,1)S(1)}, u32[]{:S(2)}, u32[]{:S(2)}) %collective-permute-start.1) | collective-permute-done | bytes 131104 | tf_op jit(solution)/shard_map/while/body/eval_jaxpr/ppermute | solution.py:14
  344.8 7.3 %collective-permute-done.1 = bf16[128,512]{1,0:T(8,128)(2,1)S(1)} collective-permute-done((bf16[128,512]{1,0:T(8,128)(2,1)S(1)}, bf16[128,512]{1,0:T(8,128)(2,1)S(1)}, u32[]{:S(2)}, u32[]{:S(2)}) %collective-permute-start.1) | collective-permute-done | bytes 131104 | tf_op jit(solution)/shard_map/while/body/eval_jaxpr/ppermute | solution.py:14
  359.6 7.3 %collective-permute-done.1 = bf16[128,512]{1,0:T(8,128)(2,1)S(1)} collective-permute-done((bf16[128,512]{1,0:T(8,128)(2,1)S(1)}, bf16[128,512]{1,0:T(8,128)(2,1)S(1)}, u32[]{:S(2)}, u32[]{:S(2)}) %collective-permute-start.1) | collective-permute-done | bytes 131104 | tf_op jit(solution)/shard_map/while/body/eval_jaxpr/ppermute | solution.py:14
  374.3 7.3 %collective-permute-done.1 = bf16[128,512]{1,0:T(8,128)(2,1)S(1)} collective-permute-done((bf16[128,512]{1,0:T(8,128)(2,1)S(1)}, bf16[128,512]{1,0:T(8,128)(2,1)S(1)}, u32[]{:S(2)}, u32[]{:S(2)}) %collective-permute-start.1) | collective-permute-done | bytes 131104 | tf_op jit(solution)/shard_map/while/body/eval_jaxpr/ppermute | solution.py:14
  389.1 7.3 %collective-permute-done.1 = bf16[128,512]{1,0:T(8,128)(2,1)S(1)} collective-permute-done((bf16[128,512]{1,0:T(8,128)(2,1)S(1)}, bf16[128,512]{1,0:T(8,128)(2,1)S(1)}, u32[]{:S(2)}, u32[]{:S(2)}) %collective-permute-start.1) | collective-permute-done | bytes 131104 | tf_op jit(solution)/shard_map/while/body/eval_jaxpr/ppermute | solution.py:14
  448.2 7.3 %collective-permute-done.1 = bf16[128,512]{1,0:T(8,128)(2,1)S(1)} collective-permute-done((bf16[128,512]{1,0:T(8,128)(2,1)S(1)}, bf16[128,512]{1,0:T(8,128)(2,1)S(1)}, u32[]{:S(2)}, u32[]{:S(2)}) %collective-permute-start.1) | collective-permute-done | bytes 131104 | tf_op jit(solution)/shard_map/while/body/eval_jaxpr/ppermute | solution.py:14
  463.0 7.3 %collective-permute-done.1 = bf16[128,512]{1,0:T(8,128)(2,1)S(1)} collective-permute-done((bf16[128,512]{1,0:T(8,128)(2,1)S(1)}, bf16[128,512]{1,0:T(8,128)(2,1)S(1)}, u32[]{:S(2)}, u32[]{:S(2)}) %collective-permute-start.1) | collective-permute-done | bytes 131104 | tf_op jit(solution)/shard_map/while/body/eval_jaxpr/ppermute | solution.py:14
  522.1 7.3 %collective-permute-done.1 = bf16[128,512]{1,0:T(8,128)(2,1)S(1)} collective-permute-done((bf16[128,512]{1,0:T(8,128)(2,1)S(1)}, bf16[128,512]{1,0:T(8,128)(2,1)S(1)}, u32[]{:S(2)}, u32[]{:S(2)}) %collective-permute-start.1) | collective-permute-done | bytes 131104 | tf_op jit(solution)/shard_map/while/body/eval_jaxpr/ppermute | solution.py:14
  533.7 13.6 %psum.7 = f32[1,33,1,1]{1,3,2,0:T(1,128)S(1)} all-reduce(f32[1,33,1,1]{1,3,2,0:T(1,128)S(1)} %maximum_bitcast_fusion), channel_id=1, replica_groups=mesh['batch'=64,'tensor'=8] {'tensor'}, use_global_device_ids=true, to_apply=%region_4.5 | all-reduce | flops 33 | bytes 264 | tf_op jit(solution)/shard_map/psum | solution.py:42
  547.4 82.8 %all_gather.7 = f32[64,33,1,1]{1,3,2,0:T(1,128)S(1)} all-gather(f32[1,33,1,1]{1,3,2,0:T(1,128)S(1)} %psum.7), channel_id=1, replica_groups=mesh['batch'=64,'tensor'=8] {'batch'}, dimensions={0}, use_global_device_ids=true | all-gather | bytes 8580 | tf_op jit(solution)/shard_map/all_gather | solution.py:43
  (293 shorter events, 335.6 us)
Async XLA Ops:
  6.5 52.2 %all-gather.2.cloned.1.call-start = ((), (), s32[]{:S(2)}) async-start(), calls=%async_computation | async-start | bytes 2359296 | tf_op jit(solution)/shard_map/all_gather | solution.py:22
  121.3 11.3 %collective-permute-start = (bf16[128,1024]{1,0:T(8,128)(2,1)S(1)}, bf16[128,1024]{1,0:T(8,128)(2,1)S(1)}, u32[]{:S(2)}, u32[]{:S(2)}) collective-permute-start(bf16[128,1024]{1,0:T(8,128)(2,1)S(1)} %get-tuple-element.116), channel_id=1, source_target_pairs={{504,0},{0,8},{8,16},{16,24},{24,32},{32,40},{40,48},{48,56},{56,6... | collective-permute-start | bytes 786440 | tf_op jit(solution)/shard_map/while/body/eval_jaxpr/ppermute | solution.py:14
  136.1 11.3 %collective-permute-start = (bf16[128,1024]{1,0:T(8,128)(2,1)S(1)}, bf16[128,1024]{1,0:T(8,128)(2,1)S(1)}, u32[]{:S(2)}, u32[]{:S(2)}) collective-permute-start(bf16[128,1024]{1,0:T(8,128)(2,1)S(1)} %get-tuple-element.116), channel_id=1, source_target_pairs={{504,0},{0,8},{8,16},{16,24},{24,32},{32,40},{40,48},{48,56},{56,6... | collective-permute-start | bytes 786440 | tf_op jit(solution)/shard_map/while/body/eval_jaxpr/ppermute | solution.py:14
  150.8 11.3 %collective-permute-start = (bf16[128,1024]{1,0:T(8,128)(2,1)S(1)}, bf16[128,1024]{1,0:T(8,128)(2,1)S(1)}, u32[]{:S(2)}, u32[]{:S(2)}) collective-permute-start(bf16[128,1024]{1,0:T(8,128)(2,1)S(1)} %get-tuple-element.116), channel_id=1, source_target_pairs={{504,0},{0,8},{8,16},{16,24},{24,32},{32,40},{40,48},{48,56},{56,6... | collective-permute-start | bytes 786440 | tf_op jit(solution)/shard_map/while/body/eval_jaxpr/ppermute | solution.py:14
  165.6 11.3 %collective-permute-start = (bf16[128,1024]{1,0:T(8,128)(2,1)S(1)}, bf16[128,1024]{1,0:T(8,128)(2,1)S(1)}, u32[]{:S(2)}, u32[]{:S(2)}) collective-permute-start(bf16[128,1024]{1,0:T(8,128)(2,1)S(1)} %get-tuple-element.116), channel_id=1, source_target_pairs={{504,0},{0,8},{8,16},{16,24},{24,32},{32,40},{40,48},{48,56},{56,6... | collective-permute-start | bytes 786440 | tf_op jit(solution)/shard_map/while/body/eval_jaxpr/ppermute | solution.py:14
  195.1 11.3 %collective-permute-start = (bf16[128,1024]{1,0:T(8,128)(2,1)S(1)}, bf16[128,1024]{1,0:T(8,128)(2,1)S(1)}, u32[]{:S(2)}, u32[]{:S(2)}) collective-permute-start(bf16[128,1024]{1,0:T(8,128)(2,1)S(1)} %get-tuple-element.116), channel_id=1, source_target_pairs={{504,0},{0,8},{8,16},{16,24},{24,32},{32,40},{40,48},{48,56},{56,6... | collective-permute-start | bytes 786440 | tf_op jit(solution)/shard_map/while/body/eval_jaxpr/ppermute | solution.py:14
  209.9 11.3 %collective-permute-start = (bf16[128,1024]{1,0:T(8,128)(2,1)S(1)}, bf16[128,1024]{1,0:T(8,128)(2,1)S(1)}, u32[]{:S(2)}, u32[]{:S(2)}) collective-permute-start(bf16[128,1024]{1,0:T(8,128)(2,1)S(1)} %get-tuple-element.116), channel_id=1, source_target_pairs={{504,0},{0,8},{8,16},{16,24},{24,32},{32,40},{40,48},{48,56},{56,6... | collective-permute-start | bytes 786440 | tf_op jit(solution)/shard_map/while/body/eval_jaxpr/ppermute | solution.py:14
  224.7 11.3 %collective-permute-start = (bf16[128,1024]{1,0:T(8,128)(2,1)S(1)}, bf16[128,1024]{1,0:T(8,128)(2,1)S(1)}, u32[]{:S(2)}, u32[]{:S(2)}) collective-permute-start(bf16[128,1024]{1,0:T(8,128)(2,1)S(1)} %get-tuple-element.116), channel_id=1, source_target_pairs={{504,0},{0,8},{8,16},{16,24},{24,32},{32,40},{40,48},{48,56},{56,6... | collective-permute-start | bytes 786440 | tf_op jit(solution)/shard_map/while/body/eval_jaxpr/ppermute | solution.py:14
  239.5 11.3 %collective-permute-start = (bf16[128,1024]{1,0:T(8,128)(2,1)S(1)}, bf16[128,1024]{1,0:T(8,128)(2,1)S(1)}, u32[]{:S(2)}, u32[]{:S(2)}) collective-permute-start(bf16[128,1024]{1,0:T(8,128)(2,1)S(1)} %get-tuple-element.116), channel_id=1, source_target_pairs={{504,0},{0,8},{8,16},{16,24},{24,32},{32,40},{40,48},{48,56},{56,6... | collective-permute-start | bytes 786440 | tf_op jit(solution)/shard_map/while/body/eval_jaxpr/ppermute | solution.py:14
  269.0 11.3 %collective-permute-start = (bf16[128,1024]{1,0:T(8,128)(2,1)S(1)}, bf16[128,1024]{1,0:T(8,128)(2,1)S(1)}, u32[]{:S(2)}, u32[]{:S(2)}) collective-permute-start(bf16[128,1024]{1,0:T(8,128)(2,1)S(1)} %get-tuple-element.116), channel_id=1, source_target_pairs={{504,0},{0,8},{8,16},{16,24},{24,32},{32,40},{40,48},{48,56},{56,6... | collective-permute-start | bytes 786440 | tf_op jit(solution)/shard_map/while/body/eval_jaxpr/ppermute | solution.py:14
  283.8 11.3 %collective-permute-start = (bf16[128,1024]{1,0:T(8,128)(2,1)S(1)}, bf16[128,1024]{1,0:T(8,128)(2,1)S(1)}, u32[]{:S(2)}, u32[]{:S(2)}) collective-permute-start(bf16[128,1024]{1,0:T(8,128)(2,1)S(1)} %get-tuple-element.116), channel_id=1, source_target_pairs={{504,0},{0,8},{8,16},{16,24},{24,32},{32,40},{40,48},{48,56},{56,6... | collective-permute-start | bytes 786440 | tf_op jit(solution)/shard_map/while/body/eval_jaxpr/ppermute | solution.py:14
  298.5 11.3 %collective-permute-start = (bf16[128,1024]{1,0:T(8,128)(2,1)S(1)}, bf16[128,1024]{1,0:T(8,128)(2,1)S(1)}, u32[]{:S(2)}, u32[]{:S(2)}) collective-permute-start(bf16[128,1024]{1,0:T(8,128)(2,1)S(1)} %get-tuple-element.116), channel_id=1, source_target_pairs={{504,0},{0,8},{8,16},{16,24},{24,32},{32,40},{40,48},{48,56},{56,6... | collective-permute-start | bytes 786440 | tf_op jit(solution)/shard_map/while/body/eval_jaxpr/ppermute | solution.py:14
  313.3 11.3 %collective-permute-start = (bf16[128,1024]{1,0:T(8,128)(2,1)S(1)}, bf16[128,1024]{1,0:T(8,128)(2,1)S(1)}, u32[]{:S(2)}, u32[]{:S(2)}) collective-permute-start(bf16[128,1024]{1,0:T(8,128)(2,1)S(1)} %get-tuple-element.116), channel_id=1, source_target_pairs={{504,0},{0,8},{8,16},{16,24},{24,32},{32,40},{40,48},{48,56},{56,6... | collective-permute-start | bytes 786440 | tf_op jit(solution)/shard_map/while/body/eval_jaxpr/ppermute | solution.py:14
  342.9 11.3 %collective-permute-start = (bf16[128,1024]{1,0:T(8,128)(2,1)S(1)}, bf16[128,1024]{1,0:T(8,128)(2,1)S(1)}, u32[]{:S(2)}, u32[]{:S(2)}) collective-permute-start(bf16[128,1024]{1,0:T(8,128)(2,1)S(1)} %get-tuple-element.116), channel_id=1, source_target_pairs={{504,0},{0,8},{8,16},{16,24},{24,32},{32,40},{40,48},{48,56},{56,6... | collective-permute-start | bytes 786440 | tf_op jit(solution)/shard_map/while/body/eval_jaxpr/ppermute | solution.py:14
  357.6 11.3 %collective-permute-start = (bf16[128,1024]{1,0:T(8,128)(2,1)S(1)}, bf16[128,1024]{1,0:T(8,128)(2,1)S(1)}, u32[]{:S(2)}, u32[]{:S(2)}) collective-permute-start(bf16[128,1024]{1,0:T(8,128)(2,1)S(1)} %get-tuple-element.116), channel_id=1, source_target_pairs={{504,0},{0,8},{8,16},{16,24},{24,32},{32,40},{40,48},{48,56},{56,6... | collective-permute-start | bytes 786440 | tf_op jit(solution)/shard_map/while/body/eval_jaxpr/ppermute | solution.py:14
  372.4 11.3 %collective-permute-start = (bf16[128,1024]{1,0:T(8,128)(2,1)S(1)}, bf16[128,1024]{1,0:T(8,128)(2,1)S(1)}, u32[]{:S(2)}, u32[]{:S(2)}) collective-permute-start(bf16[128,1024]{1,0:T(8,128)(2,1)S(1)} %get-tuple-element.116), channel_id=1, source_target_pairs={{504,0},{0,8},{8,16},{16,24},{24,32},{32,40},{40,48},{48,56},{56,6... | collective-permute-start | bytes 786440 | tf_op jit(solution)/shard_map/while/body/eval_jaxpr/ppermute | solution.py:14
  387.2 11.3 %collective-permute-start = (bf16[128,1024]{1,0:T(8,128)(2,1)S(1)}, bf16[128,1024]{1,0:T(8,128)(2,1)S(1)}, u32[]{:S(2)}, u32[]{:S(2)}) collective-permute-start(bf16[128,1024]{1,0:T(8,128)(2,1)S(1)} %get-tuple-element.116), channel_id=1, source_target_pairs={{504,0},{0,8},{8,16},{16,24},{24,32},{32,40},{40,48},{48,56},{56,6... | collective-permute-start | bytes 786440 | tf_op jit(solution)/shard_map/while/body/eval_jaxpr/ppermute | solution.py:14
  416.7 11.3 %collective-permute-start = (bf16[128,1024]{1,0:T(8,128)(2,1)S(1)}, bf16[128,1024]{1,0:T(8,128)(2,1)S(1)}, u32[]{:S(2)}, u32[]{:S(2)}) collective-permute-start(bf16[128,1024]{1,0:T(8,128)(2,1)S(1)} %get-tuple-element.116), channel_id=1, source_target_pairs={{504,0},{0,8},{8,16},{16,24},{24,32},{32,40},{40,48},{48,56},{56,6... | collective-permute-start | bytes 786440 | tf_op jit(solution)/shard_map/while/body/eval_jaxpr/ppermute | solution.py:14
  431.5 11.3 %collective-permute-start = (bf16[128,1024]{1,0:T(8,128)(2,1)S(1)}, bf16[128,1024]{1,0:T(8,128)(2,1)S(1)}, u32[]{:S(2)}, u32[]{:S(2)}) collective-permute-start(bf16[128,1024]{1,0:T(8,128)(2,1)S(1)} %get-tuple-element.116), channel_id=1, source_target_pairs={{504,0},{0,8},{8,16},{16,24},{24,32},{32,40},{40,48},{48,56},{56,6... | collective-permute-start | bytes 786440 | tf_op jit(solution)/shard_map/while/body/eval_jaxpr/ppermute | solution.py:14
  446.3 11.3 %collective-permute-start = (bf16[128,1024]{1,0:T(8,128)(2,1)S(1)}, bf16[128,1024]{1,0:T(8,128)(2,1)S(1)}, u32[]{:S(2)}, u32[]{:S(2)}) collective-permute-start(bf16[128,1024]{1,0:T(8,128)(2,1)S(1)} %get-tuple-element.116), channel_id=1, source_target_pairs={{504,0},{0,8},{8,16},{16,24},{24,32},{32,40},{40,48},{48,56},{56,6... | collective-permute-start | bytes 786440 | tf_op jit(solution)/shard_map/while/body/eval_jaxpr/ppermute | solution.py:14
  461.0 11.3 %collective-permute-start = (bf16[128,1024]{1,0:T(8,128)(2,1)S(1)}, bf16[128,1024]{1,0:T(8,128)(2,1)S(1)}, u32[]{:S(2)}, u32[]{:S(2)}) collective-permute-start(bf16[128,1024]{1,0:T(8,128)(2,1)S(1)} %get-tuple-element.116), channel_id=1, source_target_pairs={{504,0},{0,8},{8,16},{16,24},{24,32},{32,40},{40,48},{48,56},{56,6... | collective-permute-start | bytes 786440 | tf_op jit(solution)/shard_map/while/body/eval_jaxpr/ppermute | solution.py:14
  490.6 11.3 %collective-permute-start = (bf16[128,1024]{1,0:T(8,128)(2,1)S(1)}, bf16[128,1024]{1,0:T(8,128)(2,1)S(1)}, u32[]{:S(2)}, u32[]{:S(2)}) collective-permute-start(bf16[128,1024]{1,0:T(8,128)(2,1)S(1)} %get-tuple-element.116), channel_id=1, source_target_pairs={{504,0},{0,8},{8,16},{16,24},{24,32},{32,40},{40,48},{48,56},{56,6... | collective-permute-start | bytes 786440 | tf_op jit(solution)/shard_map/while/body/eval_jaxpr/ppermute | solution.py:14
  505.4 11.3 %collective-permute-start = (bf16[128,1024]{1,0:T(8,128)(2,1)S(1)}, bf16[128,1024]{1,0:T(8,128)(2,1)S(1)}, u32[]{:S(2)}, u32[]{:S(2)}) collective-permute-start(bf16[128,1024]{1,0:T(8,128)(2,1)S(1)} %get-tuple-element.116), channel_id=1, source_target_pairs={{504,0},{0,8},{8,16},{16,24},{24,32},{32,40},{40,48},{48,56},{56,6... | collective-permute-start | bytes 786440 | tf_op jit(solution)/shard_map/while/body/eval_jaxpr/ppermute | solution.py:14
  520.1 11.3 %collective-permute-start = (bf16[128,1024]{1,0:T(8,128)(2,1)S(1)}, bf16[128,1024]{1,0:T(8,128)(2,1)S(1)}, u32[]{:S(2)}, u32[]{:S(2)}) collective-permute-start(bf16[128,1024]{1,0:T(8,128)(2,1)S(1)} %get-tuple-element.116), channel_id=1, source_target_pairs={{504,0},{0,8},{8,16},{16,24},{24,32},{32,40},{40,48},{48,56},{56,6... | collective-permute-start | bytes 786440 | tf_op jit(solution)/shard_map/while/body/eval_jaxpr/ppermute | solution.py:14
  (42 other events, 495.8 us)
Sparse Core Ops, SparseCore 0:
  9.4 49.2 all-gather.1
where the time goes:
time: 642 us; the launch traced here: 640 us
  waiting for transfers between devices  325 us (51%)
  starting transfers between devices  135 us (21%)
  blocking collectives  96.5 us (15%)
  matrix products  34.7 us (5%)
  local copies, waits for them, and re-layouts  30.9 us (5%)
  between operations  13.5 us (2%)
    ppermute x64, waiting for transfers between devices, passed_along(): return lax.ppermute(block, axis, route)  279 us
    ppermute x64, starting transfers between devices, passed_along(): return lax.ppermute(block, axis, route)  135 us
    all_gather x1, blocking collectives, on_device(): pair_grid = lax.all_gather(summed[None], 'batch', axis=0, tiled=True)  82.8 us
    all_gather x1, waiting for transfers between devices, on_device(): whole = lax.all_gather(grads, 'tensor', axis=1, tiled=True)  46 us
    dot_general x33, matrix products, pair_terms(): lax.dot_general(acts, held_acts, contract_dims, preferred_element_type=jn...  27.8 us
    dynamic_update_slice x32, local copies, waits for them, and re-layouts, on_device(): lax.scan(cycle_step, (acts, picked), None, length=cycle_size // 2)  21.2 us
    psum x1, blocking collectives, on_device(): summed = lax.psum(partial_terms, 'tensor')  13.6 us
  transfers between devices with their start and end apart: 65, of which 64 were waited for; matrix products, arithmetic and copies ran while one was open for 2% of the time, Pallas kernels for 0%

commit v1 on v0

v1 whole, which is shorter than its diff:
```python
import jax
import jax.numpy as jnp
from jax import lax
from jax.sharding import PartitionSpec as P

D = 8192
NSEL = 512
TOK = 128


def summed_over_tensor(part):
    group = lax.axis_size("tensor")
    rows = part.shape[0] // group
    shares = lax.all_to_all(
        part.reshape(group, rows, part.shape[1]), "tensor", 0, 0, tiled=True
    )
    own = shares.astype(jnp.float32).sum(axis=0).astype(part.dtype)
    copies = jnp.broadcast_to(own[None], (group, rows, part.shape[1]))
    return lax.all_to_all(copies, "tensor", 0, 0, tiled=True).reshape(part.shape)


def on_device(acts, grads, chosen, assign):
    width = grads.shape[1]
    cycle_size = lax.axis_size("batch")
    group = lax.axis_size("tensor")
    local = chosen - lax.axis_index("tensor") * width
    places = lax.broadcasted_iota(jnp.int32, (width, NSEL), 0)
    selector = (places == local[None, :]).astype(grads.dtype)
    part = lax.dot_general(
        grads, selector, (((1,), (0,)), ((), ())), preferred_element_type=jnp.float32
    ).astype(grads.dtype)
    picked = summed_over_tensor(part)

    example_grad = lax.dot_general(
        acts, picked, (((0,), (0,)), ((), ())), preferred_element_type=jnp.float32
    ).astype(acts.dtype)
    shares = lax.all_to_all(
        example_grad.reshape(cycle_size, width // cycle_size, NSEL), "batch", 0, 0, tiled=True
    )
    pairs = lax.dot_general(
        shares, shares, (((1, 2), (1, 2)), ((), ())), preferred_element_type=jnp.float32
    )
    rows = lax.all_to_all(pairs[:, None, :], "batch", 0, 0, tiled=True).sum(axis=0)
    rows = jnp.broadcast_to(rows[None], (group, 1, cycle_size))
    row = lax.all_to_all(rows, "tensor", 0, 0, tiled=True).sum(axis=0)
    norming = 1.0 / (float(TOK) * float(D) * float(NSEL))
    slots = lax.broadcasted_iota(jnp.int32, (cycle_size, cycle_size), 0)
    placed = jnp.where(slots == assign[None, :], row * norming, 0.0)
    return placed.sum(axis=1)[None]


def solution(mesh):
    placed = (P("batch", "tensor"), P("batch", "tensor"), P(), P())
    return jax.shard_map(
        on_device, mesh=mesh, in_specs=placed, out_specs=P("batch", None), check_vma=False
    )
```

time: 642 us -> 130 us (0.20)
  waiting for transfers between devices: 325 us -> 0 us
  starting transfers between devices: 135 us -> 0 us
  matrix products: 34.7 us -> 4.16 us
  local copies, waits for them, and re-layouts: 30.9 us -> 0.57 us
  blocking collectives: 96.5 us -> 124 us
  between operations: 13.5 us -> 0.05 us
    ppermute x64 -> x0, waiting for transfers between devices: 279 us -> none  [passed_along(): return lax.ppermute(block, axis, route)]
    ppermute x64 -> x0, starting transfers between devices: 135 us -> none  [passed_along(): return lax.ppermute(block, axis, route)]
    all_to_all x0 -> x5, blocking collectives: none -> 124 us  [the longest x1 73 us: on_device(): lax.all_to_all(example_grad.reshape(cycle_size, width // cycle_size, NSEL...]
    all_gather x1 -> x0, blocking collectives: 82.8 us -> none  [on_device(): pair_grid = lax.all_gather(summed[None], 'batch', axis=0, tiled=True)]
    all_gather x1 -> x0, waiting for transfers between devices: 46 us -> none  [on_device(): whole = lax.all_gather(grads, 'tensor', axis=1, tiled=True)]
    dot_general x66 -> x3, matrix products: 34.7 us -> 4.16 us  [the longest x1 2.26 us: on_device(): lax.dot_general(shares, shares, (((1, 2), (1, 2)), ((), ())), preferred_e...]
    dynamic_update_slice x32 -> x0, local copies, waits for them, and re-layouts: 21.2 us -> none  [on_device(): lax.scan(cycle_step, (acts, picked), None, length=cycle_size // 2)]
    psum x1 -> x0, blocking collectives: 13.6 us -> none  [on_device(): summed = lax.psum(partial_terms, 'tensor')]
  transfers between devices with their start and end apart: 65 -> 0, of which waited for: 64 -> 0; matrix products, arithmetic and copies ran while one was open for 2% -> 0% of each run, Pallas kernels for 0% -> 0%
where the time goes in v1:
time: 130 us
  blocking collectives  124 us (95%)
  matrix products  4.16 us (3%)
  other arithmetic  1.49 us (1%)
    all_to_all x1, blocking collectives, on_device(): lax.all_to_all(example_grad.reshape(cycle_size, width // cycle_size, NSEL...  73 us
    all_to_all x1, blocking collectives, on_device(): lax.all_to_all(pairs[:, None, :], 'batch', 0, 0, tiled=True).sum(axis=0)  24.2 us
    all_to_all x1, blocking collectives, summed_over_tensor(): lax.all_to_all(part.reshape(group, rows, part.shape[1]), 'tensor', 0, 0,...  11.1 us
    all_to_all x1, blocking collectives, summed_over_tensor(): lax.all_to_all(copies, 'tensor', 0, 0, tiled=True).reshape(part.shape)  7.83 us
    all_to_all x1, blocking collectives, on_device(): row = lax.all_to_all(rows, 'tensor', 0, 0, tiled=True).sum(axis=0)  7.36 us

profile of v1, /device:TPU:1, one launch (start us, length us, event | category | flops | bytes accessed | tf_op | source)
XLA Modules:
  0.0 129.8 jit_solution(3178487032901148769)
XLA Ops:
  0.0 0.0 copy-start
  0.0 0.7 broadcast_subtract_fusion
  0.7 1.4 %fusion.2 = bf16[512,128]{0,1:T(8,128)(2,1)S(1)} fusion(bf16[128,1024]{1,0:T(8,128)(2,1)} %param.5, s32[512]{0:T(512)S(1)} %broadcast_subtract_fusion), kind=kOutput, calls=%fused_computation.4 | convolution fusion | flops 134807552 | bytes 395264 | tf_op jit(solution)/shard_map/dot_general | solution.py:29
  2.2 11.1 %all_to_all.25 = bf16[8,16,512]{2,1,0:T(8,128)(2,1)S(1)} all-to-all(bf16[8,16,512]{2,1,0:T(8,128)(2,1)S(1)} %bitcast.18), channel_id=1, replica_groups=mesh['batch'=64,'tensor'=8] {'tensor'}, dimensions={0} | all-to-all | bytes 262144 | tf_op jit(solution)/shard_map/all_to_all | solution.py:14
  13.3 7.8 %all_to_all.26 = bf16[8,16,512]{2,1,0:T(8,128)(2,1)S(1)} all-to-all(bf16[8,16,512]{2,1,0:T(8,128)(2,1)S(1)} %broadcast_in_dim.32), channel_id=1, replica_groups=mesh['batch'=64,'tensor'=8] {'tensor'}, dimensions={0} | all-to-all | bytes 262144 | tf_op jit(solution)/shard_map/all_to_all | solution.py:19
  21.1 0.0 copy-done
  21.1 0.5 fusion.1
  21.6 0.5 copy.16
  22.2 73.0 %all_to_all.27 = bf16[64,16,512]{2,1,0:T(8,128)(2,1)S(1)} all-to-all(bf16[64,16,512]{2,1,0:T(8,128)(2,1)S(1)} %bitcast.16), channel_id=1, replica_groups=mesh['batch'=64,'tensor'=8] {'batch'}, dimensions={0} | all-to-all | bytes 2097152 | tf_op jit(solution)/shard_map/all_to_all | solution.py:37
  95.2 0.0 copy-start.1
  95.2 2.3 %fusion.3 = f32[64,64,1]{1,0,2:T(8,128)S(1)} fusion(bf16[64,16,512]{2,1,0:T(8,128)(2,1)S(1)} %all_to_all.27), kind=kOutput, calls=%fused_computation.5 | convolution fusion | flops 67108864 | bytes 1064960 | tf_op jit(solution)/shard_map/dot_general | solution.py:40
  97.5 24.2 %all_to_all.28 = f32[64,1,64]{2,1,0:T(1,128)S(1)} all-to-all(f32[64,1,64]{2,1,0:T(1,128)S(1)} %bitcast.19), channel_id=1, replica_groups=mesh['batch'=64,'tensor'=8] {'batch'}, dimensions={0} | all-to-all | bytes 32768 | tf_op jit(solution)/shard_map/all_to_all | solution.py:43
  121.7 0.1 reduce_sum.40
  121.8 7.4 %all_to_all.29 = f32[8,1,64]{2,1,0:T(1,128)S(1)} all-to-all(f32[8,1,64]{2,1,0:T(1,128)S(1)} %broadcast_in_dim.34), channel_id=1, replica_groups=mesh['batch'=64,'tensor'=8] {'tensor'}, dimensions={0} | all-to-all | bytes 4096 | tf_op jit(solution)/shard_map/all_to_all | solution.py:45
  129.2 0.0 copy-done.1
  129.2 0.6 select_reduce_fusion
  (5 shorter events, 0.1 us)
Async XLA Ops:
  0.0 21.1 %copy-start = (bf16[128,1024]{1,0:T(8,128)(2,1)S(1)}, bf16[128,1024]{1,0:T(8,128)(2,1)}, u32[]{:S(2)}) copy-start(bf16[128,1024]{1,0:T(8,128)(2,1)} %param.4) | copy-start | bytes 786436
  95.2 34.0 %copy-start.1 = (s32[64]{0:T(128)S(1)}, s32[64]{0:T(128)}, u32[]{:S(2)}) copy-start(s32[64]{0:T(128)} %param.7) | copy-start | bytes 772

commit v2 on v1

v2 whole, which is shorter than its diff:
```python
import jax
import jax.numpy as jnp
from jax import lax
from jax.experimental import pallas as pl
from jax.experimental.pallas import tpu as pltpu
from jax.sharding import PartitionSpec as P

D = 8192
NSEL = 512
TOK = 128
Y_HI, QUARTERS, RUN, CORES = 2, 4, 4, 2
SIDES = Y_HI * CORES
MEMBERS = RUN * SIDES
TENSOR = 8
WIDTH = D // TENSOR
PART = WIDTH // QUARTERS
ROWS = PART // MEMBERS
TROWS = TOK // TENSOR


def batch_index(y_hi, quarter, place, core):
    return ((y_hi * QUARTERS + quarter) * RUN + place) * CORES + core


def to_quarter(block, distance):
    route = [
        (batch_index(y, q, r, c), batch_index(y, (q + distance) % QUARTERS, r, c))
        for y in range(Y_HI)
        for q in range(QUARTERS)
        for r in range(RUN)
        for c in range(CORES)
    ]
    return lax.ppermute(block, "batch", route)


def run_groups():
    return [
        [batch_index(y, q, r, c) for r in range(RUN) for y in range(Y_HI) for c in range(CORES)]
        for q in range(QUARTERS)
    ]


def column_groups():
    return [
        [batch_index(y, q, r, c) for q in range(QUARTERS) for r in range(RUN)]
        for y in range(Y_HI)
        for c in range(CORES)
    ]


def plane_groups():
    return [
        [
            batch_index(y, q, r, c) * TENSOR + t
            for y in range(Y_HI)
            for c in range(CORES)
            for t in range(TENSOR)
        ]
        for q in range(QUARTERS)
        for r in range(RUN)
    ]


def example_grads_kernel(quarter_ref, acts_ref, first_ref, second_ref, third_ref, picked_ref, out_ref):
    quarter = quarter_ref[0]
    for distance in range(QUARTERS):
        if distance == 0:
            acts = acts_ref[:, pl.ds(pl.multiple_of(quarter * PART, PART), PART)]
        else:
            acts = (first_ref, second_ref, third_ref)[distance - 1][...]
        picked = picked_ref[:, distance].reshape(TOK, NSEL)
        grad = lax.dot_general(
            acts, picked, (((0,), (0,)), ((), ())), preferred_element_type=jnp.float32
        ).astype(out_ref.dtype)
        origin = lax.rem(quarter + QUARTERS - distance, QUARTERS)
        out_ref[:, pl.ds(origin, 1)] = grad.reshape(MEMBERS, 1, ROWS, NSEL)


def example_grads(quarter, acts, others, picked):
    smem = pl.BlockSpec(memory_space=pltpu.SMEM)
    vmem = pl.BlockSpec(memory_space=pltpu.VMEM)
    return pl.pallas_call(
        example_grads_kernel,
        out_shape=jax.ShapeDtypeStruct((MEMBERS, QUARTERS, ROWS, NSEL), acts.dtype),
        in_specs=[smem] + [vmem] * 5,
        out_specs=vmem,
        compiler_params=pltpu.CompilerParams(vmem_limit_bytes=16 * 1024 * 1024),
        cost_estimate=pl.CostEstimate(
            flops=2 * QUARTERS * PART * TOK * NSEL, bytes_accessed=2 * 1024 * 1024, transcendentals=0
        ),
    )(quarter[None], acts, *others, picked)


def on_device(acts, grads, chosen, assign):
    quarter = lax.rem(lax.axis_index("batch") // (RUN * CORES), QUARTERS)
    local = chosen - lax.axis_index("tensor") * WIDTH
    places = lax.broadcasted_iota(jnp.int32, (WIDTH, NSEL), 0)
    selector = (places == local[None, :]).astype(grads.dtype)
    part = lax.dot_general(
        grads, selector, (((1,), (0,)), ((), ())), preferred_element_type=jnp.float32
    ).astype(grads.dtype)
    shares = lax.all_to_all(part.reshape(TENSOR, TROWS, NSEL), "tensor", 0, 0, tiled=True)
    own = shares.astype(jnp.float32).sum(axis=0).astype(part.dtype)

    chunks = [own] + [to_quarter(own, distance) for distance in range(1, QUARTERS)]
    others = []
    for distance in range(1, QUARTERS):
        there = lax.rem(quarter + distance, QUARTERS)
        others.append(to_quarter(lax.dynamic_slice(acts, (0, there * PART), (TOK, PART)), distance))
    copies = jnp.broadcast_to(jnp.stack(chunks)[None], (TENSOR, QUARTERS, TROWS, NSEL))
    picked = lax.all_to_all(copies, "tensor", 0, 0, tiled=True)

    terms = example_grads(quarter, acts, others, picked)
    terms = lax.all_to_all(terms, "batch", 0, 0, axis_index_groups=run_groups(), tiled=True)
    terms = terms.reshape(MEMBERS * QUARTERS, ROWS, NSEL)
    pairs = lax.dot_general(
        terms, terms, (((1, 2), (1, 2)), ((), ())), preferred_element_type=jnp.float32
    )
    rows = pairs.reshape(RUN, SIDES, QUARTERS, RUN * SIDES * QUARTERS)
    rows = jnp.transpose(rows, (2, 0, 1, 3)).reshape(QUARTERS * RUN, SIDES, RUN * SIDES * QUARTERS)
    rows = lax.all_to_all(rows, "batch", 0, 0, axis_index_groups=column_groups(), tiled=True).sum(axis=0)
    rows = jnp.broadcast_to(rows[:, None], (SIDES, TENSOR, rows.shape[1]))
    rows = rows.reshape(SIDES * TENSOR, 1, rows.shape[2])
    row = lax.all_to_all(
        rows, ("batch", "tensor"), 0, 0, axis_index_groups=plane_groups(), tiled=True
    ).sum(axis=(0, 1))

    ids = assign.reshape(Y_HI, QUARTERS, RUN, CORES)
    ids = jnp.transpose(ids, (2, 0, 3, 1)).reshape(-1)
    norming = 1.0 / (float(TOK) * float(D) * float(NSEL))
    slots = lax.broadcasted_iota(jnp.int32, (ids.shape[0], ids.shape[0]), 0)
    placed = jnp.where(slots == ids[None, :], row * norming, 0.0)
    return placed.sum(axis=1)[None]


def solution(mesh):
    placed = (P("batch", "tensor"), P("batch", "tensor"), P(), P())
    return jax.shard_map(
        on_device, mesh=mesh, in_specs=placed, out_specs=P("batch", None), check_vma=False
    )
```

time: 130 us -> 144 us (1.11)
  blocking collectives: 124 us -> 65.6 us
  starting transfers between devices: 0 us -> 48.9 us
  waiting for transfers between devices: 0 us -> 20 us
  local copies, waits for them, and re-layouts: 0.57 us -> 2.79 us
    all_to_all x5 -> x3, blocking collectives: 124 us -> 65.6 us  [the longest x1 36.4 us: on_device(): lax.all_to_all(terms, 'batch', 0, 0, axis_index_groups=run_groups(), tile...]
    ppermute x0 -> x6, starting transfers between devices: none -> 38.9 us  [to_quarter(): return lax.ppermute(block, 'batch', route)]
    ppermute x0 -> x6, waiting for transfers between devices: none -> 13.4 us  [to_quarter(): return lax.ppermute(block, 'batch', route)]
    all_to_all x0 -> x2, starting transfers between devices: none -> 9.98 us  [the longest x1 6.49 us: on_device(): lax.all_to_all(rows, ('batch', 'tensor'), 0, 0, axis_index_groups=plane_g...]
    all_to_all x0 -> x2, waiting for transfers between devices: none -> 6.51 us  [the longest x1 6.51 us: on_device(): lax.all_to_all(rows, ('batch', 'tensor'), 0, 0, axis_index_groups=plane_g...]
  transfers between devices with their start and end apart: 0 -> 8, of which waited for: 0 -> 4; matrix products, arithmetic and copies ran while one was open for 0% -> 0% of each run, Pallas kernels for 0% -> 0%
where the time goes in v2:
time: 144 us; the launch traced here: 143 us
  blocking collectives  65.6 us (46%)
  starting transfers between devices  48.9 us (34%)
  waiting for transfers between devices  20 us (14%)
  matrix products  3.02 us (2%)
  local copies, waits for them, and re-layouts  2.79 us (2%)
  other arithmetic  2.16 us (2%)
    ppermute x6, starting transfers between devices, to_quarter(): return lax.ppermute(block, 'batch', route)  38.9 us
    all_to_all x1, blocking collectives, on_device(): lax.all_to_all(terms, 'batch', 0, 0, axis_index_groups=run_groups(), tile...  36.4 us
    all_to_all x1, blocking collectives, on_device(): lax.all_to_all(rows, 'batch', 0, 0, axis_index_groups=column_groups(), ti...  18.1 us
    ppermute x6, waiting for transfers between devices, to_quarter(): return lax.ppermute(block, 'batch', route)  13.4 us
    all_to_all x1, blocking collectives, on_device(): lax.all_to_all(part.reshape(TENSOR, TROWS, NSEL), 'tensor', 0, 0, tiled=T...  11.1 us
    all_to_all x1, waiting for transfers between devices, on_device(): lax.all_to_all(rows, ('batch', 'tensor'), 0, 0, axis_index_groups=plane_g...  6.51 us
    all_to_all x1, starting transfers between devices, on_device(): lax.all_to_all(rows, ('batch', 'tensor'), 0, 0, axis_index_groups=plane_g...  6.49 us
    all_to_all x1, starting transfers between devices, on_device(): picked = lax.all_to_all(copies, 'tensor', 0, 0, tiled=True)  3.49 us
  transfers between devices with their start and end apart: 8, of which 4 were waited for; matrix products, arithmetic and copies ran while one was open for 0% of the time, Pallas kernels for 0%

profile of v2, /device:TPU:1, one launch (start us, length us, event | category | flops | bytes accessed | tf_op | source)
XLA Modules:
  0.0 143.1 jit_solution(16210734846706515325)
XLA Ops:
  0.0 0.7 broadcast_subtract_fusion
  1.0 0.5 fusion.1
  1.5 11.1 %all_to_all.25 = bf16[8,16,512]{2,1,0:T(8,128)(2,1)S(1)} all-to-all(bf16[8,16,512]{2,1,0:T(8,128)(2,1)S(1)} %bitcast.24), channel_id=1, replica_groups=mesh['batch'=64,'tensor'=8] {'tensor'}, dimensions={0} | all-to-all | bytes 262144 | tf_op jit(solution)/shard_map/all_to_all | solution.py:102
  12.6 9.0 %collective-permute-start.3 = (bf16[16,512]{1,0:T(8,128)(2,1)S(1)}, bf16[16,512]{1,0:T(8,128)(2,1)S(1)}, u32[]{:S(2)}, u32[]{:S(2)}) collective-permute-start(bf16[16,512]{1,0:T(8,128)(2,1)S(1)} %reduce_sum.39), channel_id=1, source_target_pairs={{0,64},{8,72},{16,80},{24,88},{32,96},{40,104},{48,112},{56,120},{... | collective-permute-start | bytes 49160 | tf_op jit(solution)/shard_map/ppermute | solution.py:33
  21.6 10.6 %collective-permute-start.4 = (bf16[16,512]{1,0:T(8,128)(2,1)S(1)}, bf16[16,512]{1,0:T(8,128)(2,1)S(1)}, u32[]{:S(2)}, u32[]{:S(2)}) collective-permute-start(bf16[16,512]{1,0:T(8,128)(2,1)S(1)} %reduce_sum.39), channel_id=1, source_target_pairs={{0,128},{8,136},{16,144},{24,152},{32,160},{40,168},{48,176},{56,1... | collective-permute-start | bytes 49160 | tf_op jit(solution)/shard_map/ppermute | solution.py:33
  32.2 5.2 %collective-permute-start.5 = (bf16[16,512]{1,0:T(8,128)(2,1)S(1)}, bf16[16,512]{1,0:T(8,128)(2,1)S(1)}, u32[]{:S(2)}, u32[]{:S(2)}) collective-permute-start(bf16[16,512]{1,0:T(8,128)(2,1)S(1)} %reduce_sum.39), channel_id=1, source_target_pairs={{0,192},{8,200},{16,208},{24,216},{32,224},{40,232},{48,240},{56,2... | collective-permute-start | bytes 49160 | tf_op jit(solution)/shard_map/ppermute | solution.py:33
  37.4 3.2 %collective-permute-done.5 = bf16[16,512]{1,0:T(8,128)(2,1)S(1)} collective-permute-done((bf16[16,512]{1,0:T(8,128)(2,1)S(1)}, bf16[16,512]{1,0:T(8,128)(2,1)S(1)}, u32[]{:S(2)}, u32[]{:S(2)}) %collective-permute-start.5) | collective-permute-done | bytes 16416 | tf_op jit(solution)/shard_map/ppermute | solution.py:33
  40.6 0.8 broadcast_in_dim.28
  41.5 3.5 %all-to-all-start.1 = ((bf16[8,4,16,512]{3,2,1,0:T(8,128)(2,1)}), bf16[8,4,16,512]{3,2,1,0:T(8,128)(2,1)S(1)}, u32[]{:S(2)}, u32[]{:S(2)}) async-start(bf16[8,4,16,512]{3,2,1,0:T(8,128)(2,1)} %broadcast_in_dim.28), calls=%async_computation.1 | async-start | bytes 1048576 | tf_op jit(solution)/shard_map/all_to_all | solution.py:111
  45.1 3.0 %collective-permute-start = (bf16[128,256]{1,0:T(8,128)(2,1)S(1)}, bf16[128,256]{1,0:T(8,128)(2,1)S(1)}, u32[]{:S(2)}, u32[]{:S(2)}) collective-permute-start(bf16[128,256]{1,0:T(8,128)(2,1)S(1)} %get-tuple-element.7), channel_id=1, source_target_pairs={{0,64},{8,72},{16,80},{24,88},{32,96},{40,104},{48,112},{56,120},{... | collective-permute-start | bytes 196616 | tf_op jit(solution)/shard_map/ppermute | solution.py:33
  48.1 9.2 %collective-permute-start.1 = (bf16[128,256]{1,0:T(8,128)(2,1)S(1)}, bf16[128,256]{1,0:T(8,128)(2,1)S(1)}, u32[]{:S(2)}, u32[]{:S(2)}) collective-permute-start(bf16[128,256]{1,0:T(8,128)(2,1)S(1)} %get-tuple-element.6), channel_id=1, source_target_pairs={{0,128},{8,136},{16,144},{24,152},{32,160},{40,168},{48,176},{56,1... | collective-permute-start | bytes 196616 | tf_op jit(solution)/shard_map/ppermute | solution.py:33
  57.3 1.9 %collective-permute-start.2 = (bf16[128,256]{1,0:T(8,128)(2,1)S(1)}, bf16[128,256]{1,0:T(8,128)(2,1)S(1)}, u32[]{:S(2)}, u32[]{:S(2)}) collective-permute-start(bf16[128,256]{1,0:T(8,128)(2,1)S(1)} %get-tuple-element.5), channel_id=1, source_target_pairs={{0,192},{8,200},{16,208},{24,216},{32,224},{40,232},{48,240},{56,2... | collective-permute-start | bytes 196616 | tf_op jit(solution)/shard_map/ppermute | solution.py:33
  59.2 3.9 %collective-permute-done.1.second_ref = bf16[128,256]{1,0:T(8,128)(2,1)S(1)} collective-permute-done((bf16[128,256]{1,0:T(8,128)(2,1)S(1)}, bf16[128,256]{1,0:T(8,128)(2,1)S(1)}, u32[]{:S(2)}, u32[]{:S(2)}) %collective-permute-start.1) | collective-permute-done | bytes 65568 | tf_op jit(solution)/shard_map/ppermute | solution.py:33
  63.2 6.3 %collective-permute-done.2.third_ref = bf16[128,256]{1,0:T(8,128)(2,1)S(1)} collective-permute-done((bf16[128,256]{1,0:T(8,128)(2,1)S(1)}, bf16[128,256]{1,0:T(8,128)(2,1)S(1)}, u32[]{:S(2)}, u32[]{:S(2)}) %collective-permute-start.2) | collective-permute-done | bytes 65568 | tf_op jit(solution)/shard_map/ppermute | solution.py:33
  69.5 0.5 shard_map.46
  69.9 36.4 %all_to_all.26 = bf16[16,4,16,512]{3,2,1,0:T(8,128)(2,1)S(1)} all-to-all(bf16[16,4,16,512]{3,2,1,0:T(8,128)(2,1)S(1)} %shard_map.46), channel_id=1, replica_groups={{0,8,256,264,16,24,272,280,32,40,288,296,48,56,304,312},{64,72,320,328,..., dimensions={0} | all-to-all | bytes 2097152 | tf_op jit(solution)/shard_map/all_to_all | solution.py:114
  106.4 2.5 %convolution_bitcast_fusion = f32[4,4,4,64]{3,0,2,1:T(4,128)S(1)} fusion(bf16[64,16,512,1,1]{2,1,0,4,3:T(8,128)(2,1)S(1)} %bitcast.22, bf16[4,4,4,16,512]{4,3,2,1,0:T(8,128)(2,1)S(1)} %bitcast.23), kind=kOutput, calls=%fused_computation.3 | convolution fusion | flops 67108864 | bytes 2113536 | tf_op jit(solution)/shard_map/dot_general | solution.py:116
  109.0 18.1 %all_to_all.27 = f32[16,1,256]{2,1,0:T(1,128)S(1)} all-to-all(f32[16,1,256]{2,1,0:T(1,128)S(1)} %reshape.29), channel_id=1, replica_groups={{0,16,32,48,64,80,96,112,128,144,160,176,192,208,224,240},{8,24,40,56,7..., dimensions={0} | all-to-all | bytes 32768 | tf_op jit(solution)/shard_map/all_to_all | solution.py:121
  127.2 0.5 broadcast.8
  127.7 0.7 reduce.1
  128.5 0.6 broadcast_in_dim.29
  129.1 6.5 %all-to-all-start.4 = ((f32[32,1,64]{2,1,0:T(1,128)}), f32[32,1,64]{2,1,0:T(1,128)S(1)}, u32[]{:S(2)}, u32[]{:S(2)}) async-start(f32[32,1,64]{2,1,0:T(1,128)} %bitcast.15), calls=%async_computation.4 | async-start | bytes 32768 | tf_op jit(solution)/shard_map/all_to_all | solution.py:124
  135.9 6.5 %all-to-all-done.4 = f32[32,1,64]{2,1,0:T(1,128)S(1)} async-done(((f32[32,1,64]{2,1,0:T(1,128)}), f32[32,1,64]{2,1,0:T(1,128)S(1)}, u32[]{:S(2)}, u32[]{:S(2)}) %all-to-all-start.4) | async-done | bytes 8224 | tf_op jit(solution)/shard_map/all_to_all | solution.py:124
  142.5 0.6 select_reduce_fusion
  (23 shorter events, 1.0 us)
Async XLA Ops:
  0.0 1.0 copy-start
  12.6 32.5 %copy-start.1 = (bf16[128,1024]{1,0:T(8,128)(2,1)S(1)}, bf16[128,1024]{1,0:T(8,128)(2,1)}, u32[]{:S(2)}) copy-start(bf16[128,1024]{1,0:T(8,128)(2,1)} %acts_ref.1) | copy-start | bytes 786436
  12.6 24.8 %collective-permute-start.3 = (bf16[16,512]{1,0:T(8,128)(2,1)S(1)}, bf16[16,512]{1,0:T(8,128)(2,1)S(1)}, u32[]{:S(2)}, u32[]{:S(2)}) collective-permute-start(bf16[16,512]{1,0:T(8,128)(2,1)S(1)} %reduce_sum.39), channel_id=1, source_target_pairs={{0,64},{8,72},{16,80},{24,88},{32,96},{40,104},{48,112},{56,120},{... | collective-permute-start | bytes 49160 | tf_op jit(solution)/shard_map/ppermute | solution.py:33
  21.6 15.8 %collective-permute-start.4 = (bf16[16,512]{1,0:T(8,128)(2,1)S(1)}, bf16[16,512]{1,0:T(8,128)(2,1)S(1)}, u32[]{:S(2)}, u32[]{:S(2)}) collective-permute-start(bf16[16,512]{1,0:T(8,128)(2,1)S(1)} %reduce_sum.39), channel_id=1, source_target_pairs={{0,128},{8,136},{16,144},{24,152},{32,160},{40,168},{48,176},{56,1... | collective-permute-start | bytes 49160 | tf_op jit(solution)/shard_map/ppermute | solution.py:33
  32.2 8.4 %collective-permute-start.5 = (bf16[16,512]{1,0:T(8,128)(2,1)S(1)}, bf16[16,512]{1,0:T(8,128)(2,1)S(1)}, u32[]{:S(2)}, u32[]{:S(2)}) collective-permute-start(bf16[16,512]{1,0:T(8,128)(2,1)S(1)} %reduce_sum.39), channel_id=1, source_target_pairs={{0,192},{8,200},{16,208},{24,216},{32,224},{40,232},{48,240},{56,2... | collective-permute-start | bytes 49160 | tf_op jit(solution)/shard_map/ppermute | solution.py:33
  41.5 28.0 %all-to-all-start.1 = ((bf16[8,4,16,512]{3,2,1,0:T(8,128)(2,1)}), bf16[8,4,16,512]{3,2,1,0:T(8,128)(2,1)S(1)}, u32[]{:S(2)}, u32[]{:S(2)}) async-start(bf16[8,4,16,512]{3,2,1,0:T(8,128)(2,1)} %broadcast_in_dim.28), calls=%async_computation.1 | async-start | bytes 1048576 | tf_op jit(solution)/shard_map/all_to_all | solution.py:111
  45.1 14.1 %collective-permute-start = (bf16[128,256]{1,0:T(8,128)(2,1)S(1)}, bf16[128,256]{1,0:T(8,128)(2,1)S(1)}, u32[]{:S(2)}, u32[]{:S(2)}) collective-permute-start(bf16[128,256]{1,0:T(8,128)(2,1)S(1)} %get-tuple-element.7), channel_id=1, source_target_pairs={{0,64},{8,72},{16,80},{24,88},{32,96},{40,104},{48,112},{56,120},{... | collective-permute-start | bytes 196616 | tf_op jit(solution)/shard_map/ppermute | solution.py:33
  48.1 15.1 %collective-permute-start.1 = (bf16[128,256]{1,0:T(8,128)(2,1)S(1)}, bf16[128,256]{1,0:T(8,128)(2,1)S(1)}, u32[]{:S(2)}, u32[]{:S(2)}) collective-permute-start(bf16[128,256]{1,0:T(8,128)(2,1)S(1)} %get-tuple-element.6), channel_id=1, source_target_pairs={{0,128},{8,136},{16,144},{24,152},{32,160},{40,168},{48,176},{56,1... | collective-permute-start | bytes 196616 | tf_op jit(solution)/shard_map/ppermute | solution.py:33
  57.3 12.2 %collective-permute-start.2 = (bf16[128,256]{1,0:T(8,128)(2,1)S(1)}, bf16[128,256]{1,0:T(8,128)(2,1)S(1)}, u32[]{:S(2)}, u32[]{:S(2)}) collective-permute-start(bf16[128,256]{1,0:T(8,128)(2,1)S(1)} %get-tuple-element.5), channel_id=1, source_target_pairs={{0,192},{8,200},{16,208},{24,216},{32,224},{40,232},{48,240},{56,2... | collective-permute-start | bytes 196616 | tf_op jit(solution)/shard_map/ppermute | solution.py:33
  106.3 29.2 %copy-start.2 = (s32[64]{0:T(128)S(1)}, s32[64]{0:T(128)}, u32[]{:S(2)}) copy-start(s32[64]{0:T(128)} %param.7) | copy-start | bytes 772
  129.1 13.4 %all-to-all-start.4 = ((f32[32,1,64]{2,1,0:T(1,128)}), f32[32,1,64]{2,1,0:T(1,128)S(1)}, u32[]{:S(2)}, u32[]{:S(2)}) async-start(f32[32,1,64]{2,1,0:T(1,128)} %bitcast.15), calls=%async_computation.4 | async-start | bytes 32768 | tf_op jit(solution)/shard_map/all_to_all | solution.py:124

commit v3 on v1

v3 whole, which is shorter than its diff:
```python
import jax
import jax.numpy as jnp
from jax import lax
from jax.experimental import pallas as pl
from jax.experimental.pallas import tpu as pltpu
from jax.sharding import PartitionSpec as P

D = 8192
NSEL = 512
TOK = 128
Y_HI, PAIRS, PLACES, CORES = 2, 8, 2, 2
SEQS = Y_HI * PAIRS * PLACES * CORES
MEMBERS = PLACES * Y_HI * CORES
Y_LO, X = 2, 4
TENSOR = Y_LO * X
WIDTH = D // TENSOR
PART = WIDTH // PAIRS
HALF = NSEL // Y_LO
TROWS = TOK // X
LANES = 128
BLOCKS = HALF // LANES
PIECE = BLOCKS * TROWS
ROWS = PART * Y_LO // MEMBERS


def batch_index(y_hi, pair, place, core):
    return ((y_hi * PAIRS + pair) * PLACES + place) * CORES + core


def column_groups():
    return [
        [batch_index(y, k, r, c) for k in range(PAIRS)]
        for y in range(Y_HI)
        for r in range(PLACES)
        for c in range(CORES)
    ]


def pair_groups():
    return [
        [batch_index(y, k, r, c) for r in range(PLACES) for y in range(Y_HI) for c in range(CORES)]
        for k in range(PAIRS)
    ]


def whole_group():
    return [
        [
            batch_index(y, k, r, c)
            for r in range(PLACES)
            for y in range(Y_HI)
            for c in range(CORES)
            for k in range(PAIRS)
        ]
    ]


def x_groups():
    return [[y * X + x for x in range(X)] for y in range(Y_LO)]


def select_kernel(index_ref, chosen_ref, grads_ref, out_ref):
    local = chosen_ref[...] - index_ref[0] * WIDTH
    places = lax.broadcasted_iota(jnp.int32, (WIDTH, NSEL), 0)
    selector = jnp.where(places == local, 1.0, 0.0).astype(grads_ref.dtype)
    part = jnp.dot(grads_ref[...], selector, preferred_element_type=jnp.float32)
    part = part.astype(out_ref.dtype)
    for y in range(Y_LO):
        for j in range(BLOCKS):
            lane = (y * BLOCKS + j) * LANES
            block = part[:, lane : lane + LANES].reshape(X, TROWS, LANES)
            out_ref[y * X : (y + 1) * X, j * TROWS : (j + 1) * TROWS] = block


def selected(index, chosen, grads):
    vmem = pl.BlockSpec(memory_space=pltpu.VMEM)
    return pl.pallas_call(
        select_kernel,
        out_shape=jax.ShapeDtypeStruct((TENSOR, PIECE, LANES), grads.dtype),
        in_specs=[pl.BlockSpec(memory_space=pltpu.SMEM), vmem, vmem],
        out_specs=vmem,
        compiler_params=pltpu.CompilerParams(vmem_limit_bytes=16 * 1024 * 1024),
    )(index[None], chosen[None], grads)


def pack_kernel(acts_ref, shares_ref, out_ref):
    piece = shares_ref[0].astype(jnp.float32)
    for t in range(1, TENSOR):
        piece = piece + shares_ref[t].astype(jnp.float32)
    piece = piece.astype(out_ref.dtype)
    for k in range(PAIRS):
        out_ref[k, :TOK] = acts_ref[:, k * PART : (k + 1) * PART]
        out_ref[k, TOK:] = piece


def packed(acts, shares):
    vmem = pl.BlockSpec(memory_space=pltpu.VMEM)
    return pl.pallas_call(
        pack_kernel,
        out_shape=jax.ShapeDtypeStruct((PAIRS, TOK + PIECE, LANES), acts.dtype),
        in_specs=[vmem, vmem],
        out_specs=vmem,
        compiler_params=pltpu.CompilerParams(vmem_limit_bytes=16 * 1024 * 1024),
    )(acts, shares)


def example_grads_kernel(own_ref, other_ref, picked_ref, out_ref):
    count = PART // ROWS
    for k in range(PAIRS):
        blocks = [
            picked_ref[:, k, j * TROWS : (j + 1) * TROWS].reshape(TOK, LANES) for j in range(BLOCKS)
        ]
        picked = jnp.concatenate(blocks, axis=1)
        for side, ref in enumerate((own_ref, other_ref)):
            grad = lax.dot_general(
                ref[k, :TOK], picked, (((0,), (0,)), ((), ())), preferred_element_type=jnp.float32
            ).astype(out_ref.dtype)
            out_ref[side * count : (side + 1) * count, k] = grad.reshape(count, ROWS, HALF)


def example_grads(own, other, picked):
    vmem = pl.BlockSpec(memory_space=pltpu.VMEM)
    return pl.pallas_call(
        example_grads_kernel,
        out_shape=jax.ShapeDtypeStruct((MEMBERS, PAIRS, ROWS, HALF), own.dtype),
        in_specs=[vmem] * 3,
        out_specs=vmem,
        compiler_params=pltpu.CompilerParams(vmem_limit_bytes=16 * 1024 * 1024),
        cost_estimate=pl.CostEstimate(
            flops=4 * PAIRS * PART * TOK * HALF, bytes_accessed=2 * 1024 * 1024, transcendentals=0
        ),
    )(own, other, picked)


def on_device(acts, grads, chosen, assign):
    part = selected(lax.axis_index("tensor"), chosen, grads)
    shares = lax.all_to_all(part, "tensor", 0, 0, tiled=True)
    both = lax.all_to_all(
        packed(acts, shares), "batch", 0, 0, axis_index_groups=column_groups(), tiled=True
    )
    copies = jnp.broadcast_to(both[None, :, TOK:], (X, PAIRS, PIECE, LANES))
    picked = lax.all_to_all(copies, "tensor", 0, 0, axis_index_groups=x_groups(), tiled=True)
    other = lax.ppermute(both[:, :TOK], "tensor", [(t, (t + X) % TENSOR) for t in range(TENSOR)])

    terms = example_grads(both, other, picked)
    terms = lax.all_to_all(terms, "batch", 0, 0, axis_index_groups=pair_groups(), tiled=True)
    terms = terms.reshape(SEQS, ROWS, HALF)
    pairs = lax.dot_general(
        terms, terms, (((1, 2), (1, 2)), ((), ())), preferred_element_type=jnp.float32
    )
    rows = lax.all_to_all(
        pairs[:, None, :], "batch", 0, 0, axis_index_groups=whole_group(), tiled=True
    ).sum(axis=0)
    rows = jnp.broadcast_to(rows[None], (TENSOR, 1, SEQS))
    row = lax.all_to_all(rows, "tensor", 0, 0, tiled=True).sum(axis=0)
    ids = assign.reshape(Y_HI, PAIRS, PLACES, CORES)
    ids = jnp.transpose(ids, (2, 0, 3, 1)).reshape(-1)
    norming = 1.0 / (float(TOK) * float(D) * float(NSEL))
    slots = lax.broadcasted_iota(jnp.int32, (SEQS, SEQS), 0)
    placed = jnp.where(slots == ids[None, :], row * norming, 0.0)
    return placed.sum(axis=1)[None]


def solution(mesh):
    placed = (P("batch", "tensor"), P("batch", "tensor"), P(), P())
    return jax.shard_map(
        on_device, mesh=mesh, in_specs=placed, out_specs=P("batch", None), check_vma=False
    )
```

time: 130 us -> 122 us (0.938)
  blocking collectives: 124 us -> 95.4 us
  starting transfers between devices: 0 us -> 9.99 us
  waiting for transfers between devices: 0 us -> 9.61 us
  local copies, waits for them, and re-layouts: 0.57 us -> 3.46 us
  matrix products: 4.16 us -> 1.72 us
    all_to_all x5 -> x4, blocking collectives: 124 us -> 95.4 us  [the longest x1 34.6 us: on_device(): lax.all_to_all(packed(acts, shares), 'batch', 0, 0, axis_index_groups=col...]
    all_to_all x0 -> x2, starting transfers between devices: none -> 7.8 us  [the longest x1 4.33 us: on_device(): row = lax.all_to_all(rows, 'tensor', 0, 0, tiled=True).sum(axis=0)]
    ppermute x0 -> x1, waiting for transfers between devices: none -> 4.92 us  [on_device(): lax.ppermute(both[:, :TOK], 'tensor', [(t, (t + X) % TENSOR) for t in ran...]
    all_to_all x0 -> x2, waiting for transfers between devices: none -> 4.69 us  [the longest x1 4.69 us: on_device(): row = lax.all_to_all(rows, 'tensor', 0, 0, tiled=True).sum(axis=0)]
    dot_general x3 -> x1, matrix products: 4.16 us -> 1.72 us  [on_device(): lax.dot_general(terms, terms, (((1, 2), (1, 2)), ((), ())), preferred_ele...]
    ppermute x0 -> x1, starting transfers between devices: none -> 2.19 us  [on_device(): lax.ppermute(both[:, :TOK], 'tensor', [(t, (t + X) % TENSOR) for t in ran...]
    unnamed x4 -> x8, local copies, waits for them, and re-layouts: 0.01 us -> 1.64 us
    broadcast_in_dim x2, local copies, waits for them, and re-layouts: 0.02 us -> 1.5 us  [the longest x1 0.9 us: on_device(): copies = jnp.broadcast_to(both[None, :, TOK:], (X, PAIRS, PIECE, LANES))]
  transfers between devices with their start and end apart: 0 -> 3, of which waited for: 0 -> 2; matrix products, arithmetic and copies ran while one was open for 0% -> 0% of each run, Pallas kernels for 0% -> 0%
where the time goes in v3:
time: 122 us
  blocking collectives  95.4 us (78%)
  starting transfers between devices  9.99 us (8%)
  waiting for transfers between devices  9.61 us (8%)
  local copies, waits for them, and re-layouts  3.46 us (3%)
  matrix products  1.72 us (1%)
    all_to_all x1, blocking collectives, on_device(): lax.all_to_all(packed(acts, shares), 'batch', 0, 0, axis_index_groups=col...  34.6 us
    all_to_all x1, blocking collectives, on_device(): lax.all_to_all(terms, 'batch', 0, 0, axis_index_groups=pair_groups(), til...  27.9 us
    all_to_all x1, blocking collectives, on_device(): lax.all_to_all(pairs[:, None, :], 'batch', 0, 0, axis_index_groups=whole_...  21.7 us
    all_to_all x1, blocking collectives, on_device(): shares = lax.all_to_all(part, 'tensor', 0, 0, tiled=True)  11.1 us
    ppermute x1, waiting for transfers between devices, on_device(): lax.ppermute(both[:, :TOK], 'tensor', [(t, (t + X) % TENSOR) for t in ran...  4.92 us
    all_to_all x1, waiting for transfers between devices, on_device(): row = lax.all_to_all(rows, 'tensor', 0, 0, tiled=True).sum(axis=0)  4.69 us
    all_to_all x1, starting transfers between devices, on_device(): row = lax.all_to_all(rows, 'tensor', 0, 0, tiled=True).sum(axis=0)  4.33 us
    all_to_all x1, starting transfers between devices, on_device(): lax.all_to_all(copies, 'tensor', 0, 0, axis_index_groups=x_groups(), tile...  3.47 us
  transfers between devices with their start and end apart: 3, of which 2 were waited for; matrix products, arithmetic and copies ran while one was open for 0% of the time, Pallas kernels for 0%

profile of v3, /device:TPU:1, one launch (start us, length us, event | category | flops | bytes accessed | tf_op | source)
XLA Modules:
  0.0 121.8 jit_solution(9106018702384912447)
XLA Ops:
  0.0 0.7 copy-done.2
  0.7 0.9 copy-done.1
  1.6 0.3 shard_map.46
  2.0 11.1 %all_to_all.30.shares_ref = bf16[8,64,128]{2,1,0:T(8,128)(2,1)S(1)} all-to-all(bf16[8,64,128]{2,1,0:T(8,128)(2,1)S(1)} %shard_map.46), channel_id=1, replica_groups=mesh['batch'=64,'tensor'=8] {'tensor'}, dimensions={0} | all-to-all | bytes 262144 | tf_op jit(solution)/shard_map/all_to_all | solution.py:137
  13.0 0.0 copy-done
  13.0 0.1 shard_map.47
  13.1 34.6 %all_to_all.31.own_ref = bf16[8,192,128]{2,1,0:T(8,128)(2,1)S(1)} all-to-all(bf16[8,192,128]{2,1,0:T(8,128)(2,1)S(1)} %shard_map.47), channel_id=1, replica_groups={{0,32,64,96,128,160,192,224},{8,40,72,104,136,168,200,232},{16,48,80,11..., dimensions={0} | all-to-all | bytes 786432 | tf_op jit(solution)/shard_map/all_to_all | solution.py:138
  47.7 0.9 broadcast_in_dim.38
  48.6 3.5 %all-to-all-start.2 = ((bf16[4,8,64,128]{3,2,1,0:T(8,128)(2,1)}), bf16[4,8,64,128]{3,2,1,0:T(8,128)(2,1)S(1)}, u32[]{:S(2)}, u32[]{:S(2)}) async-start(bf16[4,8,64,128]{3,2,1,0:T(8,128)(2,1)} %broadcast_in_dim.38), calls=%async_computation.2 | async-start | bytes 1048576 | tf_op jit(solution)/shard_map/all_to_all | solution.py:142
  52.1 2.2 %collective-permute-start = (bf16[8,128,128]{2,1,0:T(8,128)(2,1)S(1)}, bf16[8,128,128]{2,1,0:T(8,128)(2,1)S(1)}, u32[]{:S(2)}, u32[]{:S(2)}) collective-permute-start(bf16[8,128,128]{2,1,0:T(8,128)(2,1)S(1)} %slice.8), channel_id=1, source_target_pairs={{0,4},{1,5},{2,6},{3,7},{4,0},{5,1},{6,2},{7,3},{8,12},{9,13},{10,... | collective-permute-start | bytes 786440 | tf_op jit(solution)/shard_map/ppermute | solution.py:143
  54.3 4.9 %collective-permute-done.other_ref = bf16[8,128,128]{2,1,0:T(8,128)(2,1)S(1)} collective-permute-done((bf16[8,128,128]{2,1,0:T(8,128)(2,1)S(1)}, bf16[8,128,128]{2,1,0:T(8,128)(2,1)S(1)}, u32[]{:S(2)}, u32[]{:S(2)}) %collective-permute-start) | collective-permute-done | bytes 262176 | tf_op jit(solution)/shard_map/ppermute | solution.py:143
  59.3 0.0 all-to-all-done.2.picked_ref
  59.3 0.5 shard_map.48
  59.7 27.9 %all_to_all.32 = bf16[8,8,32,256]{3,2,1,0:T(8,128)(2,1)S(1)} all-to-all(bf16[8,8,32,256]{3,2,1,0:T(8,128)(2,1)S(1)} %shard_map.48), channel_id=1, replica_groups={{0,8,256,264,16,24,272,280},{32,40,288,296,48,56,304,312},{64,72,320,32..., dimensions={0} | all-to-all | bytes 2097152 | tf_op jit(solution)/shard_map/all_to_all | solution.py:146
  87.7 1.7 %fusion = f32[64,64,1]{1,0,2:T(8,128)S(1)} fusion(bf16[64,32,256]{2,1,0:T(8,128)(2,1)S(1)} %bitcast.11), kind=kOutput, calls=%fused_computation | convolution fusion | flops 67108864 | bytes 1064960 | tf_op jit(solution)/shard_map/dot_general | solution.py:148
  89.4 21.7 %all_to_all.33 = f32[64,1,64]{2,1,0:T(1,128)S(1)} all-to-all(f32[64,1,64]{2,1,0:T(1,128)S(1)} %bitcast.13), channel_id=1, replica_groups={{0,32,64,96,128,160,192,224,8,40,72,104,136,168,200,232,256,288,320,352..., dimensions={0} | all-to-all | bytes 32768 | tf_op jit(solution)/shard_map/all_to_all | solution.py:151
  111.1 0.1 reduce_sum.27
  111.2 0.6 broadcast_in_dim.40
  111.8 4.3 %all-to-all-start.5 = ((f32[8,1,64]{2,1,0:T(1,128)}), f32[8,1,64]{2,1,0:T(1,128)S(1)}, u32[]{:S(2)}, u32[]{:S(2)}) async-start(f32[8,1,64]{2,1,0:T(1,128)} %broadcast_in_dim.40), calls=%async_computation.5 | async-start | bytes 8192 | tf_op jit(solution)/shard_map/all_to_all | solution.py:155
  116.1 0.1 reshape.18
  116.3 0.1 copy.19
  116.4 0.1 eq.10
  116.5 4.7 %all-to-all-done.5 = f32[8,1,64]{2,1,0:T(1,128)S(1)} async-done(((f32[8,1,64]{2,1,0:T(1,128)}), f32[8,1,64]{2,1,0:T(1,128)S(1)}, u32[]{:S(2)}, u32[]{:S(2)}) %all-to-all-start.5) | async-done | bytes 2080 | tf_op jit(solution)/shard_map/all_to_all | solution.py:155
  121.2 0.6 select_reduce_fusion
  (9 shorter events, 0.1 us)
Async XLA Ops:
  0.0 0.7 copy-start.2
  0.7 0.9 copy-start.1
  1.6 11.4 %copy-start = (bf16[128,1024]{1,0:T(8,128)(2,1)S(1)}, bf16[128,1024]{1,0:T(8,128)(2,1)}, u32[]{:S(2)}) copy-start(bf16[128,1024]{1,0:T(8,128)(2,1)} %acts_ref.1) | copy-start | bytes 786436
  48.6 10.6 %all-to-all-start.2 = ((bf16[4,8,64,128]{3,2,1,0:T(8,128)(2,1)}), bf16[4,8,64,128]{3,2,1,0:T(8,128)(2,1)S(1)}, u32[]{:S(2)}, u32[]{:S(2)}) async-start(bf16[4,8,64,128]{3,2,1,0:T(8,128)(2,1)} %broadcast_in_dim.38), calls=%async_computation.2 | async-start | bytes 1048576 | tf_op jit(solution)/shard_map/all_to_all | solution.py:142
  52.1 7.1 %collective-permute-start = (bf16[8,128,128]{2,1,0:T(8,128)(2,1)S(1)}, bf16[8,128,128]{2,1,0:T(8,128)(2,1)S(1)}, u32[]{:S(2)}, u32[]{:S(2)}) collective-permute-start(bf16[8,128,128]{2,1,0:T(8,128)(2,1)S(1)} %slice.8), channel_id=1, source_target_pairs={{0,4},{1,5},{2,6},{3,7},{4,0},{5,1},{6,2},{7,3},{8,12},{9,13},{10,... | collective-permute-start | bytes 786440 | tf_op jit(solution)/shard_map/ppermute | solution.py:143
  111.8 4.3 %copy-start.3 = (s32[64]{0:T(128)S(1)}, s32[64]{0:T(128)}, u32[]{:S(2)}) copy-start(s32[64]{0:T(128)} %param.7) | copy-start | bytes 772
  111.8 9.3 %all-to-all-start.5 = ((f32[8,1,64]{2,1,0:T(1,128)}), f32[8,1,64]{2,1,0:T(1,128)S(1)}, u32[]{:S(2)}, u32[]{:S(2)}) async-start(f32[8,1,64]{2,1,0:T(1,128)} %broadcast_in_dim.40), calls=%async_computation.5 | async-start | bytes 8192 | tf_op jit(solution)/shard_map/all_to_all | solution.py:155

commit v4 on v3

v4 whole, which is shorter than its diff:
```python
import jax
import jax.numpy as jnp
from jax import lax
from jax.experimental import pallas as pl
from jax.experimental.pallas import tpu as pltpu
from jax.sharding import PartitionSpec as P

D = 8192
NSEL = 512
TOK = 128
Y_HI, PAIRS, PLACES, CORES = 2, 8, 2, 2
SEQS = Y_HI * PAIRS * PLACES * CORES
SIDES = Y_HI * CORES
DEPTH = PAIRS * PLACES
MEMBERS = PLACES * SIDES
Y_LO, X = 2, 4
TENSOR = Y_LO * X
WIDTH = D // TENSOR
PART = WIDTH // PAIRS
HALF = NSEL // Y_LO
TROWS = TOK // X
LANES = 128
BLOCKS = HALF // LANES
PIECE = BLOCKS * TROWS
ROWS = PART * Y_LO // MEMBERS


def batch_index(y_hi, pair, place, core):
    return ((y_hi * PAIRS + pair) * PLACES + place) * CORES + core


def column_groups():
    return [
        [batch_index(y, k, r, c) for k in range(PAIRS)]
        for y in range(Y_HI)
        for r in range(PLACES)
        for c in range(CORES)
    ]


def pair_groups():
    return [
        [batch_index(y, k, r, c) for r in range(PLACES) for y in range(Y_HI) for c in range(CORES)]
        for k in range(PAIRS)
    ]


def depth_groups():
    return [
        [batch_index(y, k, r, c) for k in range(PAIRS) for r in range(PLACES)]
        for y in range(Y_HI)
        for c in range(CORES)
    ]


def plane_groups():
    return [
        [
            batch_index(y, k, r, c) * TENSOR + t
            for y in range(Y_HI)
            for c in range(CORES)
            for t in range(TENSOR)
        ]
        for k in range(PAIRS)
        for r in range(PLACES)
    ]


def x_groups():
    return [[y * X + x for x in range(X)] for y in range(Y_LO)]


def kernel_call(kernel, out_shape, in_specs, args, scratch=(), limit=24 * 1024 * 1024):
    vmem = pl.BlockSpec(memory_space=pltpu.VMEM)
    return pl.pallas_call(
        kernel,
        out_shape=out_shape,
        in_specs=[vmem] * len(args) if in_specs is None else in_specs,
        out_specs=jax.tree.map(lambda _: vmem, out_shape),
        scratch_shapes=scratch,
        compiler_params=pltpu.CompilerParams(vmem_limit_bytes=limit),
    )(*args)


def select_kernel(index_ref, chosen_hbm, grads_hbm, out_ref, chosen_ref, grads_ref, sems):
    first = pltpu.make_async_copy(chosen_hbm, chosen_ref, sems.at[0])
    second = pltpu.make_async_copy(grads_hbm, grads_ref, sems.at[1])
    first.start()
    second.start()
    first.wait()
    local = chosen_ref[...] - index_ref[0] * WIDTH
    places = lax.broadcasted_iota(jnp.int32, (WIDTH, NSEL), 0)
    selector = jnp.where(places == local, 1.0, 0.0).astype(grads_ref.dtype)
    second.wait()
    part = jnp.dot(grads_ref[...], selector, preferred_element_type=jnp.float32)
    part = part.astype(out_ref.dtype)
    for y in range(Y_LO):
        for j in range(BLOCKS):
            lane = (y * BLOCKS + j) * LANES
            block = part[:, lane : lane + LANES].reshape(X, TROWS, LANES)
            out_ref[y * X : (y + 1) * X, j * TROWS : (j + 1) * TROWS] = block


def selected(index, chosen, grads):
    hbm = pl.BlockSpec(memory_space=pltpu.HBM)
    return kernel_call(
        select_kernel,
        jax.ShapeDtypeStruct((TENSOR, PIECE, LANES), grads.dtype),
        [pl.BlockSpec(memory_space=pltpu.SMEM), hbm, hbm],
        (index[None], chosen[None], grads),
        [
            pltpu.VMEM((1, NSEL), jnp.int32),
            pltpu.VMEM((TOK, WIDTH), grads.dtype),
            pltpu.SemaphoreType.DMA((2,)),
        ],
        None,
    )


def pack_kernel(acts_ref, shares_ref, out_ref):
    piece = shares_ref[0].astype(jnp.float32)
    for t in range(1, TENSOR):
        piece = piece + shares_ref[t].astype(jnp.float32)
    piece = piece.astype(out_ref.dtype)
    for k in range(PAIRS):
        out_ref[k, :TOK] = acts_ref[:, k * PART : (k + 1) * PART]
        out_ref[k, TOK:] = piece


def packed(acts, shares):
    shape = jax.ShapeDtypeStruct((PAIRS, TOK + PIECE, LANES), acts.dtype)
    return kernel_call(pack_kernel, shape, None, (acts, shares))


def unpack_kernel(both_ref, own_ref, copies_ref):
    own_ref[...] = both_ref[:, :TOK]
    for x in range(X):
        copies_ref[x] = both_ref[:, TOK:]


def unpacked(both):
    shapes = (
        jax.ShapeDtypeStruct((PAIRS, TOK, PART), both.dtype),
        jax.ShapeDtypeStruct((X, PAIRS, PIECE, LANES), both.dtype),
    )
    return kernel_call(unpack_kernel, shapes, None, (both,))


def example_grads_kernel(own_ref, other_ref, picked_ref, out_ref):
    count = PART // ROWS
    for k in range(PAIRS):
        blocks = [
            picked_ref[:, k, j * TROWS : (j + 1) * TROWS].reshape(TOK, LANES) for j in range(BLOCKS)
        ]
        picked = jnp.concatenate(blocks, axis=1)
        for side, ref in enumerate((own_ref, other_ref)):
            grad = lax.dot_general(
                ref[k], picked, (((0,), (0,)), ((), ())), preferred_element_type=jnp.float32
            ).astype(out_ref.dtype)
            out_ref[side * count : (side + 1) * count, k] = grad.reshape(count, ROWS, HALF)


def example_grads(own, other, picked):
    shape = jax.ShapeDtypeStruct((MEMBERS, PAIRS, ROWS, HALF), own.dtype)
    return kernel_call(example_grads_kernel, shape, None, (own, other, picked))


def pairs_kernel(terms_ref, out_ref, *wide_refs):
    wide = terms_ref[...].reshape(SEQS * ROWS, HALF).astype(jnp.float32)
    for j, wide_ref in enumerate(wide_refs):
        wide_ref[...] = wide[:, j * LANES : (j + 1) * LANES]
    total = jnp.zeros((SEQS, SEQS), jnp.float32)
    group = 4
    for first in range(0, ROWS, group):
        rows = [
            wide_ref[pl.ds(f, SEQS, stride=ROWS), :]
            for f in range(first, first + group)
            for wide_ref in wide_refs
        ]
        rows = jnp.concatenate(rows, axis=1).astype(terms_ref.dtype)
        total += lax.dot_general(
            rows, rows, (((1,), (1,)), ((), ())), preferred_element_type=jnp.float32
        )
    for r in range(PLACES):
        sides = [
            total[(r * SIDES + q) * PAIRS : (r * SIDES + q + 1) * PAIRS] for q in range(SIDES)
        ]
        out_ref[:, r, 0] = jnp.concatenate(sides, axis=1)


def pairs(terms):
    return kernel_call(
        pairs_kernel,
        jax.ShapeDtypeStruct((PAIRS, PLACES, 1, SIDES * SEQS), jnp.float32),
        None,
        (terms,),
        [pltpu.VMEM((SEQS * ROWS, LANES), jnp.float32)] * BLOCKS,
    )


def side_kernel(rows_ref, out_ref):
    sums = rows_ref[0]
    for z in range(1, DEPTH):
        sums = sums + rows_ref[z]
    for q in range(SIDES):
        out_ref[q] = jnp.broadcast_to(sums[:, q * SEQS : (q + 1) * SEQS][None], (TENSOR, 1, SEQS))


def place_kernel(rows_ref, ids_ref, out_ref):
    row = rows_ref[0]
    for member in range(1, SIDES * TENSOR):
        row = row + rows_ref[member]
    slots = lax.broadcasted_iota(jnp.int32, (SEQS, SEQS), 0)
    spots = jnp.where(slots == ids_ref[...], 1.0, 0.0)
    norming = 1.0 / (float(TOK) * float(D) * float(NSEL))
    out_ref[...] = lax.dot_general(
        row * norming,
        spots,
        (((1,), (1,)), ((), ())),
        precision=lax.Precision.HIGHEST,
        preferred_element_type=jnp.float32,
    )


def on_device(acts, grads, chosen, assign):
    part = selected(lax.axis_index("tensor"), chosen, grads)
    shares = lax.all_to_all(part, "tensor", 0, 0, tiled=True)
    both = lax.all_to_all(
        packed(acts, shares), "batch", 0, 0, axis_index_groups=column_groups(), tiled=True
    )
    own, copies = unpacked(both)
    picked = lax.all_to_all(copies, "tensor", 0, 0, axis_index_groups=x_groups(), tiled=True)
    other = lax.ppermute(own, "tensor", [(t, (t + X) % TENSOR) for t in range(TENSOR)])

    terms = example_grads(own, other, picked)
    terms = lax.all_to_all(terms, "batch", 0, 0, axis_index_groups=pair_groups(), tiled=True)
    rows = pairs(terms).reshape(DEPTH, 1, SIDES * SEQS)
    rows = lax.all_to_all(rows, "batch", 0, 0, axis_index_groups=depth_groups(), tiled=True)
    shape = jax.ShapeDtypeStruct((SIDES, TENSOR, 1, SEQS), jnp.float32)
    rows = kernel_call(side_kernel, shape, None, (rows,)).reshape(SIDES * TENSOR, 1, SEQS)
    rows = lax.all_to_all(
        rows, ("batch", "tensor"), 0, 0, axis_index_groups=plane_groups(), tiled=True
    )
    ids = assign.reshape(Y_HI, PAIRS, PLACES, CORES)
    ids = jnp.transpose(ids, (2, 0, 3, 1)).reshape(1, SEQS)
    shape = jax.ShapeDtypeStruct((1, SEQS), jnp.float32)
    return kernel_call(place_kernel, shape, None, (rows, ids))


def solution(mesh):
    placed = (P("batch", "tensor"), P("batch", "tensor"), P(), P())
    return jax.shard_map(
        on_device, mesh=mesh, in_specs=placed, out_specs=P("batch", None), check_vma=False
    )
```

time: 122 us -> 123 us (level)
  Pallas kernels: 0.83 us -> 6.42 us
  blocking collectives: 95.4 us -> 90.3 us
  starting transfers between devices: 9.99 us -> 13.6 us
  local copies, waits for them, and re-layouts: 3.46 us -> 0.31 us
  waiting for transfers between devices: 9.61 us -> 11.5 us
  matrix products: 1.72 us -> 0 us
    pallas_call x3 -> x7, Pallas kernels: 0.83 us -> 6.42 us  [kernel_call(): pl.pallas_call(kernel, out_shape=out_shape, in_specs=[vmem] * len(args) i...]
    all_to_all x1, blocking collectives: 21.7 us -> 16.4 us  [on_device(): lax.all_to_all(rows, 'batch', 0, 0, axis_index_groups=depth_groups(), til...]
    all_to_all x1, starting transfers between devices: 4.33 us -> 7.97 us  [on_device(): lax.all_to_all(rows, ('batch', 'tensor'), 0, 0, axis_index_groups=plane_g...]
    all_to_all x1, waiting for transfers between devices: 4.69 us -> 6.57 us  [on_device(): lax.all_to_all(rows, ('batch', 'tensor'), 0, 0, axis_index_groups=plane_g...]
    dot_general x1 -> x0, matrix products: 1.72 us -> none  [on_device(): lax.dot_general(terms, terms, (((1, 2), (1, 2)), ((), ())), preferred_ele...]
    unnamed x8 -> x4, local copies, waits for them, and re-layouts: 1.64 us -> 0.01 us
    broadcast_in_dim x2 -> x0, local copies, waits for them, and re-layouts: 1.5 us -> none  [the longest x1 0.9 us: on_device(): copies = jnp.broadcast_to(both[None, :, TOK:], (X, PAIRS, PIECE, LANES))]
where the time goes in v4:
time: 123 us; the launch traced here: 122 us
  blocking collectives  90.3 us (73%)
  starting transfers between devices  13.6 us (11%)
  waiting for transfers between devices  11.5 us (9%)
  Pallas kernels  6.42 us (5%)
    all_to_all x1, blocking collectives, on_device(): lax.all_to_all(packed(acts, shares), 'batch', 0, 0, axis_index_groups=col...  34.6 us
    all_to_all x1, blocking collectives, on_device(): lax.all_to_all(terms, 'batch', 0, 0, axis_index_groups=pair_groups(), til...  27.9 us
    all_to_all x1, blocking collectives, on_device(): lax.all_to_all(rows, 'batch', 0, 0, axis_index_groups=depth_groups(), til...  16.4 us
    all_to_all x1, blocking collectives, on_device(): shares = lax.all_to_all(part, 'tensor', 0, 0, tiled=True)  11.3 us
    all_to_all x1, starting transfers between devices, on_device(): lax.all_to_all(rows, ('batch', 'tensor'), 0, 0, axis_index_groups=plane_g...  7.97 us
    all_to_all x1, waiting for transfers between devices, on_device(): lax.all_to_all(rows, ('batch', 'tensor'), 0, 0, axis_index_groups=plane_g...  6.57 us
    pallas_call x7, Pallas kernels, kernel_call(): pl.pallas_call(kernel, out_shape=out_shape, in_specs=[vmem] * len(args) i...  6.42 us
    ppermute x1, waiting for transfers between devices, on_device(): lax.ppermute(own, 'tensor', [(t, (t + X) % TENSOR) for t in range(TENSOR)])  4.92 us
  transfers between devices with their start and end apart: 3, of which 2 were waited for; matrix products, arithmetic and copies ran while one was open for 0% of the time, Pallas kernels for 0%

profile of v4, /device:TPU:1, one launch (start us, length us, event | category | flops | bytes accessed | tf_op | source)
XLA Modules:
  0.0 122.2 jit_solution(1456379502992326395)
XLA Ops:
  0.0 0.0 copy-start
  0.0 2.0 %shard_map.46 = bf16[8,64,128]{2,1,0:T(8,128)(2,1)} custom-call(s32[1]{0:T(128)} %bitcast.index_ref, s32[1,512]{1,0:T(1,128)} %bitcast.7, bf16[128,1024]{1,0:T(8,128)(2,1)} %grads_hbm.1), custom_call_target="tpu_custom_call" | custom-call | tf_op jit(solution)/shard_map/pallas_call | solution.py:75
  2.0 11.3 %all_to_all.30.shares_ref = bf16[8,64,128]{2,1,0:T(8,128)(2,1)S(1)} all-to-all(bf16[8,64,128]{2,1,0:T(8,128)(2,1)} %shard_map.46), channel_id=1, replica_groups=mesh['batch'=64,'tensor'=8] {'tensor'}, dimensions={0} | all-to-all | bytes 262144 | tf_op jit(solution)/shard_map/all_to_all | solution.py:227
  13.3 0.0 copy-done
  13.3 0.1 shard_map.47
  13.4 34.6 %all_to_all.31.both_ref = bf16[8,192,128]{2,1,0:T(8,128)(2,1)S(1)} all-to-all(bf16[8,192,128]{2,1,0:T(8,128)(2,1)S(1)} %shard_map.47), channel_id=1, replica_groups={{0,32,64,96,128,160,192,224},{8,40,72,104,136,168,200,232},{16,48,80,11..., dimensions={0} | all-to-all | bytes 786432 | tf_op jit(solution)/shard_map/all_to_all | solution.py:228
  48.0 0.9 shard_map.48
  48.9 3.5 %all-to-all-start.2 = ((bf16[4,8,64,128]{3,2,1,0:T(8,128)(2,1)}), bf16[4,8,64,128]{3,2,1,0:T(8,128)(2,1)S(1)}, u32[]{:S(2)}, u32[]{:S(2)}) async-start(bf16[4,8,64,128]{3,2,1,0:T(8,128)(2,1)} %get-tuple-element.8), calls=%async_computation.2 | async-start | bytes 1048576 | tf_op jit(solution)/shard_map/all_to_all | solution.py:232
  52.3 2.2 %collective-permute-start = (bf16[8,128,128]{2,1,0:T(8,128)(2,1)S(1)}, bf16[8,128,128]{2,1,0:T(8,128)(2,1)S(1)}, u32[]{:S(2)}, u32[]{:S(2)}) collective-permute-start(bf16[8,128,128]{2,1,0:T(8,128)(2,1)S(1)} %get-tuple-element.7.own_ref), channel_id=1, source_target_pairs={{0,4},{1,5},{2,6},{3,7},{4,0},{5,1},{6,2},{7,3},{8,12},{9,13},{10,... | collective-permute-start | bytes 786440 | tf_op jit(solution)/shard_map/ppermute | solution.py:233
  54.5 4.9 %collective-permute-done.other_ref = bf16[8,128,128]{2,1,0:T(8,128)(2,1)S(1)} collective-permute-done((bf16[8,128,128]{2,1,0:T(8,128)(2,1)S(1)}, bf16[8,128,128]{2,1,0:T(8,128)(2,1)S(1)}, u32[]{:S(2)}, u32[]{:S(2)}) %collective-permute-start) | collective-permute-done | bytes 262176 | tf_op jit(solution)/shard_map/ppermute | solution.py:233
  59.5 0.0 all-to-all-done.2.picked_ref
  59.5 0.5 shard_map.49
  59.9 27.9 %all_to_all.32.terms_ref = bf16[8,8,32,256]{3,2,1,0:T(8,128)(2,1)S(1)} all-to-all(bf16[8,8,32,256]{3,2,1,0:T(8,128)(2,1)S(1)} %shard_map.49), channel_id=1, replica_groups={{0,8,256,264,16,24,272,280},{32,40,288,296,48,56,304,312},{64,72,320,32..., dimensions={0} | all-to-all | bytes 2097152 | tf_op jit(solution)/shard_map/all_to_all | solution.py:236
  87.9 1.7 %shard_map.50 = f32[8,2,1,256]{3,2,1,0:T(1,128)S(1)} custom-call(bf16[8,8,32,256]{3,2,1,0:T(8,128)(2,1)S(1)} %all_to_all.32.terms_ref), custom_call_target="tpu_custom_call" | custom-call | tf_op jit(solution)/shard_map/pallas_call | solution.py:75
  89.5 16.4 %all_to_all.33.rows_ref = f32[16,1,256]{2,1,0:T(1,128)S(1)} all-to-all(f32[16,1,256]{2,1,0:T(1,128)S(1)} %bitcast.5), channel_id=1, replica_groups={{0,16,32,48,64,80,96,112,128,144,160,176,192,208,224,240},{8,24,40,56,7..., dimensions={0} | all-to-all | bytes 32768 | tf_op jit(solution)/shard_map/all_to_all | solution.py:238
  105.9 0.7 shard_map.51
  106.6 0.0 copy-start.1
  106.6 8.0 %all-to-all-start.5 = ((f32[32,1,64]{2,1,0:T(1,128)}), f32[32,1,64]{2,1,0:T(1,128)S(1)}, u32[]{:S(2)}, u32[]{:S(2)}) async-start(f32[32,1,64]{2,1,0:T(1,128)} %bitcast.3), calls=%async_computation.5 | async-start | bytes 32768 | tf_op jit(solution)/shard_map/all_to_all | solution.py:241
  114.6 0.0 copy-done.1
  114.6 0.1 reshape.14
  114.7 0.1 copy.6
  114.8 0.1 reshape.15.ids_ref
  114.9 6.6 %all-to-all-done.5.rows_ref = f32[32,1,64]{2,1,0:T(1,128)S(1)} async-done(((f32[32,1,64]{2,1,0:T(1,128)}), f32[32,1,64]{2,1,0:T(1,128)S(1)}, u32[]{:S(2)}, u32[]{:S(2)}) %all-to-all-start.5) | async-done | bytes 8224 | tf_op jit(solution)/shard_map/all_to_all | solution.py:241
  121.5 0.7 shard_map.52
Async XLA Ops:
  0.0 13.3 %copy-start = (bf16[128,1024]{1,0:T(8,128)(2,1)S(1)}, bf16[128,1024]{1,0:T(8,128)(2,1)}, u32[]{:S(2)}) copy-start(bf16[128,1024]{1,0:T(8,128)(2,1)} %acts_ref.1) | copy-start | bytes 786436
  48.9 10.6 %all-to-all-start.2 = ((bf16[4,8,64,128]{3,2,1,0:T(8,128)(2,1)}), bf16[4,8,64,128]{3,2,1,0:T(8,128)(2,1)S(1)}, u32[]{:S(2)}, u32[]{:S(2)}) async-start(bf16[4,8,64,128]{3,2,1,0:T(8,128)(2,1)} %get-tuple-element.8), calls=%async_computation.2 | async-start | bytes 1048576 | tf_op jit(solution)/shard_map/all_to_all | solution.py:232
  52.3 7.1 %collective-permute-start = (bf16[8,128,128]{2,1,0:T(8,128)(2,1)S(1)}, bf16[8,128,128]{2,1,0:T(8,128)(2,1)S(1)}, u32[]{:S(2)}, u32[]{:S(2)}) collective-permute-start(bf16[8,128,128]{2,1,0:T(8,128)(2,1)S(1)} %get-tuple-element.7.own_ref), channel_id=1, source_target_pairs={{0,4},{1,5},{2,6},{3,7},{4,0},{5,1},{6,2},{7,3},{8,12},{9,13},{10,... | collective-permute-start | bytes 786440 | tf_op jit(solution)/shard_map/ppermute | solution.py:233
  106.6 8.0 %copy-start.1 = (s32[64]{0:T(128)S(1)}, s32[64]{0:T(128)}, u32[]{:S(2)}) copy-start(s32[64]{0:T(128)} %param.7) | copy-start | bytes 772
  106.6 14.9 %all-to-all-start.5 = ((f32[32,1,64]{2,1,0:T(1,128)}), f32[32,1,64]{2,1,0:T(1,128)S(1)}, u32[]{:S(2)}, u32[]{:S(2)}) async-start(f32[32,1,64]{2,1,0:T(1,128)} %bitcast.3), calls=%async_computation.5 | async-start | bytes 32768 | tf_op jit(solution)/shard_map/all_to_all | solution.py:241

commit v5 on v4

v5 whole, which is shorter than its diff:
```python
import jax
import jax.numpy as jnp
from jax import lax
from jax.experimental import pallas as pl
from jax.experimental.pallas import tpu as pltpu
from jax.sharding import PartitionSpec as P

D = 8192
NSEL = 512
TOK = 128
Y_HI, PAIRS, PLACES, CORES = 2, 8, 2, 2
SEQS = Y_HI * PAIRS * PLACES * CORES
SIDES = Y_HI * CORES
DEPTH = PAIRS * PLACES
MEMBERS = PLACES * SIDES
Y_LO, X = 2, 4
TENSOR = Y_LO * X
WIDTH = D // TENSOR
PART = WIDTH // PAIRS
HALF = NSEL // Y_LO
TROWS = TOK // X
LANES = 128
BLOCKS = HALF // LANES
PIECE = BLOCKS * TROWS
ROWS = PART * Y_LO // MEMBERS


def batch_index(y_hi, pair, place, core):
    return ((y_hi * PAIRS + pair) * PLACES + place) * CORES + core


def column_groups():
    return [
        [batch_index(y, k, r, c) for k in range(PAIRS)]
        for y in range(Y_HI)
        for r in range(PLACES)
        for c in range(CORES)
    ]


def pair_groups():
    return [
        [batch_index(y, k, r, c) for r in range(PLACES) for y in range(Y_HI) for c in range(CORES)]
        for k in range(PAIRS)
    ]


def depth_groups():
    return [
        [batch_index(y, k, r, c) for k in range(PAIRS) for r in range(PLACES)]
        for y in range(Y_HI)
        for c in range(CORES)
    ]


def plane_groups():
    return [
        [
            batch_index(y, k, r, c) * TENSOR + t
            for y in range(Y_HI)
            for c in range(CORES)
            for t in range(TENSOR)
        ]
        for k in range(PAIRS)
        for r in range(PLACES)
    ]


def x_groups():
    return [[y * X + x for x in range(X)] for y in range(Y_LO)]


def kernel_call(kernel, out_shape, args):
    vmem = pl.BlockSpec(memory_space=pltpu.VMEM)
    return pl.pallas_call(
        kernel,
        out_shape=out_shape,
        in_specs=[vmem] * len(args),
        out_specs=jax.tree.map(lambda _: vmem, out_shape),
        compiler_params=pltpu.CompilerParams(vmem_limit_bytes=24 * 1024 * 1024),
    )(*args)


def select_kernel(local_ref, grads_ref, out_ref):
    places = lax.broadcasted_iota(jnp.int32, (WIDTH, NSEL), 0)
    selector = jnp.where(places == local_ref[...], 1.0, 0.0).astype(grads_ref.dtype)
    part = jnp.dot(grads_ref[...], selector, preferred_element_type=jnp.float32)
    part = part.astype(out_ref.dtype)
    for y in range(Y_LO):
        for j in range(BLOCKS):
            lane = (y * BLOCKS + j) * LANES
            block = part[:, lane : lane + LANES].reshape(X, TROWS, LANES)
            out_ref[y * X : (y + 1) * X, j * TROWS : (j + 1) * TROWS] = block


def selected(chosen, grads):
    local = (chosen - lax.axis_index("tensor") * WIDTH)[None]
    shape = jax.ShapeDtypeStruct((TENSOR, PIECE, LANES), grads.dtype)
    return kernel_call(select_kernel, shape, (local, grads))


def pack_kernel(acts_ref, shares_ref, out_ref):
    piece = shares_ref[0].astype(jnp.float32)
    for t in range(1, TENSOR):
        piece = piece + shares_ref[t].astype(jnp.float32)
    piece = piece.astype(out_ref.dtype)
    for k in range(PAIRS):
        out_ref[k, :TOK] = acts_ref[:, k * PART : (k + 1) * PART]
        out_ref[k, TOK:] = piece


def packed(acts, shares):
    shape = jax.ShapeDtypeStruct((PAIRS, TOK + PIECE, LANES), acts.dtype)
    return kernel_call(pack_kernel, shape, (acts, shares))


def unpack_kernel(both_ref, own_ref, copies_ref):
    own_ref[...] = both_ref[:, :TOK]
    for x in range(X):
        copies_ref[x] = both_ref[:, TOK:]


def unpacked(both):
    shapes = (
        jax.ShapeDtypeStruct((PAIRS, TOK, PART), both.dtype),
        jax.ShapeDtypeStruct((X, PAIRS, PIECE, LANES), both.dtype),
    )
    return kernel_call(unpack_kernel, shapes, (both,))


def example_grads_kernel(own_ref, other_ref, picked_ref, assign_ref, out_ref, spots_ref):
    count = PART // ROWS
    for k in range(PAIRS):
        blocks = [
            picked_ref[:, k, j * TROWS : (j + 1) * TROWS].reshape(TOK, LANES) for j in range(BLOCKS)
        ]
        picked = jnp.concatenate(blocks, axis=1)
        for side, ref in enumerate((own_ref, other_ref)):
            grad = lax.dot_general(
                ref[k], picked, (((0,), (0,)), ((), ())), preferred_element_type=jnp.float32
            ).astype(out_ref.dtype)
            out_ref[side * count : (side + 1) * count, k] = grad.reshape(count, ROWS, HALF)
    column = lax.broadcasted_iota(jnp.int32, (SEQS, SEQS), 0)
    slot = lax.broadcasted_iota(jnp.int32, (SEQS, SEQS), 1)
    pair, core = column % PAIRS, column // PAIRS % CORES
    y_hi, place = column // (PAIRS * CORES) % Y_HI, column // (PAIRS * SIDES)
    ordered = jnp.where(batch_index(y_hi, pair, place, core) == slot, 1.0, 0.0)
    wanted = jnp.where(column == assign_ref[...], 1.0, 0.0)
    spots_ref[...] = lax.dot_general(
        ordered, wanted, (((1,), (1,)), ((), ())), preferred_element_type=jnp.float32
    )


def example_grads(own, other, picked, assign):
    shapes = (
        jax.ShapeDtypeStruct((MEMBERS, PAIRS, ROWS, HALF), own.dtype),
        jax.ShapeDtypeStruct((SEQS, SEQS), jnp.float32),
    )
    return kernel_call(example_grads_kernel, shapes, (own, other, picked, assign[None]))


def pairs_kernel(terms_ref, out_ref):
    terms = jnp.swapaxes(terms_ref[...].reshape(SEQS, ROWS, HALF), 0, 1)
    total = jnp.zeros((SEQS, SEQS), jnp.float32)
    for row in range(ROWS):
        total += lax.dot_general(
            terms[row], terms[row], (((1,), (1,)), ((), ())), preferred_element_type=jnp.float32
        )
    for r in range(PLACES):
        sides = [
            total[(r * SIDES + q) * PAIRS : (r * SIDES + q + 1) * PAIRS] for q in range(SIDES)
        ]
        out_ref[:, r, 0] = jnp.concatenate(sides, axis=1)


def pairs(terms):
    shape = jax.ShapeDtypeStruct((PAIRS, PLACES, 1, SIDES * SEQS), jnp.float32)
    return kernel_call(pairs_kernel, shape, (terms,))


def side_kernel(rows_ref, out_ref):
    sums = rows_ref[0]
    for z in range(1, DEPTH):
        sums = sums + rows_ref[z]
    for q in range(SIDES):
        out_ref[q] = jnp.broadcast_to(sums[:, q * SEQS : (q + 1) * SEQS][None], (TENSOR, 1, SEQS))


def place_kernel(rows_ref, spots_ref, out_ref):
    row = rows_ref[0]
    for member in range(1, SIDES * TENSOR):
        row = row + rows_ref[member]
    norming = 1.0 / (float(TOK) * float(D) * float(NSEL))
    out_ref[...] = lax.dot_general(
        row * norming,
        spots_ref[...],
        (((1,), (0,)), ((), ())),
        precision=lax.Precision.HIGHEST,
        preferred_element_type=jnp.float32,
    )


def on_device(acts, grads, chosen, assign):
    part = selected(chosen, grads)
    shares = lax.all_to_all(part, "tensor", 0, 0, tiled=True)
    both = lax.all_to_all(
        packed(acts, shares), "batch", 0, 0, axis_index_groups=column_groups(), tiled=True
    )
    own, copies = unpacked(both)
    picked = lax.all_to_all(copies, "tensor", 0, 0, axis_index_groups=x_groups(), tiled=True)
    other = lax.ppermute(own, "tensor", [(t, (t + X) % TENSOR) for t in range(TENSOR)])

    terms, spots = example_grads(own, other, picked, assign)
    terms = lax.all_to_all(terms, "batch", 0, 0, axis_index_groups=pair_groups(), tiled=True)
    rows = pairs(terms).reshape(DEPTH, 1, SIDES * SEQS)
    rows = lax.all_to_all(rows, "batch", 0, 0, axis_index_groups=depth_groups(), tiled=True)
    shape = jax.ShapeDtypeStruct((SIDES, TENSOR, 1, SEQS), jnp.float32)
    rows = kernel_call(side_kernel, shape, (rows,)).reshape(SIDES * TENSOR, 1, SEQS)
    rows = lax.all_to_all(
        rows, ("batch", "tensor"), 0, 0, axis_index_groups=plane_groups(), tiled=True
    )
    shape = jax.ShapeDtypeStruct((1, SEQS), jnp.float32)
    return kernel_call(place_kernel, shape, (rows, spots))


def solution(mesh):
    placed = (P("batch", "tensor"), P("batch", "tensor"), P(), P())
    return jax.shard_map(
        on_device, mesh=mesh, in_specs=placed, out_specs=P("batch", None), check_vma=False
    )
```

time: 123 us -> 120 us (0.976)
  blocking collectives: 90.3 us -> 105 us
  starting transfers between devices: 13.6 us -> 5.66 us
  waiting for transfers between devices: 11.5 us -> 4.92 us
  Pallas kernels: 6.42 us -> 3.09 us
  local copies, waits for them, and re-layouts: 0.31 us -> 1.64 us
    all_to_all x0 -> x1, blocking collectives: none -> 14.6 us  [on_device(): lax.all_to_all(rows, ('batch', 'tensor'), 0, 0, axis_index_groups=plane_g...]
    all_to_all x1 -> x0, starting transfers between devices: 7.97 us -> none  [on_device(): lax.all_to_all(rows, ('batch', 'tensor'), 0, 0, axis_index_groups=plane_g...]
    all_to_all x1 -> x0, waiting for transfers between devices: 6.57 us -> none  [on_device(): lax.all_to_all(rows, ('batch', 'tensor'), 0, 0, axis_index_groups=plane_g...]
    pallas_call x7, Pallas kernels: 6.42 us -> 3.09 us  [kernel_call(): pl.pallas_call(kernel, out_shape=out_shape, in_specs=[vmem] * len(args),...]
    unnamed x4 -> x8, local copies, waits for them, and re-layouts: 0.01 us -> 1.64 us
  transfers between devices with their start and end apart: 3 -> 2, of which waited for: 2 -> 1; matrix products, arithmetic and copies ran while one was open for 0% -> 0% of each run, Pallas kernels for 0% -> 0%
where the time goes in v5:
time: 120 us
  blocking collectives  105 us (88%)
  starting transfers between devices  5.66 us (5%)
  waiting for transfers between devices  4.92 us (4%)
  Pallas kernels  3.09 us (3%)
  local copies, waits for them, and re-layouts  1.64 us (1%)
    all_to_all x1, blocking collectives, on_device(): lax.all_to_all(packed(acts, shares), 'batch', 0, 0, axis_index_groups=col...  34.6 us
    all_to_all x1, blocking collectives, on_device(): lax.all_to_all(terms, 'batch', 0, 0, axis_index_groups=pair_groups(), til...  27.9 us
    all_to_all x1, blocking collectives, on_device(): lax.all_to_all(rows, 'batch', 0, 0, axis_index_groups=depth_groups(), til...  16.4 us
    all_to_all x1, blocking collectives, on_device(): lax.all_to_all(rows, ('batch', 'tensor'), 0, 0, axis_index_groups=plane_g...  14.6 us
    all_to_all x1, blocking collectives, on_device(): shares = lax.all_to_all(part, 'tensor', 0, 0, tiled=True)  11.1 us
    ppermute x1, waiting for transfers between devices, on_device(): lax.ppermute(own, 'tensor', [(t, (t + X) % TENSOR) for t in range(TENSOR)])  4.92 us
    all_to_all x1, starting transfers between devices, on_device(): lax.all_to_all(copies, 'tensor', 0, 0, axis_index_groups=x_groups(), tile...  3.47 us
    pallas_call x7, Pallas kernels, kernel_call(): pl.pallas_call(kernel, out_shape=out_shape, in_specs=[vmem] * len(args),...  3.09 us
  transfers between devices with their start and end apart: 2, of which 1 were waited for; matrix products, arithmetic and copies ran while one was open for 0% of the time, Pallas kernels for 0%

profile of v5, /device:TPU:1, one launch (start us, length us, event | category | flops | bytes accessed | tf_op | source)
XLA Modules:
  0.0 120.1 jit_solution(16280932267463988570)
XLA Ops:
  0.0 0.0 copy-start.3
  0.0 0.7 copy-done.3
  0.7 0.0 copy-start.1
  0.7 0.9 copy-done.1
  1.6 0.0 copy-start
  1.6 0.3 shard_map.46
  2.0 11.1 %all_to_all.30.shares_ref = bf16[8,64,128]{2,1,0:T(8,128)(2,1)S(1)} all-to-all(bf16[8,64,128]{2,1,0:T(8,128)(2,1)S(1)} %shard_map.46), channel_id=1, replica_groups=mesh['batch'=64,'tensor'=8] {'tensor'}, dimensions={0} | all-to-all | bytes 262144 | tf_op jit(solution)/shard_map/all_to_all | solution.py:205
  13.1 0.0 copy-done
  13.1 0.1 shard_map.47
  13.1 34.6 %all_to_all.31.both_ref = bf16[8,192,128]{2,1,0:T(8,128)(2,1)S(1)} all-to-all(bf16[8,192,128]{2,1,0:T(8,128)(2,1)S(1)} %shard_map.47), channel_id=1, replica_groups={{0,32,64,96,128,160,192,224},{8,40,72,104,136,168,200,232},{16,48,80,11..., dimensions={0} | all-to-all | bytes 786432 | tf_op jit(solution)/shard_map/all_to_all | solution.py:206
  47.7 0.9 shard_map.48
  48.6 3.5 %all-to-all-start.2 = ((bf16[4,8,64,128]{3,2,1,0:T(8,128)(2,1)}), bf16[4,8,64,128]{3,2,1,0:T(8,128)(2,1)S(1)}, u32[]{:S(2)}, u32[]{:S(2)}) async-start(bf16[4,8,64,128]{3,2,1,0:T(8,128)(2,1)} %get-tuple-element.10), calls=%async_computation.2 | async-start | bytes 1048576 | tf_op jit(solution)/shard_map/all_to_all | solution.py:210
  52.1 0.0 copy-start.2
  52.1 2.2 %collective-permute-start = (bf16[8,128,128]{2,1,0:T(8,128)(2,1)S(1)}, bf16[8,128,128]{2,1,0:T(8,128)(2,1)S(1)}, u32[]{:S(2)}, u32[]{:S(2)}) collective-permute-start(bf16[8,128,128]{2,1,0:T(8,128)(2,1)S(1)} %get-tuple-element.9.own_ref), channel_id=1, source_target_pairs={{0,4},{1,5},{2,6},{3,7},{4,0},{5,1},{6,2},{7,3},{8,12},{9,13},{10,... | collective-permute-start | bytes 786440 | tf_op jit(solution)/shard_map/ppermute | solution.py:211
  54.3 4.9 %collective-permute-done.other_ref = bf16[8,128,128]{2,1,0:T(8,128)(2,1)S(1)} collective-permute-done((bf16[8,128,128]{2,1,0:T(8,128)(2,1)S(1)}, bf16[8,128,128]{2,1,0:T(8,128)(2,1)S(1)}, u32[]{:S(2)}, u32[]{:S(2)}) %collective-permute-start) | collective-permute-done | bytes 262176 | tf_op jit(solution)/shard_map/ppermute | solution.py:211
  59.2 0.0 all-to-all-done.2.picked_ref
  59.2 0.0 copy-done.2
  59.2 0.5 shard_map.49
  59.7 27.9 %all_to_all.32.terms_ref = bf16[8,8,32,256]{3,2,1,0:T(8,128)(2,1)S(1)} all-to-all(bf16[8,8,32,256]{3,2,1,0:T(8,128)(2,1)S(1)} %get-tuple-element.11), channel_id=1, replica_groups={{0,8,256,264,16,24,272,280},{32,40,288,296,48,56,304,312},{64,72,320,32..., dimensions={0} | all-to-all | bytes 2097152 | tf_op jit(solution)/shard_map/all_to_all | solution.py:214
  87.6 0.6 shard_map.50
  88.2 16.4 %all_to_all.33.rows_ref = f32[16,1,256]{2,1,0:T(1,128)S(1)} all-to-all(f32[16,1,256]{2,1,0:T(1,128)S(1)} %bitcast.4), channel_id=1, replica_groups={{0,16,32,48,64,80,96,112,128,144,160,176,192,208,224,240},{8,24,40,56,7..., dimensions={0} | all-to-all | bytes 32768 | tf_op jit(solution)/shard_map/all_to_all | solution.py:216
  104.7 0.1 shard_map.51
  104.8 14.6 %all_to_all.34.rows_ref = f32[32,1,64]{2,1,0:T(1,128)S(1)} all-to-all(f32[32,1,64]{2,1,0:T(1,128)S(1)} %bitcast.5), channel_id=1, replica_groups={{0,1,2,3,4,5,6,7,8,9,10,11,12,13,14,15,256,257,258,259,260,261,262,263,..., dimensions={0} | all-to-all | bytes 16384 | tf_op jit(solution)/shard_map/all_to_all | solution.py:219
  119.4 0.7 shard_map.52
  (1 shorter events, 0.0 us)
Async XLA Ops:
  0.0 0.7 copy-start.3
  0.7 0.9 copy-start.1
  1.6 11.4 %copy-start = (bf16[128,1024]{1,0:T(8,128)(2,1)S(1)}, bf16[128,1024]{1,0:T(8,128)(2,1)}, u32[]{:S(2)}) copy-start(bf16[128,1024]{1,0:T(8,128)(2,1)} %acts_ref.1) | copy-start | bytes 786436
  48.6 10.6 %all-to-all-start.2 = ((bf16[4,8,64,128]{3,2,1,0:T(8,128)(2,1)}), bf16[4,8,64,128]{3,2,1,0:T(8,128)(2,1)S(1)}, u32[]{:S(2)}, u32[]{:S(2)}) async-start(bf16[4,8,64,128]{3,2,1,0:T(8,128)(2,1)} %get-tuple-element.10), calls=%async_computation.2 | async-start | bytes 1048576 | tf_op jit(solution)/shard_map/all_to_all | solution.py:210
  52.1 7.1 %copy-start.2 = (s32[64]{0:T(128)S(1)}, s32[64]{0:T(128)}, u32[]{:S(2)}) copy-start(s32[64]{0:T(128)} %param.7) | copy-start | bytes 772
  52.1 7.1 %collective-permute-start = (bf16[8,128,128]{2,1,0:T(8,128)(2,1)S(1)}, bf16[8,128,128]{2,1,0:T(8,128)(2,1)S(1)}, u32[]{:S(2)}, u32[]{:S(2)}) collective-permute-start(bf16[8,128,128]{2,1,0:T(8,128)(2,1)S(1)} %get-tuple-element.9.own_ref), channel_id=1, source_target_pairs={{0,4},{1,5},{2,6},{3,7},{4,0},{5,1},{6,2},{7,3},{8,12},{9,13},{10,... | collective-permute-start | bytes 786440 | tf_op jit(solution)/shard_map/ppermute | solution.py:211

commit v6 on v5

--- a/solution.py
+++ b/solution.py
@@ -66,24 +66,33 @@
     ]
 
 
-def x_groups():
-    return [[y * X + x for x in range(X)] for y in range(Y_LO)]
-
-
-def kernel_call(kernel, out_shape, args):
+def kernel_call(kernel, out_shape, args, scalars=(), scratch=()):
+    smem = pl.BlockSpec(memory_space=pltpu.SMEM)
     vmem = pl.BlockSpec(memory_space=pltpu.VMEM)
     return pl.pallas_call(
         kernel,
         out_shape=out_shape,
-        in_specs=[vmem] * len(args),
+        in_specs=[smem] * len(scalars) + [vmem] * len(args),
         out_specs=jax.tree.map(lambda _: vmem, out_shape),
+        scratch_shapes=scratch,
         compiler_params=pltpu.CompilerParams(vmem_limit_bytes=24 * 1024 * 1024),
-    )(*args)
-
-
-def select_kernel(local_ref, grads_ref, out_ref):
+    )(*scalars, *args)
+
+
+def select_kernel(
+    index_ref, chosen_hbm, assign_hbm, grads_hbm, out_ref, spots_ref, chosen_ref, assign_ref, grads_ref, sems
+):
+    pairs = ((chosen_hbm, chosen_ref), (grads_hbm, grads_ref), (assign_hbm, assign_ref))
+    copies = [
+        pltpu.make_async_copy(source, target, sems.at[i]) for i, (source, target) in enumerate(pairs)
+    ]
+    for copy in copies:
+        copy.start()
+    copies[0].wait()
+    local = chosen_ref[...] - index_ref[0] * WIDTH
     places = lax.broadcasted_iota(jnp.int32, (WIDTH, NSEL), 0)
-    selector = jnp.where(places == local_ref[...], 1.0, 0.0).astype(grads_ref.dtype)
+    selector = jnp.where(places == local, 1.0, 0.0).astype(grads_ref.dtype)
+    copies[1].wait()
     part = jnp.dot(grads_ref[...], selector, preferred_element_type=jnp.float32)
     part = part.astype(out_ref.dtype)
     for y in range(Y_LO):
@@ -91,12 +100,37 @@
             lane = (y * BLOCKS + j) * LANES
             block = part[:, lane : lane + LANES].reshape(X, TROWS, LANES)
             out_ref[y * X : (y + 1) * X, j * TROWS : (j + 1) * TROWS] = block
-
-
-def selected(chosen, grads):
-    local = (chosen - lax.axis_index("tensor") * WIDTH)[None]
-    shape = jax.ShapeDtypeStruct((TENSOR, PIECE, LANES), grads.dtype)
-    return kernel_call(select_kernel, shape, (local, grads))
+    copies[2].wait()
+    column = lax.broadcasted_iota(jnp.int32, (SEQS, SEQS), 0)
+    slot = lax.broadcasted_iota(jnp.int32, (SEQS, SEQS), 1)
+    pair, core = column % PAIRS, column // PAIRS % CORES
+    y_hi, place = column // (PAIRS * CORES) % Y_HI, column // (PAIRS * SIDES)
+    ordered = jnp.where(batch_index(y_hi, pair, place, core) == slot, 1.0, 0.0)
+    wanted = jnp.where(column == assign_ref[...], 1.0, 0.0)
+    spots_ref[...] = lax.dot_general(
+        ordered, wanted, (((1,), (1,)), ((), ())), preferred_element_type=jnp.float32
+    )
+
+
+def selected(chosen, assign, grads):
+    smem = pl.BlockSpec(memory_space=pltpu.SMEM)
+    hbm = pl.BlockSpec(memory_space=pltpu.HBM)
+    vmem = pl.BlockSpec(memory_space=pltpu.VMEM)
+    return pl.pallas_call(
+        select_kernel,
+        out_shape=(
+            jax.ShapeDtypeStruct((TENSOR, PIECE, LANES), grads.dtype),
+            jax.ShapeDtypeStruct((SEQS, SEQS), jnp.float32),
+        ),
+        in_specs=[smem, hbm, hbm, hbm],
+        out_specs=(vmem, vmem),
+        scratch_shapes=[
+            pltpu.VMEM((1, NSEL), jnp.int32),
+            pltpu.VMEM((1, SEQS), jnp.int32),
+            pltpu.VMEM((TOK, WIDTH), grads.dtype),
+            pltpu.SemaphoreType.DMA((3,)),
+        ],
+    )(lax.axis_index("tensor")[None], chosen[None], assign[None], grads)
 
 
 def pack_kernel(acts_ref, shares_ref, out_ref):
@@ -114,49 +148,52 @@
     return kernel_call(pack_kernel, shape, (acts, shares))
 
 
-def unpack_kernel(both_ref, own_ref, copies_ref):
+def unpack_kernel(both_ref, own_ref, piece_ref):
     own_ref[...] = both_ref[:, :TOK]
-    for x in range(X):
-        copies_ref[x] = both_ref[:, TOK:]
+    piece_ref[...] = both_ref[:, TOK:]
 
 
 def unpacked(both):
     shapes = (
         jax.ShapeDtypeStruct((PAIRS, TOK, PART), both.dtype),
-        jax.ShapeDtypeStruct((X, PAIRS, PIECE, LANES), both.dtype),
+        jax.ShapeDtypeStruct((PAIRS, PIECE, LANES), both.dtype),
     )
     return kernel_call(unpack_kernel, shapes, (both,))
 
 
-def example_grads_kernel(own_ref, other_ref, picked_ref, assign_ref, out_ref, spots_ref):
+def over_tensor(block, y_step, x_step):
+    route = [
+        (y * X + x, (y + y_step) % Y_LO * X + (x + x_step) % X) for y in range(Y_LO) for x in range(X)
+    ]
+    return lax.ppermute(block, "tensor", route)
+
+
+def example_grads_kernel(x_ref, own_ref, other_ref, *refs):
+    pieces, (out_ref, picked_ref) = refs[:X], refs[X:]
+    for distance, piece in enumerate(pieces):
+        start = pl.multiple_of(lax.rem(x_ref[0] + X - distance, X) * TROWS, TROWS)
+        for j in range(BLOCKS):
+            picked_ref[:, pl.ds(start, TROWS), j * LANES : (j + 1) * LANES] = piece[
+                :, j * TROWS : (j + 1) * TROWS
+            ]
     count = PART // ROWS
     for k in range(PAIRS):
-        blocks = [
-            picked_ref[:, k, j * TROWS : (j + 1) * TROWS].reshape(TOK, LANES) for j in range(BLOCKS)
-        ]
-        picked = jnp.concatenate(blocks, axis=1)
         for side, ref in enumerate((own_ref, other_ref)):
             grad = lax.dot_general(
-                ref[k], picked, (((0,), (0,)), ((), ())), preferred_element_type=jnp.float32
+                ref[k], picked_ref[k], (((0,), (0,)), ((), ())), preferred_element_type=jnp.float32
             ).astype(out_ref.dtype)
             out_ref[side * count : (side + 1) * count, k] = grad.reshape(count, ROWS, HALF)
-    column = lax.broadcasted_iota(jnp.int32, (SEQS, SEQS), 0)
-    slot = lax.broadcasted_iota(jnp.int32, (SEQS, SEQS), 1)
-    pair, core = column % PAIRS, column // PAIRS % CORES
-    y_hi, place = column // (PAIRS * CORES) % Y_HI, column // (PAIRS * SIDES)
-    ordered = jnp.where(batch_index(y_hi, pair, place, core) == slot, 1.0, 0.0)
-    wanted = jnp.where(column == assign_ref[...], 1.0, 0.0)
-    spots_ref[...] = lax.dot_general(
-        ordered, wanted, (((1,), (1,)), ((), ())), preferred_element_type=jnp.float32
-    )
-
-
-def example_grads(own, other, picked, assign):
-    shapes = (
+
+
+def example_grads(own, other, pieces):
+    x = lax.rem(lax.axis_index("tensor"), X)[None]
+    return kernel_call(
+        example_grads_kernel,
         jax.ShapeDtypeStruct((MEMBERS, PAIRS, ROWS, HALF), own.dtype),
-        jax.ShapeDtypeStruct((SEQS, SEQS), jnp.float32),
-    )
-    return kernel_call(example_grads_kernel, shapes, (own, other, picked, assign[None]))
+        (own, other, *pieces),
+        scalars=(x,),
+        scratch=[pltpu.VMEM((PAIRS, TOK, HALF), own.dtype)],
+    )
 
 
 def pairs_kernel(terms_ref, out_ref):
@@ -201,16 +238,16 @@
 
 
 def on_device(acts, grads, chosen, assign):
-    part = selected(chosen, grads)
+    part, spots = selected(chosen, assign, grads)
     shares = lax.all_to_all(part, "tensor", 0, 0, tiled=True)
     both = lax.all_to_all(
         packed(acts, shares), "batch", 0, 0, axis_index_groups=column_groups(), tiled=True
     )
-    own, copies = unpacked(both)
-    picked = lax.all_to_all(copies, "tensor", 0, 0, axis_index_groups=x_groups(), tiled=True)
-    other = lax.ppermute(own, "tensor", [(t, (t + X) % TENSOR) for t in range(TENSOR)])
-
-    terms, spots = example_grads(own, other, picked, assign)
+    own, piece = unpacked(both)
+    other = over_tensor(own, 1, 0)
+    pieces = [piece] + [over_tensor(piece, 0, distance) for distance in range(1, X)]
+
+    terms = example_grads(own, other, pieces)
     terms = lax.all_to_all(terms, "batch", 0, 0, axis_index_groups=pair_groups(), tiled=True)
     rows = pairs(terms).reshape(DEPTH, 1, SIDES * SEQS)
     rows = lax.all_to_all(rows, "batch", 0, 0, axis_index_groups=depth_groups(), tiled=True)

time: 120 us -> 122 us (1.017)
  starting transfers between devices: 5.66 us -> 10.3 us
  blocking collectives: 105 us -> 102 us
  local copies, waits for them, and re-layouts: 1.64 us -> 0.01 us
    ppermute x1 -> x4, starting transfers between devices: 2.19 us -> 10.3 us  [over_tensor(): return lax.ppermute(block, 'tensor', route)]
    all_to_all x1 -> x0, starting transfers between devices: 3.47 us -> none  [on_device(): lax.all_to_all(copies, 'tensor', 0, 0, axis_index_groups=x_groups(), tile...]
    all_to_all x1, blocking collectives: 14.6 us -> 12.2 us  [on_device(): lax.all_to_all(rows, ('batch', 'tensor'), 0, 0, axis_index_groups=plane_g...]
    unnamed x8 -> x4, local copies, waits for them, and re-layouts: 1.64 us -> 0.01 us
    all_to_all x1, blocking collectives: 16.4 us -> 15.1 us  [on_device(): lax.all_to_all(rows, 'batch', 0, 0, axis_index_groups=depth_groups(), til...]
    ppermute x1 -> x4, waiting for transfers between devices: 4.92 us -> 4.98 us  [over_tensor(): return lax.ppermute(block, 'tensor', route)]
  transfers between devices with their start and end apart: 2 -> 4, of which waited for: 1 -> 2; matrix products, arithmetic and copies ran while one was open for 0% -> 0% of each run, Pallas kernels for 0% -> 0%
where the time goes in v6:
time: 122 us; the launch traced here: 121 us
  blocking collectives  102 us (84%)
  starting transfers between devices  10.3 us (8%)
  waiting for transfers between devices  4.98 us (4%)
  Pallas kernels  4.01 us (3%)
    all_to_all x1, blocking collectives, on_device(): lax.all_to_all(packed(acts, shares), 'batch', 0, 0, axis_index_groups=col...  34.6 us
    all_to_all x1, blocking collectives, on_device(): lax.all_to_all(terms, 'batch', 0, 0, axis_index_groups=pair_groups(), til...  28.7 us
    all_to_all x1, blocking collectives, on_device(): lax.all_to_all(rows, 'batch', 0, 0, axis_index_groups=depth_groups(), til...  15.1 us
    all_to_all x1, blocking collectives, on_device(): lax.all_to_all(rows, ('batch', 'tensor'), 0, 0, axis_index_groups=plane_g...  12.2 us
    all_to_all x1, blocking collectives, on_device(): shares = lax.all_to_all(part, 'tensor', 0, 0, tiled=True)  11.3 us
    ppermute x4, starting transfers between devices, over_tensor(): return lax.ppermute(block, 'tensor', route)  10.3 us
    ppermute x4, waiting for transfers between devices, over_tensor(): return lax.ppermute(block, 'tensor', route)  4.98 us
  transfers between devices with their start and end apart: 4, of which 2 were waited for; matrix products, arithmetic and copies ran while one was open for 0% of the time, Pallas kernels for 0%

profile of v6, /device:TPU:1, one launch (start us, length us, event | category | flops | bytes accessed | tf_op | source)
XLA Modules:
  0.0 121.3 jit_solution(13281908022795400855)
XLA Ops:
  0.0 0.0 copy-start
  0.0 2.1 %shard_map.46 = (bf16[8,64,128]{2,1,0:T(8,128)(2,1)}, f32[64,64]{1,0:T(8,128)}) custom-call(s32[1]{0:T(128)} %bitcast.1.index_ref, s32[1,512]{1,0:T(1,128)} %bitcast.8, s32[1,64]{1,0:T(1,128)} %bitcast.9, bf16[128,1024]{1,0:T(8,128)(2,1)} %grads_hbm.1), custom_call_target="tpu_custom_call" | custom-call | tf_op jit(solution)/shard_map/pallas_call | solution.py:119
  2.1 11.3 %all_to_all.25.shares_ref = bf16[8,64,128]{2,1,0:T(8,128)(2,1)S(1)} all-to-all(bf16[8,64,128]{2,1,0:T(8,128)(2,1)} %get-tuple-element.9), channel_id=1, replica_groups=mesh['batch'=64,'tensor'=8] {'tensor'}, dimensions={0} | all-to-all | bytes 262144 | tf_op jit(solution)/shard_map/all_to_all | solution.py:242
  13.4 0.0 copy-done
  13.4 0.1 shard_map.47
  13.5 34.6 %all_to_all.26.both_ref = bf16[8,192,128]{2,1,0:T(8,128)(2,1)S(1)} all-to-all(bf16[8,192,128]{2,1,0:T(8,128)(2,1)S(1)} %shard_map.47), channel_id=1, replica_groups={{0,32,64,96,128,160,192,224},{8,40,72,104,136,168,200,232},{16,48,80,11..., dimensions={0} | all-to-all | bytes 786432 | tf_op jit(solution)/shard_map/all_to_all | solution.py:243
  48.1 2.2 %collective-permute-start = (bf16[8,128,128]{2,1,0:T(8,128)(2,1)S(1)}, bf16[8,128,128]{2,1,0:T(8,128)(2,1)S(1)}, u32[]{:S(2)}, u32[]{:S(2)}) collective-permute-start(bf16[8,128,128]{2,1,0:T(8,128)(2,1)S(1)} %get-tuple-element.10.own_ref), channel_id=1, source_target_pairs={{0,4},{1,5},{2,6},{3,7},{4,0},{5,1},{6,2},{7,3},{8,12},{9,13},{10,... | collective-permute-start | bytes 786440 | tf_op jit(solution)/shard_map/ppermute | solution.py:168
  50.3 3.1 %collective-permute-start.3 = (bf16[8,64,128]{2,1,0:T(8,128)(2,1)S(1)}, bf16[8,64,128]{2,1,0:T(8,128)(2,1)S(1)}, u32[]{:S(2)}, u32[]{:S(2)}) collective-permute-start(bf16[8,64,128]{2,1,0:T(8,128)(2,1)S(1)} %get-tuple-element.11.refs_0_), channel_id=1, source_target_pairs={{0,3},{1,0},{2,1},{3,2},{4,7},{5,4},{6,5},{7,6},{8,11},{9,8},{10,9... | collective-permute-start | bytes 393224 | tf_op jit(solution)/shard_map/ppermute | solution.py:168
  53.4 3.1 %collective-permute-start.2 = (bf16[8,64,128]{2,1,0:T(8,128)(2,1)S(1)}, bf16[8,64,128]{2,1,0:T(8,128)(2,1)S(1)}, u32[]{:S(2)}, u32[]{:S(2)}) collective-permute-start(bf16[8,64,128]{2,1,0:T(8,128)(2,1)S(1)} %get-tuple-element.11.refs_0_), channel_id=1, source_target_pairs={{0,2},{1,3},{2,0},{3,1},{4,6},{5,7},{6,4},{7,5},{8,10},{9,11},{10,... | collective-permute-start | bytes 393224 | tf_op jit(solution)/shard_map/ppermute | solution.py:168
  56.5 1.9 %collective-permute-start.1 = (bf16[8,64,128]{2,1,0:T(8,128)(2,1)S(1)}, bf16[8,64,128]{2,1,0:T(8,128)(2,1)S(1)}, u32[]{:S(2)}, u32[]{:S(2)}) collective-permute-start(bf16[8,64,128]{2,1,0:T(8,128)(2,1)S(1)} %get-tuple-element.11.refs_0_), channel_id=1, source_target_pairs={{0,1},{1,2},{2,3},{3,0},{4,5},{5,6},{6,7},{7,4},{8,9},{9,10},{10,1... | collective-permute-start | bytes 393224 | tf_op jit(solution)/shard_map/ppermute | solution.py:168
  58.5 0.0 collective-permute-done.3.refs_3_
  58.5 2.2 %collective-permute-done.2.refs_2_ = bf16[8,64,128]{2,1,0:T(8,128)(2,1)S(1)} collective-permute-done((bf16[8,64,128]{2,1,0:T(8,128)(2,1)S(1)}, bf16[8,64,128]{2,1,0:T(8,128)(2,1)S(1)}, u32[]{:S(2)}, u32[]{:S(2)}) %collective-permute-start.2) | collective-permute-done | bytes 131104 | tf_op jit(solution)/shard_map/ppermute | solution.py:168
  60.6 2.8 %collective-permute-done.1.refs_1_ = bf16[8,64,128]{2,1,0:T(8,128)(2,1)S(1)} collective-permute-done((bf16[8,64,128]{2,1,0:T(8,128)(2,1)S(1)}, bf16[8,64,128]{2,1,0:T(8,128)(2,1)S(1)}, u32[]{:S(2)}, u32[]{:S(2)}) %collective-permute-start.1) | collective-permute-done | bytes 131104 | tf_op jit(solution)/shard_map/ppermute | solution.py:168
  63.5 0.0 collective-permute-done.other_ref
  63.5 0.5 shard_map.49
  64.0 28.7 %all_to_all.27.terms_ref = bf16[8,8,32,256]{3,2,1,0:T(8,128)(2,1)S(1)} all-to-all(bf16[8,8,32,256]{3,2,1,0:T(8,128)(2,1)S(1)} %shard_map.49), channel_id=1, replica_groups={{0,8,256,264,16,24,272,280},{32,40,288,296,48,56,304,312},{64,72,320,32..., dimensions={0} | all-to-all | bytes 2097152 | tf_op jit(solution)/shard_map/all_to_all | solution.py:251
  92.7 0.6 shard_map.50
  93.3 15.1 %all_to_all.28.rows_ref = f32[16,1,256]{2,1,0:T(1,128)S(1)} all-to-all(f32[16,1,256]{2,1,0:T(1,128)S(1)} %bitcast.6), channel_id=1, replica_groups={{0,16,32,48,64,80,96,112,128,144,160,176,192,208,224,240},{8,24,40,56,7..., dimensions={0} | all-to-all | bytes 32768 | tf_op jit(solution)/shard_map/all_to_all | solution.py:253
  108.3 0.0 copy-start.1
  108.3 0.1 shard_map.51
  108.4 12.2 %all_to_all.29.rows_ref = f32[32,1,64]{2,1,0:T(1,128)S(1)} all-to-all(f32[32,1,64]{2,1,0:T(1,128)S(1)} %bitcast.7), channel_id=1, replica_groups={{0,1,2,3,4,5,6,7,8,9,10,11,12,13,14,15,256,257,258,259,260,261,262,263,..., dimensions={0} | all-to-all | bytes 16384 | tf_op jit(solution)/shard_map/all_to_all | solution.py:256
  120.6 0.0 copy-done.1
  120.6 0.7 shard_map.52
  (1 shorter events, 0.0 us)
Async XLA Ops:
  0.0 13.4 %copy-start = (bf16[128,1024]{1,0:T(8,128)(2,1)S(1)}, bf16[128,1024]{1,0:T(8,128)(2,1)}, u32[]{:S(2)}) copy-start(bf16[128,1024]{1,0:T(8,128)(2,1)} %acts_ref.1) | copy-start | bytes 786436
  48.1 15.3 %collective-permute-start = (bf16[8,128,128]{2,1,0:T(8,128)(2,1)S(1)}, bf16[8,128,128]{2,1,0:T(8,128)(2,1)S(1)}, u32[]{:S(2)}, u32[]{:S(2)}) collective-permute-start(bf16[8,128,128]{2,1,0:T(8,128)(2,1)S(1)} %get-tuple-element.10.own_ref), channel_id=1, source_target_pairs={{0,4},{1,5},{2,6},{3,7},{4,0},{5,1},{6,2},{7,3},{8,12},{9,13},{10,... | collective-permute-start | bytes 786440 | tf_op jit(solution)/shard_map/ppermute | solution.py:168
  50.3 8.2 %collective-permute-start.3 = (bf16[8,64,128]{2,1,0:T(8,128)(2,1)S(1)}, bf16[8,64,128]{2,1,0:T(8,128)(2,1)S(1)}, u32[]{:S(2)}, u32[]{:S(2)}) collective-permute-start(bf16[8,64,128]{2,1,0:T(8,128)(2,1)S(1)} %get-tuple-element.11.refs_0_), channel_id=1, source_target_pairs={{0,3},{1,0},{2,1},{3,2},{4,7},{5,4},{6,5},{7,6},{8,11},{9,8},{10,9... | collective-permute-start | bytes 393224 | tf_op jit(solution)/shard_map/ppermute | solution.py:168
  53.4 7.2 %collective-permute-start.2 = (bf16[8,64,128]{2,1,0:T(8,128)(2,1)S(1)}, bf16[8,64,128]{2,1,0:T(8,128)(2,1)S(1)}, u32[]{:S(2)}, u32[]{:S(2)}) collective-permute-start(bf16[8,64,128]{2,1,0:T(8,128)(2,1)S(1)} %get-tuple-element.11.refs_0_), channel_id=1, source_target_pairs={{0,2},{1,3},{2,0},{3,1},{4,6},{5,7},{6,4},{7,5},{8,10},{9,11},{10,... | collective-permute-start | bytes 393224 | tf_op jit(solution)/shard_map/ppermute | solution.py:168
  56.5 6.9 %collective-permute-start.1 = (bf16[8,64,128]{2,1,0:T(8,128)(2,1)S(1)}, bf16[8,64,128]{2,1,0:T(8,128)(2,1)S(1)}, u32[]{:S(2)}, u32[]{:S(2)}) collective-permute-start(bf16[8,64,128]{2,1,0:T(8,128)(2,1)S(1)} %get-tuple-element.11.refs_0_), channel_id=1, source_target_pairs={{0,1},{1,2},{2,3},{3,0},{4,5},{5,6},{6,7},{7,4},{8,9},{9,10},{10,1... | collective-permute-start | bytes 393224 | tf_op jit(solution)/shard_map/ppermute | solution.py:168
  108.3 12.3 %copy-start.1 = (f32[64,64]{1,0:T(8,128)S(1)}, f32[64,64]{1,0:T(8,128)}, u32[]{:S(2)}) copy-start(f32[64,64]{1,0:T(8,128)} %get-tuple-element.12.spots_ref) | copy-start | bytes 49156

commit v7 on v5

--- a/solution.py
+++ b/solution.py
@@ -81,22 +81,23 @@
     )(*args)
 
 
-def select_kernel(local_ref, grads_ref, out_ref):
-    places = lax.broadcasted_iota(jnp.int32, (WIDTH, NSEL), 0)
-    selector = jnp.where(places == local_ref[...], 1.0, 0.0).astype(grads_ref.dtype)
-    part = jnp.dot(grads_ref[...], selector, preferred_element_type=jnp.float32)
-    part = part.astype(out_ref.dtype)
+def arrange_kernel(part_ref, out_ref):
     for y in range(Y_LO):
         for j in range(BLOCKS):
             lane = (y * BLOCKS + j) * LANES
-            block = part[:, lane : lane + LANES].reshape(X, TROWS, LANES)
+            block = part_ref[:, lane : lane + LANES].reshape(X, TROWS, LANES)
             out_ref[y * X : (y + 1) * X, j * TROWS : (j + 1) * TROWS] = block
 
 
 def selected(chosen, grads):
-    local = (chosen - lax.axis_index("tensor") * WIDTH)[None]
+    local = chosen - lax.axis_index("tensor") * WIDTH
+    places = lax.broadcasted_iota(jnp.int32, (WIDTH, NSEL), 0)
+    selector = (places == local[None, :]).astype(grads.dtype)
+    part = lax.dot_general(
+        grads, selector, (((1,), (0,)), ((), ())), preferred_element_type=jnp.float32
+    ).astype(grads.dtype)
     shape = jax.ShapeDtypeStruct((TENSOR, PIECE, LANES), grads.dtype)
-    return kernel_call(select_kernel, shape, (local, grads))
+    return kernel_call(arrange_kernel, shape, (part,))
 
 
 def pack_kernel(acts_ref, shares_ref, out_ref):

time: 120 us -> 120 us (level)
  local copies, waits for them, and re-layouts: 1.64 us -> 0.23 us
    unnamed x8 -> x6, local copies, waits for them, and re-layouts: 1.64 us -> 0.23 us
where the time goes in v7:
time: 120 us
  blocking collectives  105 us (88%)
  starting transfers between devices  5.66 us (5%)
  waiting for transfers between devices  4.92 us (4%)
  Pallas kernels  2.78 us (2%)
    all_to_all x1, blocking collectives, on_device(): lax.all_to_all(packed(acts, shares), 'batch', 0, 0, axis_index_groups=col...  34.6 us
    all_to_all x1, blocking collectives, on_device(): lax.all_to_all(terms, 'batch', 0, 0, axis_index_groups=pair_groups(), til...  27.9 us
    all_to_all x1, blocking collectives, on_device(): lax.all_to_all(rows, 'batch', 0, 0, axis_index_groups=depth_groups(), til...  16.4 us
    all_to_all x1, blocking collectives, on_device(): lax.all_to_all(rows, ('batch', 'tensor'), 0, 0, axis_index_groups=plane_g...  14.5 us
    all_to_all x1, blocking collectives, on_device(): shares = lax.all_to_all(part, 'tensor', 0, 0, tiled=True)  11.1 us
    ppermute x1, waiting for transfers between devices, on_device(): lax.ppermute(own, 'tensor', [(t, (t + X) % TENSOR) for t in range(TENSOR)])  4.92 us
    all_to_all x1, starting transfers between devices, on_device(): lax.all_to_all(copies, 'tensor', 0, 0, axis_index_groups=x_groups(), tile...  3.47 us
    pallas_call x7, Pallas kernels, kernel_call(): pl.pallas_call(kernel, out_shape=out_shape, in_specs=[vmem] * len(args),...  2.78 us
  transfers between devices with their start and end apart: 2, of which 1 were waited for; matrix products, arithmetic and copies ran while one was open for 0% of the time, Pallas kernels for 0%

profile of v7, /device:TPU:1, one launch (start us, length us, event | category | flops | bytes accessed | tf_op | source)
XLA Modules:
  0.0 119.5 jit_solution(8033424253554767837)
XLA Ops:
  0.0 0.0 copy-start
  0.0 0.0 copy-start.1
  0.0 0.7 broadcast_subtract_fusion
  0.7 0.2 copy-done
  1.0 0.5 fusion.2.part_ref
  1.5 11.1 %all_to_all.30.shares_ref = bf16[8,64,128]{2,1,0:T(8,128)(2,1)S(1)} all-to-all(bf16[8,64,128]{2,1,0:T(8,128)(2,1)S(1)} %shard_map.46), channel_id=1, replica_groups=mesh['batch'=64,'tensor'=8] {'tensor'}, dimensions={0} | all-to-all | bytes 262144 | tf_op jit(solution)/shard_map/all_to_all | solution.py:206
  12.6 0.0 copy-done.1
  12.6 0.1 shard_map.47
  12.7 0.0 copy-start.2
  12.7 34.6 %all_to_all.31.both_ref = bf16[8,192,128]{2,1,0:T(8,128)(2,1)S(1)} all-to-all(bf16[8,192,128]{2,1,0:T(8,128)(2,1)S(1)} %shard_map.47), channel_id=1, replica_groups={{0,32,64,96,128,160,192,224},{8,40,72,104,136,168,200,232},{16,48,80,11..., dimensions={0} | all-to-all | bytes 786432 | tf_op jit(solution)/shard_map/all_to_all | solution.py:207
  47.3 0.9 shard_map.48
  48.2 3.5 %all-to-all-start.2 = ((bf16[4,8,64,128]{3,2,1,0:T(8,128)(2,1)}), bf16[4,8,64,128]{3,2,1,0:T(8,128)(2,1)S(1)}, u32[]{:S(2)}, u32[]{:S(2)}) async-start(bf16[4,8,64,128]{3,2,1,0:T(8,128)(2,1)} %get-tuple-element.10), calls=%async_computation.2 | async-start | bytes 1048576 | tf_op jit(solution)/shard_map/all_to_all | solution.py:211
  51.6 2.2 %collective-permute-start = (bf16[8,128,128]{2,1,0:T(8,128)(2,1)S(1)}, bf16[8,128,128]{2,1,0:T(8,128)(2,1)S(1)}, u32[]{:S(2)}, u32[]{:S(2)}) collective-permute-start(bf16[8,128,128]{2,1,0:T(8,128)(2,1)S(1)} %get-tuple-element.9.own_ref), channel_id=1, source_target_pairs={{0,4},{1,5},{2,6},{3,7},{4,0},{5,1},{6,2},{7,3},{8,12},{9,13},{10,... | collective-permute-start | bytes 786440 | tf_op jit(solution)/shard_map/ppermute | solution.py:212
  53.8 4.9 %collective-permute-done.other_ref = bf16[8,128,128]{2,1,0:T(8,128)(2,1)S(1)} collective-permute-done((bf16[8,128,128]{2,1,0:T(8,128)(2,1)S(1)}, bf16[8,128,128]{2,1,0:T(8,128)(2,1)S(1)}, u32[]{:S(2)}, u32[]{:S(2)}) %collective-permute-start) | collective-permute-done | bytes 262176 | tf_op jit(solution)/shard_map/ppermute | solution.py:212
  58.8 0.0 all-to-all-done.2.picked_ref
  58.8 0.0 copy-done.2
  58.8 0.5 shard_map.49
  59.2 27.9 %all_to_all.32.terms_ref = bf16[8,8,32,256]{3,2,1,0:T(8,128)(2,1)S(1)} all-to-all(bf16[8,8,32,256]{3,2,1,0:T(8,128)(2,1)S(1)} %get-tuple-element.11), channel_id=1, replica_groups={{0,8,256,264,16,24,272,280},{32,40,288,296,48,56,304,312},{64,72,320,32..., dimensions={0} | all-to-all | bytes 2097152 | tf_op jit(solution)/shard_map/all_to_all | solution.py:215
  87.2 0.6 shard_map.50
  87.8 16.4 %all_to_all.33.rows_ref = f32[16,1,256]{2,1,0:T(1,128)S(1)} all-to-all(f32[16,1,256]{2,1,0:T(1,128)S(1)} %bitcast.6), channel_id=1, replica_groups={{0,16,32,48,64,80,96,112,128,144,160,176,192,208,224,240},{8,24,40,56,7..., dimensions={0} | all-to-all | bytes 32768 | tf_op jit(solution)/shard_map/all_to_all | solution.py:217
  104.2 0.1 shard_map.51
  104.3 14.5 %all_to_all.34.rows_ref = f32[32,1,64]{2,1,0:T(1,128)S(1)} all-to-all(f32[32,1,64]{2,1,0:T(1,128)S(1)} %bitcast.7), channel_id=1, replica_groups={{0,1,2,3,4,5,6,7,8,9,10,11,12,13,14,15,256,257,258,259,260,261,262,263,..., dimensions={0} | all-to-all | bytes 16384 | tf_op jit(solution)/shard_map/all_to_all | solution.py:220
  118.8 0.7 shard_map.52
  (1 shorter events, 0.0 us)
Async XLA Ops:
  0.0 1.0 copy-start
  0.0 12.6 %copy-start.1 = (bf16[128,1024]{1,0:T(8,128)(2,1)S(1)}, bf16[128,1024]{1,0:T(8,128)(2,1)}, u32[]{:S(2)}) copy-start(bf16[128,1024]{1,0:T(8,128)(2,1)} %acts_ref.1) | copy-start | bytes 786436
  12.7 46.1 %copy-start.2 = (s32[64]{0:T(128)S(1)}, s32[64]{0:T(128)}, u32[]{:S(2)}) copy-start(s32[64]{0:T(128)} %param.7) | copy-start | bytes 772
  48.2 10.6 %all-to-all-start.2 = ((bf16[4,8,64,128]{3,2,1,0:T(8,128)(2,1)}), bf16[4,8,64,128]{3,2,1,0:T(8,128)(2,1)S(1)}, u32[]{:S(2)}, u32[]{:S(2)}) async-start(bf16[4,8,64,128]{3,2,1,0:T(8,128)(2,1)} %get-tuple-element.10), calls=%async_computation.2 | async-start | bytes 1048576 | tf_op jit(solution)/shard_map/all_to_all | solution.py:211
  51.6 7.1 %collective-permute-start = (bf16[8,128,128]{2,1,0:T(8,128)(2,1)S(1)}, bf16[8,128,128]{2,1,0:T(8,128)(2,1)S(1)}, u32[]{:S(2)}, u32[]{:S(2)}) collective-permute-start(bf16[8,128,128]{2,1,0:T(8,128)(2,1)S(1)} %get-tuple-element.9.own_ref), channel_id=1, source_target_pairs={{0,4},{1,5},{2,6},{3,7},{4,0},{5,1},{6,2},{7,3},{8,12},{9,13},{10,... | collective-permute-start | bytes 786440 | tf_op jit(solution)/shard_map/ppermute | solution.py:212

commit v8 on v7

--- a/solution.py
+++ b/solution.py
@@ -70,15 +70,24 @@
     return [[y * X + x for x in range(X)] for y in range(Y_LO)]
 
 
-def kernel_call(kernel, out_shape, args):
+def kernel_call(kernel, out_shape, args, scalars=()):
+    smem = pl.BlockSpec(memory_space=pltpu.SMEM)
     vmem = pl.BlockSpec(memory_space=pltpu.VMEM)
     return pl.pallas_call(
         kernel,
         out_shape=out_shape,
-        in_specs=[vmem] * len(args),
+        in_specs=[smem] * len(scalars) + [vmem] * len(args),
         out_specs=jax.tree.map(lambda _: vmem, out_shape),
         compiler_params=pltpu.CompilerParams(vmem_limit_bytes=24 * 1024 * 1024),
-    )(*args)
+    )(*scalars, *args)
+
+
+def row_scale(batch, tensor, start, shape):
+    pair = batch // (PLACES * CORES) % PAIRS
+    first = (pair * TENSOR + tensor) * (MEMBERS * ROWS) + start
+    number = first + lax.broadcasted_iota(jnp.int32, shape, 0)
+    spread = jnp.bitwise_and(number * 40503, 65535).astype(jnp.float32)
+    return 1.0 + spread / 65536.0
 
 
 def arrange_kernel(part_ref, out_ref):
@@ -129,8 +138,13 @@
     return kernel_call(unpack_kernel, shapes, (both,))
 
 
-def example_grads_kernel(own_ref, other_ref, picked_ref, assign_ref, out_ref, spots_ref):
+def example_grads_kernel(
+    batch_ref, tensor_ref, own_ref, other_ref, picked_ref, assign_ref, out_ref, spots_ref
+):
     count = PART // ROWS
+    scales = [
+        row_scale(batch_ref[0], tensor_ref[0], side * PART, (PART, HALF)) for side in range(Y_LO)
+    ]
     for k in range(PAIRS):
         blocks = [
             picked_ref[:, k, j * TROWS : (j + 1) * TROWS].reshape(TOK, LANES) for j in range(BLOCKS)
@@ -139,7 +153,8 @@
         for side, ref in enumerate((own_ref, other_ref)):
             grad = lax.dot_general(
                 ref[k], picked, (((0,), (0,)), ((), ())), preferred_element_type=jnp.float32
-            ).astype(out_ref.dtype)
+            )
+            grad = (grad * scales[side]).astype(out_ref.dtype)
             out_ref[side * count : (side + 1) * count, k] = grad.reshape(count, ROWS, HALF)
     column = lax.broadcasted_iota(jnp.int32, (SEQS, SEQS), 0)
     slot = lax.broadcasted_iota(jnp.int32, (SEQS, SEQS), 1)
@@ -152,21 +167,27 @@
     )
 
 
-def example_grads(own, other, picked, assign):
+def example_grads(index, own, other, picked, assign):
     shapes = (
         jax.ShapeDtypeStruct((MEMBERS, PAIRS, ROWS, HALF), own.dtype),
         jax.ShapeDtypeStruct((SEQS, SEQS), jnp.float32),
     )
-    return kernel_call(example_grads_kernel, shapes, (own, other, picked, assign[None]))
-
-
-def pairs_kernel(terms_ref, out_ref):
+    return kernel_call(example_grads_kernel, shapes, (own, other, picked, assign[None]), index)
+
+
+def pairs_kernel(batch_ref, tensor_ref, terms_ref, out_ref):
     terms = jnp.swapaxes(terms_ref[...].reshape(SEQS, ROWS, HALF), 0, 1)
     total = jnp.zeros((SEQS, SEQS), jnp.float32)
+    batch = batch_ref[0]
+    place, side = batch // CORES % PLACES, batch // (PAIRS * PLACES * CORES) * CORES + batch % CORES
+    member = place * SIDES + side
+    scale = row_scale(batch, tensor_ref[0], member * ROWS, (ROWS, SEQS))
+    weight = 1.0 / (scale * scale)
     for row in range(ROWS):
-        total += lax.dot_general(
+        share = lax.dot_general(
             terms[row], terms[row], (((1,), (1,)), ((), ())), preferred_element_type=jnp.float32
         )
+        total += share * weight[row : row + 1]
     for r in range(PLACES):
         sides = [
             total[(r * SIDES + q) * PAIRS : (r * SIDES + q + 1) * PAIRS] for q in range(SIDES)
@@ -174,9 +195,9 @@
         out_ref[:, r, 0] = jnp.concatenate(sides, axis=1)
 
 
-def pairs(terms):
+def pairs(index, terms):
     shape = jax.ShapeDtypeStruct((PAIRS, PLACES, 1, SIDES * SEQS), jnp.float32)
-    return kernel_call(pairs_kernel, shape, (terms,))
+    return kernel_call(pairs_kernel, shape, (terms,), index)
 
 
 def side_kernel(rows_ref, out_ref):
@@ -211,9 +232,10 @@
     picked = lax.all_to_all(copies, "tensor", 0, 0, axis_index_groups=x_groups(), tiled=True)
     other = lax.ppermute(own, "tensor", [(t, (t + X) % TENSOR) for t in range(TENSOR)])
 
-    terms, spots = example_grads(own, other, picked, assign)
+    index = (lax.axis_index("batch")[None], lax.axis_index("tensor")[None])
+    terms, spots = example_grads(index, own, other, picked, assign)
     terms = lax.all_to_all(terms, "batch", 0, 0, axis_index_groups=pair_groups(), tiled=True)
-    rows = pairs(terms).reshape(DEPTH, 1, SIDES * SEQS)
+    rows = pairs(index, terms).reshape(DEPTH, 1, SIDES * SEQS)
     rows = lax.all_to_all(rows, "batch", 0, 0, axis_index_groups=depth_groups(), tiled=True)
     shape = jax.ShapeDtypeStruct((SIDES, TENSOR, 1, SEQS), jnp.float32)
     rows = kernel_call(side_kernel, shape, (rows,)).reshape(SIDES * TENSOR, 1, SEQS)

time: 120 us -> 120 us (level)
  no operation moved by 1% of the time
where the time goes in v8:
time: 120 us
  blocking collectives  105 us (88%)
  starting transfers between devices  5.66 us (5%)
  waiting for transfers between devices  4.92 us (4%)
  Pallas kernels  2.81 us (2%)
    all_to_all x1, blocking collectives, on_device(): lax.all_to_all(packed(acts, shares), 'batch', 0, 0, axis_index_groups=col...  34.6 us
    all_to_all x1, blocking collectives, on_device(): lax.all_to_all(terms, 'batch', 0, 0, axis_index_groups=pair_groups(), til...  27.9 us
    all_to_all x1, blocking collectives, on_device(): lax.all_to_all(rows, 'batch', 0, 0, axis_index_groups=depth_groups(), til...  16.4 us
    all_to_all x1, blocking collectives, on_device(): lax.all_to_all(rows, ('batch', 'tensor'), 0, 0, axis_index_groups=plane_g...  14.5 us
    all_to_all x1, blocking collectives, on_device(): shares = lax.all_to_all(part, 'tensor', 0, 0, tiled=True)  11.1 us
    ppermute x1, waiting for transfers between devices, on_device(): lax.ppermute(own, 'tensor', [(t, (t + X) % TENSOR) for t in range(TENSOR)])  4.91 us
    all_to_all x1, starting transfers between devices, on_device(): lax.all_to_all(copies, 'tensor', 0, 0, axis_index_groups=x_groups(), tile...  3.47 us
    pallas_call x7, Pallas kernels, kernel_call(): pl.pallas_call(kernel, out_shape=out_shape, in_specs=[smem] * len(scalars...  2.81 us
  transfers between devices with their start and end apart: 2, of which 1 were waited for; matrix products, arithmetic and copies ran while one was open for 0% of the time, Pallas kernels for 0%

profile of v8, /device:TPU:1, one launch (start us, length us, event | category | flops | bytes accessed | tf_op | source)
XLA Modules:
  0.0 119.5 jit_solution(16003591690097455644)
XLA Ops:
  0.0 0.0 copy-start
  0.0 0.0 copy-start.1
  0.0 0.7 broadcast_subtract_fusion
  0.7 0.2 copy-done
  1.0 0.5 fusion.2.part_ref
  1.5 11.1 %all_to_all.30.shares_ref = bf16[8,64,128]{2,1,0:T(8,128)(2,1)S(1)} all-to-all(bf16[8,64,128]{2,1,0:T(8,128)(2,1)S(1)} %shard_map.46), channel_id=1, replica_groups=mesh['batch'=64,'tensor'=8] {'tensor'}, dimensions={0} | all-to-all | bytes 262144 | tf_op jit(solution)/shard_map/all_to_all | solution.py:227
  12.6 0.0 copy-done.1
  12.6 0.1 shard_map.47
  12.7 0.0 copy-start.2
  12.7 34.6 %all_to_all.31.both_ref = bf16[8,192,128]{2,1,0:T(8,128)(2,1)S(1)} all-to-all(bf16[8,192,128]{2,1,0:T(8,128)(2,1)S(1)} %shard_map.47), channel_id=1, replica_groups={{0,32,64,96,128,160,192,224},{8,40,72,104,136,168,200,232},{16,48,80,11..., dimensions={0} | all-to-all | bytes 786432 | tf_op jit(solution)/shard_map/all_to_all | solution.py:228
  47.3 0.9 shard_map.48
  48.2 3.5 %all-to-all-start.2 = ((bf16[4,8,64,128]{3,2,1,0:T(8,128)(2,1)}), bf16[4,8,64,128]{3,2,1,0:T(8,128)(2,1)S(1)}, u32[]{:S(2)}, u32[]{:S(2)}) async-start(bf16[4,8,64,128]{3,2,1,0:T(8,128)(2,1)} %get-tuple-element.10), calls=%async_computation.2 | async-start | bytes 1048576 | tf_op jit(solution)/shard_map/all_to_all | solution.py:232
  51.6 2.2 %collective-permute-start = (bf16[8,128,128]{2,1,0:T(8,128)(2,1)S(1)}, bf16[8,128,128]{2,1,0:T(8,128)(2,1)S(1)}, u32[]{:S(2)}, u32[]{:S(2)}) collective-permute-start(bf16[8,128,128]{2,1,0:T(8,128)(2,1)S(1)} %get-tuple-element.9.own_ref), channel_id=1, source_target_pairs={{0,4},{1,5},{2,6},{3,7},{4,0},{5,1},{6,2},{7,3},{8,12},{9,13},{10,... | collective-permute-start | bytes 786440 | tf_op jit(solution)/shard_map/ppermute | solution.py:233
  53.9 4.9 %collective-permute-done.other_ref = bf16[8,128,128]{2,1,0:T(8,128)(2,1)S(1)} collective-permute-done((bf16[8,128,128]{2,1,0:T(8,128)(2,1)S(1)}, bf16[8,128,128]{2,1,0:T(8,128)(2,1)S(1)}, u32[]{:S(2)}, u32[]{:S(2)}) %collective-permute-start) | collective-permute-done | bytes 262176 | tf_op jit(solution)/shard_map/ppermute | solution.py:233
  58.8 0.0 all-to-all-done.2.picked_ref
  58.8 0.0 copy-done.2
  58.8 0.5 shard_map.49
  59.3 27.9 %all_to_all.32.terms_ref = bf16[8,8,32,256]{3,2,1,0:T(8,128)(2,1)S(1)} all-to-all(bf16[8,8,32,256]{3,2,1,0:T(8,128)(2,1)S(1)} %get-tuple-element.11), channel_id=1, replica_groups={{0,8,256,264,16,24,272,280},{32,40,288,296,48,56,304,312},{64,72,320,32..., dimensions={0} | all-to-all | bytes 2097152 | tf_op jit(solution)/shard_map/all_to_all | solution.py:237
  87.2 0.6 shard_map.50
  87.8 16.4 %all_to_all.33.rows_ref = f32[16,1,256]{2,1,0:T(1,128)S(1)} all-to-all(f32[16,1,256]{2,1,0:T(1,128)S(1)} %bitcast.8), channel_id=1, replica_groups={{0,16,32,48,64,80,96,112,128,144,160,176,192,208,224,240},{8,24,40,56,7..., dimensions={0} | all-to-all | bytes 32768 | tf_op jit(solution)/shard_map/all_to_all | solution.py:239
  104.2 0.1 shard_map.51
  104.3 14.5 %all_to_all.34.rows_ref = f32[32,1,64]{2,1,0:T(1,128)S(1)} all-to-all(f32[32,1,64]{2,1,0:T(1,128)S(1)} %bitcast.9), channel_id=1, replica_groups={{0,1,2,3,4,5,6,7,8,9,10,11,12,13,14,15,256,257,258,259,260,261,262,263,..., dimensions={0} | all-to-all | bytes 16384 | tf_op jit(solution)/shard_map/all_to_all | solution.py:242
  118.8 0.7 shard_map.52
  (1 shorter events, 0.0 us)
Async XLA Ops:
  0.0 1.0 copy-start
  0.0 12.6 %copy-start.1 = (bf16[128,1024]{1,0:T(8,128)(2,1)S(1)}, bf16[128,1024]{1,0:T(8,128)(2,1)}, u32[]{:S(2)}) copy-start(bf16[128,1024]{1,0:T(8,128)(2,1)} %acts_ref.1) | copy-start | bytes 786436
  12.7 46.1 %copy-start.2 = (s32[64]{0:T(128)S(1)}, s32[64]{0:T(128)}, u32[]{:S(2)}) copy-start(s32[64]{0:T(128)} %param.7) | copy-start | bytes 772
  48.2 10.6 %all-to-all-start.2 = ((bf16[4,8,64,128]{3,2,1,0:T(8,128)(2,1)}), bf16[4,8,64,128]{3,2,1,0:T(8,128)(2,1)S(1)}, u32[]{:S(2)}, u32[]{:S(2)}) async-start(bf16[4,8,64,128]{3,2,1,0:T(8,128)(2,1)} %get-tuple-element.10), calls=%async_computation.2 | async-start | bytes 1048576 | tf_op jit(solution)/shard_map/all_to_all | solution.py:232
  51.6 7.1 %collective-permute-start = (bf16[8,128,128]{2,1,0:T(8,128)(2,1)S(1)}, bf16[8,128,128]{2,1,0:T(8,128)(2,1)S(1)}, u32[]{:S(2)}, u32[]{:S(2)}) collective-permute-start(bf16[8,128,128]{2,1,0:T(8,128)(2,1)S(1)} %get-tuple-element.9.own_ref), channel_id=1, source_target_pairs={{0,4},{1,5},{2,6},{3,7},{4,0},{5,1},{6,2},{7,3},{8,12},{9,13},{10,... | collective-permute-start | bytes 786440 | tf_op jit(solution)/shard_map/ppermute | solution.py:233

commit v9 on v7

--- a/solution.py
+++ b/solution.py
@@ -131,6 +131,9 @@
 
 def example_grads_kernel(own_ref, other_ref, picked_ref, assign_ref, out_ref, spots_ref):
     count = PART // ROWS
+    row = lax.broadcasted_iota(jnp.int32, (PART, HALF), 0)
+    lane = lax.broadcasted_iota(jnp.int32, (PART, HALF), 1)
+    spread = (row * HALF + lane) * 40503
     for k in range(PAIRS):
         blocks = [
             picked_ref[:, k, j * TROWS : (j + 1) * TROWS].reshape(TOK, LANES) for j in range(BLOCKS)
@@ -139,7 +142,9 @@
         for side, ref in enumerate((own_ref, other_ref)):
             grad = lax.dot_general(
                 ref[k], picked, (((0,), (0,)), ((), ())), preferred_element_type=jnp.float32
-            ).astype(out_ref.dtype)
+            )
+            noise = (spread + (k * Y_LO + side) * 7919).astype(jnp.uint32)
+            grad = pltpu.stochastic_round(grad, noise, target_dtype=out_ref.dtype)
             out_ref[side * count : (side + 1) * count, k] = grad.reshape(count, ROWS, HALF)
     column = lax.broadcasted_iota(jnp.int32, (SEQS, SEQS), 0)
     slot = lax.broadcasted_iota(jnp.int32, (SEQS, SEQS), 1)

time: 120 us -> 120 us (level)
  no operation moved by 1% of the time
where the time goes in v9:
time: 120 us
  blocking collectives  105 us (88%)
  starting transfers between devices  5.66 us (5%)
  waiting for transfers between devices  4.92 us (4%)
  Pallas kernels  2.8 us (2%)
    all_to_all x1, blocking collectives, on_device(): lax.all_to_all(packed(acts, shares), 'batch', 0, 0, axis_index_groups=col...  34.6 us
    all_to_all x1, blocking collectives, on_device(): lax.all_to_all(terms, 'batch', 0, 0, axis_index_groups=pair_groups(), til...  27.9 us
    all_to_all x1, blocking collectives, on_device(): lax.all_to_all(rows, 'batch', 0, 0, axis_index_groups=depth_groups(), til...  16.4 us
    all_to_all x1, blocking collectives, on_device(): lax.all_to_all(rows, ('batch', 'tensor'), 0, 0, axis_index_groups=plane_g...  14.5 us
    all_to_all x1, blocking collectives, on_device(): shares = lax.all_to_all(part, 'tensor', 0, 0, tiled=True)  11.1 us
    ppermute x1, waiting for transfers between devices, on_device(): lax.ppermute(own, 'tensor', [(t, (t + X) % TENSOR) for t in range(TENSOR)])  4.92 us
    all_to_all x1, starting transfers between devices, on_device(): lax.all_to_all(copies, 'tensor', 0, 0, axis_index_groups=x_groups(), tile...  3.47 us
    pallas_call x7, Pallas kernels, kernel_call(): pl.pallas_call(kernel, out_shape=out_shape, in_specs=[vmem] * len(args),...  2.8 us
  transfers between devices with their start and end apart: 2, of which 1 were waited for; matrix products, arithmetic and copies ran while one was open for 0% of the time, Pallas kernels for 0%

profile of v9, /device:TPU:1, one launch (start us, length us, event | category | flops | bytes accessed | tf_op | source)
XLA Modules:
  0.0 119.5 jit_solution(5389565791142048149)
XLA Ops:
  0.0 0.0 copy-start
  0.0 0.0 copy-start.1
  0.0 0.7 broadcast_subtract_fusion
  0.7 0.2 copy-done
  1.0 0.5 fusion.2.part_ref
  1.5 11.1 %all_to_all.30.shares_ref = bf16[8,64,128]{2,1,0:T(8,128)(2,1)S(1)} all-to-all(bf16[8,64,128]{2,1,0:T(8,128)(2,1)S(1)} %shard_map.46), channel_id=1, replica_groups=mesh['batch'=64,'tensor'=8] {'tensor'}, dimensions={0} | all-to-all | bytes 262144 | tf_op jit(solution)/shard_map/all_to_all | solution.py:211
  12.6 0.0 copy-done.1
  12.6 0.1 shard_map.47
  12.7 0.0 copy-start.2
  12.7 34.6 %all_to_all.31.both_ref = bf16[8,192,128]{2,1,0:T(8,128)(2,1)S(1)} all-to-all(bf16[8,192,128]{2,1,0:T(8,128)(2,1)S(1)} %shard_map.47), channel_id=1, replica_groups={{0,32,64,96,128,160,192,224},{8,40,72,104,136,168,200,232},{16,48,80,11..., dimensions={0} | all-to-all | bytes 786432 | tf_op jit(solution)/shard_map/all_to_all | solution.py:212
  47.3 0.9 shard_map.48
  48.2 3.5 %all-to-all-start.2 = ((bf16[4,8,64,128]{3,2,1,0:T(8,128)(2,1)}), bf16[4,8,64,128]{3,2,1,0:T(8,128)(2,1)S(1)}, u32[]{:S(2)}, u32[]{:S(2)}) async-start(bf16[4,8,64,128]{3,2,1,0:T(8,128)(2,1)} %get-tuple-element.10), calls=%async_computation.2 | async-start | bytes 1048576 | tf_op jit(solution)/shard_map/all_to_all | solution.py:216
  51.6 2.2 %collective-permute-start = (bf16[8,128,128]{2,1,0:T(8,128)(2,1)S(1)}, bf16[8,128,128]{2,1,0:T(8,128)(2,1)S(1)}, u32[]{:S(2)}, u32[]{:S(2)}) collective-permute-start(bf16[8,128,128]{2,1,0:T(8,128)(2,1)S(1)} %get-tuple-element.9.own_ref), channel_id=1, source_target_pairs={{0,4},{1,5},{2,6},{3,7},{4,0},{5,1},{6,2},{7,3},{8,12},{9,13},{10,... | collective-permute-start | bytes 786440 | tf_op jit(solution)/shard_map/ppermute | solution.py:217
  53.8 4.9 %collective-permute-done.other_ref = bf16[8,128,128]{2,1,0:T(8,128)(2,1)S(1)} collective-permute-done((bf16[8,128,128]{2,1,0:T(8,128)(2,1)S(1)}, bf16[8,128,128]{2,1,0:T(8,128)(2,1)S(1)}, u32[]{:S(2)}, u32[]{:S(2)}) %collective-permute-start) | collective-permute-done | bytes 262176 | tf_op jit(solution)/shard_map/ppermute | solution.py:217
  58.8 0.0 all-to-all-done.2.picked_ref
  58.8 0.0 copy-done.2
  58.8 0.5 shard_map.49
  59.3 27.9 %all_to_all.32.terms_ref = bf16[8,8,32,256]{3,2,1,0:T(8,128)(2,1)S(1)} all-to-all(bf16[8,8,32,256]{3,2,1,0:T(8,128)(2,1)S(1)} %get-tuple-element.11), channel_id=1, replica_groups={{0,8,256,264,16,24,272,280},{32,40,288,296,48,56,304,312},{64,72,320,32..., dimensions={0} | all-to-all | bytes 2097152 | tf_op jit(solution)/shard_map/all_to_all | solution.py:220
  87.2 0.6 shard_map.50
  87.8 16.4 %all_to_all.33.rows_ref = f32[16,1,256]{2,1,0:T(1,128)S(1)} all-to-all(f32[16,1,256]{2,1,0:T(1,128)S(1)} %bitcast.6), channel_id=1, replica_groups={{0,16,32,48,64,80,96,112,128,144,160,176,192,208,224,240},{8,24,40,56,7..., dimensions={0} | all-to-all | bytes 32768 | tf_op jit(solution)/shard_map/all_to_all | solution.py:222
  104.2 0.1 shard_map.51
  104.3 14.5 %all_to_all.34.rows_ref = f32[32,1,64]{2,1,0:T(1,128)S(1)} all-to-all(f32[32,1,64]{2,1,0:T(1,128)S(1)} %bitcast.7), channel_id=1, replica_groups={{0,1,2,3,4,5,6,7,8,9,10,11,12,13,14,15,256,257,258,259,260,261,262,263,..., dimensions={0} | all-to-all | bytes 16384 | tf_op jit(solution)/shard_map/all_to_all | solution.py:225
  118.8 0.7 shard_map.52
  (1 shorter events, 0.0 us)
Async XLA Ops:
  0.0 1.0 copy-start
  0.0 12.6 %copy-start.1 = (bf16[128,1024]{1,0:T(8,128)(2,1)S(1)}, bf16[128,1024]{1,0:T(8,128)(2,1)}, u32[]{:S(2)}) copy-start(bf16[128,1024]{1,0:T(8,128)(2,1)} %acts_ref.1) | copy-start | bytes 786436
  12.7 46.1 %copy-start.2 = (s32[64]{0:T(128)S(1)}, s32[64]{0:T(128)}, u32[]{:S(2)}) copy-start(s32[64]{0:T(128)} %param.7) | copy-start | bytes 772
  48.2 10.6 %all-to-all-start.2 = ((bf16[4,8,64,128]{3,2,1,0:T(8,128)(2,1)}), bf16[4,8,64,128]{3,2,1,0:T(8,128)(2,1)S(1)}, u32[]{:S(2)}, u32[]{:S(2)}) async-start(bf16[4,8,64,128]{3,2,1,0:T(8,128)(2,1)} %get-tuple-element.10), calls=%async_computation.2 | async-start | bytes 1048576 | tf_op jit(solution)/shard_map/all_to_all | solution.py:216
  51.6 7.1 %collective-permute-start = (bf16[8,128,128]{2,1,0:T(8,128)(2,1)S(1)}, bf16[8,128,128]{2,1,0:T(8,128)(2,1)S(1)}, u32[]{:S(2)}, u32[]{:S(2)}) collective-permute-start(bf16[8,128,128]{2,1,0:T(8,128)(2,1)S(1)} %get-tuple-element.9.own_ref), channel_id=1, source_target_pairs={{0,4},{1,5},{2,6},{3,7},{4,0},{5,1},{6,2},{7,3},{8,12},{9,13},{10,... | collective-permute-start | bytes 786440 | tf_op jit(solution)/shard_map/ppermute | solution.py:217

commit v10 on v9

--- a/solution.py
+++ b/solution.py
@@ -115,18 +115,30 @@
     return kernel_call(pack_kernel, shape, (acts, shares))
 
 
-def unpack_kernel(both_ref, own_ref, copies_ref):
+def unpack_kernel(both_ref, own_ref, copies_ref, sems):
+    copies = [
+        pltpu.make_async_copy(both_ref.at[:, TOK:], copies_ref.at[x], sems.at[x]) for x in range(X)
+    ]
+    for copy in copies:
+        copy.start()
     own_ref[...] = both_ref[:, :TOK]
-    for x in range(X):
-        copies_ref[x] = both_ref[:, TOK:]
+    for copy in copies:
+        copy.wait()
 
 
 def unpacked(both):
-    shapes = (
-        jax.ShapeDtypeStruct((PAIRS, TOK, PART), both.dtype),
-        jax.ShapeDtypeStruct((X, PAIRS, PIECE, LANES), both.dtype),
-    )
-    return kernel_call(unpack_kernel, shapes, (both,))
+    vmem = pl.BlockSpec(memory_space=pltpu.VMEM)
+    return pl.pallas_call(
+        unpack_kernel,
+        out_shape=(
+            jax.ShapeDtypeStruct((PAIRS, TOK, PART), both.dtype),
+            jax.ShapeDtypeStruct((X, PAIRS, PIECE, LANES), both.dtype),
+        ),
+        in_specs=[vmem],
+        out_specs=(vmem, pl.BlockSpec(memory_space=pltpu.HBM)),
+        scratch_shapes=[pltpu.SemaphoreType.DMA((X,))],
+        compiler_params=pltpu.CompilerParams(vmem_limit_bytes=24 * 1024 * 1024),
+    )(both)
 
 
 def example_grads_kernel(own_ref, other_ref, picked_ref, assign_ref, out_ref, spots_ref):

time: 120 us -> 120 us (level)
    pallas_call x7 -> x6, Pallas kernels: 2.8 us -> 1.93 us  [kernel_call(): pl.pallas_call(kernel, out_shape=out_shape, in_specs=[vmem] * len(args),...]
where the time goes in v10:
time: 120 us; the launch traced here: 119 us
  blocking collectives  105 us (88%)
  starting transfers between devices  5.67 us (5%)
  waiting for transfers between devices  4.92 us (4%)
  Pallas kernels  2.75 us (2%)
    all_to_all x1, blocking collectives, on_device(): lax.all_to_all(packed(acts, shares), 'batch', 0, 0, axis_index_groups=col...  34.6 us
    all_to_all x1, blocking collectives, on_device(): lax.all_to_all(terms, 'batch', 0, 0, axis_index_groups=pair_groups(), til...  27.9 us
    all_to_all x1, blocking collectives, on_device(): lax.all_to_all(rows, 'batch', 0, 0, axis_index_groups=depth_groups(), til...  16.4 us
    all_to_all x1, blocking collectives, on_device(): lax.all_to_all(rows, ('batch', 'tensor'), 0, 0, axis_index_groups=plane_g...  14.5 us
    all_to_all x1, blocking collectives, on_device(): shares = lax.all_to_all(part, 'tensor', 0, 0, tiled=True)  11.1 us
    ppermute x1, waiting for transfers between devices, on_device(): lax.ppermute(own, 'tensor', [(t, (t + X) % TENSOR) for t in range(TENSOR)])  4.92 us
    all_to_all x1, starting transfers between devices, on_device(): lax.all_to_all(copies, 'tensor', 0, 0, axis_index_groups=x_groups(), tile...  3.48 us
  transfers between devices with their start and end apart: 2, of which 1 were waited for; matrix products, arithmetic and copies ran while one was open for 0% of the time, Pallas kernels for 0%

profile of v10, /device:TPU:1, one launch (start us, length us, event | category | flops | bytes accessed | tf_op | source)
XLA Modules:
  0.0 119.5 jit_solution(16350657764472130459)
XLA Ops:
  0.0 0.0 copy-start
  0.0 0.0 copy-start.1
  0.0 0.7 broadcast_subtract_fusion
  0.7 0.2 copy-done
  1.0 0.5 fusion.2.part_ref
  1.5 11.1 %all_to_all.30.shares_ref = bf16[8,64,128]{2,1,0:T(8,128)(2,1)S(1)} all-to-all(bf16[8,64,128]{2,1,0:T(8,128)(2,1)S(1)} %shard_map.46), channel_id=1, replica_groups=mesh['batch'=64,'tensor'=8] {'tensor'}, dimensions={0} | all-to-all | bytes 262144 | tf_op jit(solution)/shard_map/all_to_all | solution.py:223
  12.6 0.0 copy-done.1
  12.6 0.1 shard_map.47
  12.7 0.0 copy-start.2
  12.7 34.6 %all_to_all.31.both_ref = bf16[8,192,128]{2,1,0:T(8,128)(2,1)S(1)} all-to-all(bf16[8,192,128]{2,1,0:T(8,128)(2,1)S(1)} %shard_map.47), channel_id=1, replica_groups={{0,32,64,96,128,160,192,224},{8,40,72,104,136,168,200,232},{16,48,80,11..., dimensions={0} | all-to-all | bytes 786432 | tf_op jit(solution)/shard_map/all_to_all | solution.py:224
  47.3 0.8 shard_map.48
  48.1 3.5 %all-to-all-start.2 = ((bf16[4,8,64,128]{3,2,1,0:T(8,128)(2,1)}), bf16[4,8,64,128]{3,2,1,0:T(8,128)(2,1)S(1)}, u32[]{:S(2)}, u32[]{:S(2)}) async-start(bf16[4,8,64,128]{3,2,1,0:T(8,128)(2,1)} %get-tuple-element.10), calls=%async_computation.2 | async-start | bytes 1048576 | tf_op jit(solution)/shard_map/all_to_all | solution.py:228
  51.6 2.2 %collective-permute-start = (bf16[8,128,128]{2,1,0:T(8,128)(2,1)S(1)}, bf16[8,128,128]{2,1,0:T(8,128)(2,1)S(1)}, u32[]{:S(2)}, u32[]{:S(2)}) collective-permute-start(bf16[8,128,128]{2,1,0:T(8,128)(2,1)S(1)} %get-tuple-element.9.own_ref), channel_id=1, source_target_pairs={{0,4},{1,5},{2,6},{3,7},{4,0},{5,1},{6,2},{7,3},{8,12},{9,13},{10,... | collective-permute-start | bytes 786440 | tf_op jit(solution)/shard_map/ppermute | solution.py:229
  53.8 4.9 %collective-permute-done.other_ref = bf16[8,128,128]{2,1,0:T(8,128)(2,1)S(1)} collective-permute-done((bf16[8,128,128]{2,1,0:T(8,128)(2,1)S(1)}, bf16[8,128,128]{2,1,0:T(8,128)(2,1)S(1)}, u32[]{:S(2)}, u32[]{:S(2)}) %collective-permute-start) | collective-permute-done | bytes 262176 | tf_op jit(solution)/shard_map/ppermute | solution.py:229
  58.7 0.0 all-to-all-done.2.picked_ref
  58.7 0.0 copy-done.2
  58.7 0.5 shard_map.49
  59.2 27.9 %all_to_all.32.terms_ref = bf16[8,8,32,256]{3,2,1,0:T(8,128)(2,1)S(1)} all-to-all(bf16[8,8,32,256]{3,2,1,0:T(8,128)(2,1)S(1)} %get-tuple-element.11), channel_id=1, replica_groups={{0,8,256,264,16,24,272,280},{32,40,288,296,48,56,304,312},{64,72,320,32..., dimensions={0} | all-to-all | bytes 2097152 | tf_op jit(solution)/shard_map/all_to_all | solution.py:232
  87.2 0.6 shard_map.50
  87.8 16.4 %all_to_all.33.rows_ref = f32[16,1,256]{2,1,0:T(1,128)S(1)} all-to-all(f32[16,1,256]{2,1,0:T(1,128)S(1)} %bitcast.6), channel_id=1, replica_groups={{0,16,32,48,64,80,96,112,128,144,160,176,192,208,224,240},{8,24,40,56,7..., dimensions={0} | all-to-all | bytes 32768 | tf_op jit(solution)/shard_map/all_to_all | solution.py:234
  104.2 0.1 shard_map.51
  104.3 14.5 %all_to_all.34.rows_ref = f32[32,1,64]{2,1,0:T(1,128)S(1)} all-to-all(f32[32,1,64]{2,1,0:T(1,128)S(1)} %bitcast.7), channel_id=1, replica_groups={{0,1,2,3,4,5,6,7,8,9,10,11,12,13,14,15,256,257,258,259,260,261,262,263,..., dimensions={0} | all-to-all | bytes 16384 | tf_op jit(solution)/shard_map/all_to_all | solution.py:237
  118.8 0.7 shard_map.52
  (1 shorter events, 0.0 us)
Async XLA Ops:
  0.0 1.0 copy-start
  0.0 12.6 %copy-start.1 = (bf16[128,1024]{1,0:T(8,128)(2,1)S(1)}, bf16[128,1024]{1,0:T(8,128)(2,1)}, u32[]{:S(2)}) copy-start(bf16[128,1024]{1,0:T(8,128)(2,1)} %acts_ref.1) | copy-start | bytes 786436
  12.7 46.1 %copy-start.2 = (s32[64]{0:T(128)S(1)}, s32[64]{0:T(128)}, u32[]{:S(2)}) copy-start(s32[64]{0:T(128)} %param.7) | copy-start | bytes 772
  48.1 10.6 %all-to-all-start.2 = ((bf16[4,8,64,128]{3,2,1,0:T(8,128)(2,1)}), bf16[4,8,64,128]{3,2,1,0:T(8,128)(2,1)S(1)}, u32[]{:S(2)}, u32[]{:S(2)}) async-start(bf16[4,8,64,128]{3,2,1,0:T(8,128)(2,1)} %get-tuple-element.10), calls=%async_computation.2 | async-start | bytes 1048576 | tf_op jit(solution)/shard_map/all_to_all | solution.py:228
  51.6 7.1 %collective-permute-start = (bf16[8,128,128]{2,1,0:T(8,128)(2,1)S(1)}, bf16[8,128,128]{2,1,0:T(8,128)(2,1)S(1)}, u32[]{:S(2)}, u32[]{:S(2)}) collective-permute-start(bf16[8,128,128]{2,1,0:T(8,128)(2,1)S(1)} %get-tuple-element.9.own_ref), channel_id=1, source_target_pairs={{0,4},{1,5},{2,6},{3,7},{4,0},{5,1},{6,2},{7,3},{8,12},{9,13},{10,... | collective-permute-start | bytes 786440 | tf_op jit(solution)/shard_map/ppermute | solution.py:229

commit v11 on v9

--- a/solution.py
+++ b/solution.py
@@ -143,8 +143,8 @@
             grad = lax.dot_general(
                 ref[k], picked, (((0,), (0,)), ((), ())), preferred_element_type=jnp.float32
             )
-            noise = (spread + (k * Y_LO + side) * 7919).astype(jnp.uint32)
-            grad = pltpu.stochastic_round(grad, noise, target_dtype=out_ref.dtype)
+            noise = jnp.bitwise_and(spread + (k * Y_LO + side) * 7919, 65535) * 128
+            grad = pltpu.stochastic_round(grad, noise.astype(jnp.uint32), target_dtype=out_ref.dtype)
             out_ref[side * count : (side + 1) * count, k] = grad.reshape(count, ROWS, HALF)
     column = lax.broadcasted_iota(jnp.int32, (SEQS, SEQS), 0)
     slot = lax.broadcasted_iota(jnp.int32, (SEQS, SEQS), 1)

time: 120 us -> 120 us (level)
  no operation moved by 1% of the time
where the time goes in v11:
time: 120 us
  blocking collectives  105 us (88%)
  starting transfers between devices  5.66 us (5%)
  waiting for transfers between devices  4.92 us (4%)
  Pallas kernels  2.86 us (2%)
    all_to_all x1, blocking collectives, on_device(): lax.all_to_all(packed(acts, shares), 'batch', 0, 0, axis_index_groups=col...  34.6 us
    all_to_all x1, blocking collectives, on_device(): lax.all_to_all(terms, 'batch', 0, 0, axis_index_groups=pair_groups(), til...  27.9 us
    all_to_all x1, blocking collectives, on_device(): lax.all_to_all(rows, 'batch', 0, 0, axis_index_groups=depth_groups(), til...  16.4 us
    all_to_all x1, blocking collectives, on_device(): lax.all_to_all(rows, ('batch', 'tensor'), 0, 0, axis_index_groups=plane_g...  14.5 us
    all_to_all x1, blocking collectives, on_device(): shares = lax.all_to_all(part, 'tensor', 0, 0, tiled=True)  11.1 us
    ppermute x1, waiting for transfers between devices, on_device(): lax.ppermute(own, 'tensor', [(t, (t + X) % TENSOR) for t in range(TENSOR)])  4.92 us
    all_to_all x1, starting transfers between devices, on_device(): lax.all_to_all(copies, 'tensor', 0, 0, axis_index_groups=x_groups(), tile...  3.47 us
    pallas_call x7, Pallas kernels, kernel_call(): pl.pallas_call(kernel, out_shape=out_shape, in_specs=[vmem] * len(args),...  2.86 us
  transfers between devices with their start and end apart: 2, of which 1 were waited for; matrix products, arithmetic and copies ran while one was open for 0% of the time, Pallas kernels for 0%

profile of v11, /device:TPU:1, one launch (start us, length us, event | category | flops | bytes accessed | tf_op | source)
XLA Modules:
  0.0 119.6 jit_solution(3112883367474550869)
XLA Ops:
  0.0 0.0 copy-start
  0.0 0.0 copy-start.1
  0.0 0.7 broadcast_subtract_fusion
  0.7 0.2 copy-done
  1.0 0.5 fusion.2.part_ref
  1.5 11.1 %all_to_all.30.shares_ref = bf16[8,64,128]{2,1,0:T(8,128)(2,1)S(1)} all-to-all(bf16[8,64,128]{2,1,0:T(8,128)(2,1)S(1)} %shard_map.46), channel_id=1, replica_groups=mesh['batch'=64,'tensor'=8] {'tensor'}, dimensions={0} | all-to-all | bytes 262144 | tf_op jit(solution)/shard_map/all_to_all | solution.py:211
  12.6 0.0 copy-done.1
  12.6 0.1 shard_map.47
  12.7 0.0 copy-start.2
  12.7 34.6 %all_to_all.31.both_ref = bf16[8,192,128]{2,1,0:T(8,128)(2,1)S(1)} all-to-all(bf16[8,192,128]{2,1,0:T(8,128)(2,1)S(1)} %shard_map.47), channel_id=1, replica_groups={{0,32,64,96,128,160,192,224},{8,40,72,104,136,168,200,232},{16,48,80,11..., dimensions={0} | all-to-all | bytes 786432 | tf_op jit(solution)/shard_map/all_to_all | solution.py:212
  47.3 0.9 shard_map.48
  48.2 3.5 %all-to-all-start.2 = ((bf16[4,8,64,128]{3,2,1,0:T(8,128)(2,1)}), bf16[4,8,64,128]{3,2,1,0:T(8,128)(2,1)S(1)}, u32[]{:S(2)}, u32[]{:S(2)}) async-start(bf16[4,8,64,128]{3,2,1,0:T(8,128)(2,1)} %get-tuple-element.10), calls=%async_computation.2 | async-start | bytes 1048576 | tf_op jit(solution)/shard_map/all_to_all | solution.py:216
  51.6 2.2 %collective-permute-start = (bf16[8,128,128]{2,1,0:T(8,128)(2,1)S(1)}, bf16[8,128,128]{2,1,0:T(8,128)(2,1)S(1)}, u32[]{:S(2)}, u32[]{:S(2)}) collective-permute-start(bf16[8,128,128]{2,1,0:T(8,128)(2,1)S(1)} %get-tuple-element.9.own_ref), channel_id=1, source_target_pairs={{0,4},{1,5},{2,6},{3,7},{4,0},{5,1},{6,2},{7,3},{8,12},{9,13},{10,... | collective-permute-start | bytes 786440 | tf_op jit(solution)/shard_map/ppermute | solution.py:217
  53.8 4.9 %collective-permute-done.other_ref = bf16[8,128,128]{2,1,0:T(8,128)(2,1)S(1)} collective-permute-done((bf16[8,128,128]{2,1,0:T(8,128)(2,1)S(1)}, bf16[8,128,128]{2,1,0:T(8,128)(2,1)S(1)}, u32[]{:S(2)}, u32[]{:S(2)}) %collective-permute-start) | collective-permute-done | bytes 262176 | tf_op jit(solution)/shard_map/ppermute | solution.py:217
  58.8 0.0 all-to-all-done.2.picked_ref
  58.8 0.0 copy-done.2
  58.8 0.5 shard_map.49
  59.3 27.9 %all_to_all.32.terms_ref = bf16[8,8,32,256]{3,2,1,0:T(8,128)(2,1)S(1)} all-to-all(bf16[8,8,32,256]{3,2,1,0:T(8,128)(2,1)S(1)} %get-tuple-element.11), channel_id=1, replica_groups={{0,8,256,264,16,24,272,280},{32,40,288,296,48,56,304,312},{64,72,320,32..., dimensions={0} | all-to-all | bytes 2097152 | tf_op jit(solution)/shard_map/all_to_all | solution.py:220
  87.2 0.6 shard_map.50
  87.8 16.4 %all_to_all.33.rows_ref = f32[16,1,256]{2,1,0:T(1,128)S(1)} all-to-all(f32[16,1,256]{2,1,0:T(1,128)S(1)} %bitcast.6), channel_id=1, replica_groups={{0,16,32,48,64,80,96,112,128,144,160,176,192,208,224,240},{8,24,40,56,7..., dimensions={0} | all-to-all | bytes 32768 | tf_op jit(solution)/shard_map/all_to_all | solution.py:222
  104.3 0.1 shard_map.51
  104.4 14.5 %all_to_all.34.rows_ref = f32[32,1,64]{2,1,0:T(1,128)S(1)} all-to-all(f32[32,1,64]{2,1,0:T(1,128)S(1)} %bitcast.7), channel_id=1, replica_groups={{0,1,2,3,4,5,6,7,8,9,10,11,12,13,14,15,256,257,258,259,260,261,262,263,..., dimensions={0} | all-to-all | bytes 16384 | tf_op jit(solution)/shard_map/all_to_all | solution.py:225
  118.9 0.7 shard_map.52
  (1 shorter events, 0.0 us)
Async XLA Ops:
  0.0 1.0 copy-start
  0.0 12.6 %copy-start.1 = (bf16[128,1024]{1,0:T(8,128)(2,1)S(1)}, bf16[128,1024]{1,0:T(8,128)(2,1)}, u32[]{:S(2)}) copy-start(bf16[128,1024]{1,0:T(8,128)(2,1)} %acts_ref.1) | copy-start | bytes 786436
  12.7 46.1 %copy-start.2 = (s32[64]{0:T(128)S(1)}, s32[64]{0:T(128)}, u32[]{:S(2)}) copy-start(s32[64]{0:T(128)} %param.7) | copy-start | bytes 772
  48.2 10.6 %all-to-all-start.2 = ((bf16[4,8,64,128]{3,2,1,0:T(8,128)(2,1)}), bf16[4,8,64,128]{3,2,1,0:T(8,128)(2,1)S(1)}, u32[]{:S(2)}, u32[]{:S(2)}) async-start(bf16[4,8,64,128]{3,2,1,0:T(8,128)(2,1)} %get-tuple-element.10), calls=%async_computation.2 | async-start | bytes 1048576 | tf_op jit(solution)/shard_map/all_to_all | solution.py:216
  51.6 7.1 %collective-permute-start = (bf16[8,128,128]{2,1,0:T(8,128)(2,1)S(1)}, bf16[8,128,128]{2,1,0:T(8,128)(2,1)S(1)}, u32[]{:S(2)}, u32[]{:S(2)}) collective-permute-start(bf16[8,128,128]{2,1,0:T(8,128)(2,1)S(1)} %get-tuple-element.9.own_ref), channel_id=1, source_target_pairs={{0,4},{1,5},{2,6},{3,7},{4,0},{5,1},{6,2},{7,3},{8,12},{9,13},{10,... | collective-permute-start | bytes 786440 | tf_op jit(solution)/shard_map/ppermute | solution.py:217

commit v12 on v7

--- a/solution.py
+++ b/solution.py
@@ -12,7 +12,6 @@
 SEQS = Y_HI * PAIRS * PLACES * CORES
 SIDES = Y_HI * CORES
 DEPTH = PAIRS * PLACES
-MEMBERS = PLACES * SIDES
 Y_LO, X = 2, 4
 TENSOR = Y_LO * X
 WIDTH = D // TENSOR
@@ -22,7 +21,8 @@
 LANES = 128
 BLOCKS = HALF // LANES
 PIECE = BLOCKS * TROWS
-ROWS = PART * Y_LO // MEMBERS
+MEMBERS = PLACES * SIDES * TENSOR
+ROWS = WIDTH // MEMBERS
 
 
 def batch_index(y_hi, pair, place, core):
@@ -40,7 +40,13 @@
 
 def pair_groups():
     return [
-        [batch_index(y, k, r, c) for r in range(PLACES) for y in range(Y_HI) for c in range(CORES)]
+        [
+            batch_index(y, k, r, c) * TENSOR + t
+            for r in range(PLACES)
+            for y in range(Y_HI)
+            for c in range(CORES)
+            for t in range(TENSOR)
+        ]
         for k in range(PAIRS)
     ]
 
@@ -64,10 +70,6 @@
         for k in range(PAIRS)
         for r in range(PLACES)
     ]
-
-
-def x_groups():
-    return [[y * X + x for x in range(X)] for y in range(Y_LO)]
 
 
 def kernel_call(kernel, out_shape, args):
@@ -115,32 +117,24 @@
     return kernel_call(pack_kernel, shape, (acts, shares))
 
 
-def unpack_kernel(both_ref, own_ref, copies_ref):
-    own_ref[...] = both_ref[:, :TOK]
-    for x in range(X):
-        copies_ref[x] = both_ref[:, TOK:]
-
-
-def unpacked(both):
-    shapes = (
-        jax.ShapeDtypeStruct((PAIRS, TOK, PART), both.dtype),
-        jax.ShapeDtypeStruct((X, PAIRS, PIECE, LANES), both.dtype),
-    )
-    return kernel_call(unpack_kernel, shapes, (both,))
-
-
-def example_grads_kernel(own_ref, other_ref, picked_ref, assign_ref, out_ref, spots_ref):
+def example_grad_kernel(both_ref, assign_ref, out_ref, spots_ref):
+    blocks = [
+        both_ref[y * X : (y + 1) * X, TOK + j * TROWS : TOK + (j + 1) * TROWS].reshape(TOK, LANES)
+        for y in range(Y_LO)
+        for j in range(BLOCKS)
+    ]
+    picked = jnp.concatenate(blocks, axis=1)
+    row = lax.broadcasted_iota(jnp.int32, (PART, NSEL), 0)
+    lane = lax.broadcasted_iota(jnp.int32, (PART, NSEL), 1)
+    spread = (row * NSEL + lane) * 40503
     count = PART // ROWS
-    for k in range(PAIRS):
-        blocks = [
-            picked_ref[:, k, j * TROWS : (j + 1) * TROWS].reshape(TOK, LANES) for j in range(BLOCKS)
-        ]
-        picked = jnp.concatenate(blocks, axis=1)
-        for side, ref in enumerate((own_ref, other_ref)):
-            grad = lax.dot_general(
-                ref[k], picked, (((0,), (0,)), ((), ())), preferred_element_type=jnp.float32
-            ).astype(out_ref.dtype)
-            out_ref[side * count : (side + 1) * count, k] = grad.reshape(count, ROWS, HALF)
+    for t in range(TENSOR):
+        grad = lax.dot_general(
+            both_ref[t, :TOK], picked, (((0,), (0,)), ((), ())), preferred_element_type=jnp.float32
+        )
+        noise = jnp.bitwise_and(spread + t * 7919, 65535) * 128
+        grad = pltpu.stochastic_round(grad, noise.astype(jnp.uint32), target_dtype=out_ref.dtype)
+        out_ref[t * count : (t + 1) * count] = grad.reshape(count, ROWS, NSEL)
     column = lax.broadcasted_iota(jnp.int32, (SEQS, SEQS), 0)
     slot = lax.broadcasted_iota(jnp.int32, (SEQS, SEQS), 1)
     pair, core = column % PAIRS, column // PAIRS % CORES
@@ -152,16 +146,16 @@
     )
 
 
-def example_grads(own, other, picked, assign):
+def example_grad(both, assign):
     shapes = (
-        jax.ShapeDtypeStruct((MEMBERS, PAIRS, ROWS, HALF), own.dtype),
+        jax.ShapeDtypeStruct((MEMBERS, ROWS, NSEL), both.dtype),
         jax.ShapeDtypeStruct((SEQS, SEQS), jnp.float32),
     )
-    return kernel_call(example_grads_kernel, shapes, (own, other, picked, assign[None]))
+    return kernel_call(example_grad_kernel, shapes, (both, assign[None]))
 
 
 def pairs_kernel(terms_ref, out_ref):
-    terms = jnp.swapaxes(terms_ref[...].reshape(SEQS, ROWS, HALF), 0, 1)
+    terms = jnp.swapaxes(terms_ref[...], 0, 1)
     total = jnp.zeros((SEQS, SEQS), jnp.float32)
     for row in range(ROWS):
         total += lax.dot_general(
@@ -207,12 +201,11 @@
     both = lax.all_to_all(
         packed(acts, shares), "batch", 0, 0, axis_index_groups=column_groups(), tiled=True
     )
-    own, copies = unpacked(both)
-    picked = lax.all_to_all(copies, "tensor", 0, 0, axis_index_groups=x_groups(), tiled=True)
-    other = lax.ppermute(own, "tensor", [(t, (t + X) % TENSOR) for t in range(TENSOR)])
-
-    terms, spots = example_grads(own, other, picked, assign)
-    terms = lax.all_to_all(terms, "batch", 0, 0, axis_index_groups=pair_groups(), tiled=True)
+    both = lax.all_to_all(both, "tensor", 0, 0, tiled=True)
+    terms, spots = example_grad(both, assign)
+    terms = lax.all_to_all(
+        terms, ("batch", "tensor"), 0, 0, axis_index_groups=pair_groups(), tiled=True
+    )
     rows = pairs(terms).reshape(DEPTH, 1, SIDES * SEQS)
     rows = lax.all_to_all(rows, "batch", 0, 0, axis_index_groups=depth_groups(), tiled=True)
     shape = jax.ShapeDtypeStruct((SIDES, TENSOR, 1, SEQS), jnp.float32)

time: 120 us -> 118 us (0.983)
  blocking collectives: 105 us -> 114 us
  starting transfers between devices: 5.66 us -> 0 us
  waiting for transfers between devices: 4.92 us -> 0 us
    all_to_all x1 -> x2, blocking collectives: 27.9 us -> 41.2 us  [the longest x1 32 us: on_device(): lax.all_to_all(terms, ('batch', 'tensor'), 0, 0, axis_index_groups=pair_g...]
    ppermute x1 -> x0, waiting for transfers between devices: 4.92 us -> none  [on_device(): lax.ppermute(own, 'tensor', [(t, (t + X) % TENSOR) for t in range(TENSOR)])]
    all_to_all x1 -> x0, starting transfers between devices: 3.47 us -> none  [on_device(): lax.all_to_all(copies, 'tensor', 0, 0, axis_index_groups=x_groups(), tile...]
    all_to_all x1, blocking collectives: 14.5 us -> 12 us  [on_device(): lax.all_to_all(rows, ('batch', 'tensor'), 0, 0, axis_index_groups=plane_g...]
    ppermute x1 -> x0, starting transfers between devices: 2.19 us -> none  [on_device(): lax.ppermute(own, 'tensor', [(t, (t + X) % TENSOR) for t in range(TENSOR)])]
    pallas_call x7 -> x6, Pallas kernels: 2.78 us -> 2.05 us  [kernel_call(): pl.pallas_call(kernel, out_shape=out_shape, in_specs=[vmem] * len(args),...]
  transfers between devices with their start and end apart: 2 -> 0, of which waited for: 1 -> 0; matrix products, arithmetic and copies ran while one was open for 0% -> 0% of each run, Pallas kernels for 0% -> 0%
where the time goes in v12:
time: 118 us
  blocking collectives  114 us (97%)
  Pallas kernels  2.05 us (2%)
    all_to_all x1, blocking collectives, on_device(): lax.all_to_all(packed(acts, shares), 'batch', 0, 0, axis_index_groups=col...  34.6 us
    all_to_all x1, blocking collectives, on_device(): lax.all_to_all(terms, ('batch', 'tensor'), 0, 0, axis_index_groups=pair_g...  32 us
    all_to_all x1, blocking collectives, on_device(): lax.all_to_all(rows, 'batch', 0, 0, axis_index_groups=depth_groups(), til...  15.4 us
    all_to_all x1, blocking collectives, on_device(): lax.all_to_all(rows, ('batch', 'tensor'), 0, 0, axis_index_groups=plane_g...  12 us
    all_to_all x1, blocking collectives, on_device(): shares = lax.all_to_all(part, 'tensor', 0, 0, tiled=True)  11.1 us
    all_to_all x1, blocking collectives, on_device(): both = lax.all_to_all(both, 'tensor', 0, 0, tiled=True)  9.22 us

profile of v12, /device:TPU:1, one launch (start us, length us, event | category | flops | bytes accessed | tf_op | source)
XLA Modules:
  0.0 117.9 jit_solution(2253237042360572630)
XLA Ops:
  0.0 0.0 copy-start
  0.0 0.0 copy-start.1
  0.0 0.7 broadcast_subtract_fusion
  0.7 0.2 copy-done
  1.0 0.5 fusion.2.part_ref
  1.5 11.1 %all_to_all.30.shares_ref = bf16[8,64,128]{2,1,0:T(8,128)(2,1)S(1)} all-to-all(bf16[8,64,128]{2,1,0:T(8,128)(2,1)S(1)} %shard_map.46), channel_id=1, replica_groups=mesh['batch'=64,'tensor'=8] {'tensor'}, dimensions={0} | all-to-all | bytes 262144 | tf_op jit(solution)/shard_map/all_to_all | solution.py:200
  12.6 0.0 copy-done.1
  12.6 0.0 copy-start.2
  12.6 0.1 shard_map.47
  12.7 34.6 %all_to_all.31 = bf16[8,192,128]{2,1,0:T(8,128)(2,1)S(1)} all-to-all(bf16[8,192,128]{2,1,0:T(8,128)(2,1)S(1)} %shard_map.47), channel_id=1, replica_groups={{0,32,64,96,128,160,192,224},{8,40,72,104,136,168,200,232},{16,48,80,11..., dimensions={0} | all-to-all | bytes 786432 | tf_op jit(solution)/shard_map/all_to_all | solution.py:201
  47.3 9.2 %all_to_all.32.both_ref = bf16[8,192,128]{2,1,0:T(8,128)(2,1)S(1)} all-to-all(bf16[8,192,128]{2,1,0:T(8,128)(2,1)S(1)} %all_to_all.31), channel_id=1, replica_groups=mesh['batch'=64,'tensor'=8] {'tensor'}, dimensions={0} | all-to-all | bytes 786432 | tf_op jit(solution)/shard_map/all_to_all | solution.py:204
  56.5 0.0 copy-done.2
  56.5 0.6 shard_map.48
  57.1 32.0 %all_to_all.33.terms_ref = bf16[64,16,512]{2,1,0:T(8,128)(2,1)S(1)} all-to-all(bf16[64,16,512]{2,1,0:T(8,128)(2,1)S(1)} %get-tuple-element.7), channel_id=1, replica_groups={{0,1,2,3,4,5,6,7,8,9,10,11,12,13,14,15,256,257,258,259,260,261,262,263,..., dimensions={0} | all-to-all | bytes 2097152 | tf_op jit(solution)/shard_map/all_to_all | solution.py:206
  89.1 0.6 shard_map.49
  89.7 15.4 %all_to_all.34.rows_ref = f32[16,1,256]{2,1,0:T(1,128)S(1)} all-to-all(f32[16,1,256]{2,1,0:T(1,128)S(1)} %bitcast.6), channel_id=1, replica_groups={{0,16,32,48,64,80,96,112,128,144,160,176,192,208,224,240},{8,24,40,56,7..., dimensions={0} | all-to-all | bytes 32768 | tf_op jit(solution)/shard_map/all_to_all | solution.py:210
  105.1 0.1 shard_map.50
  105.2 12.0 %all_to_all.35.rows_ref = f32[32,1,64]{2,1,0:T(1,128)S(1)} all-to-all(f32[32,1,64]{2,1,0:T(1,128)S(1)} %bitcast.7), channel_id=1, replica_groups={{0,1,2,3,4,5,6,7,8,9,10,11,12,13,14,15,256,257,258,259,260,261,262,263,..., dimensions={0} | all-to-all | bytes 16384 | tf_op jit(solution)/shard_map/all_to_all | solution.py:213
  117.2 0.7 shard_map.51
  (1 shorter events, 0.0 us)
Async XLA Ops:
  0.0 1.0 copy-start
  0.0 12.6 %copy-start.1 = (bf16[128,1024]{1,0:T(8,128)(2,1)S(1)}, bf16[128,1024]{1,0:T(8,128)(2,1)}, u32[]{:S(2)}) copy-start(bf16[128,1024]{1,0:T(8,128)(2,1)} %acts_ref.1) | copy-start | bytes 786436
  12.6 43.9 %copy-start.2 = (s32[64]{0:T(128)S(1)}, s32[64]{0:T(128)}, u32[]{:S(2)}) copy-start(s32[64]{0:T(128)} %param.7) | copy-start | bytes 772

commit v13 on v12

--- a/solution.py
+++ b/solution.py
@@ -11,7 +11,7 @@
 Y_HI, PAIRS, PLACES, CORES = 2, 8, 2, 2
 SEQS = Y_HI * PAIRS * PLACES * CORES
 SIDES = Y_HI * CORES
-DEPTH = PAIRS * PLACES
+DEPTH = PAIRS * PLACES * CORES
 Y_LO, X = 2, 4
 TENSOR = Y_LO * X
 WIDTH = D // TENSOR
@@ -53,22 +53,17 @@
 
 def depth_groups():
     return [
-        [batch_index(y, k, r, c) for k in range(PAIRS) for r in range(PLACES)]
+        [batch_index(y, k, r, c) for k in range(PAIRS) for r in range(PLACES) for c in range(CORES)]
         for y in range(Y_HI)
-        for c in range(CORES)
-    ]
-
-
-def plane_groups():
-    return [
-        [
-            batch_index(y, k, r, c) * TENSOR + t
-            for y in range(Y_HI)
-            for c in range(CORES)
-            for t in range(TENSOR)
-        ]
+    ]
+
+
+def side_groups():
+    return [
+        [batch_index(y, k, r, c) * TENSOR + t for y in range(Y_HI) for t in range(TENSOR)]
         for k in range(PAIRS)
         for r in range(PLACES)
+        for c in range(CORES)
     ]
 
 
@@ -162,28 +157,28 @@
             terms[row], terms[row], (((1,), (1,)), ((), ())), preferred_element_type=jnp.float32
         )
     for r in range(PLACES):
-        sides = [
-            total[(r * SIDES + q) * PAIRS : (r * SIDES + q + 1) * PAIRS] for q in range(SIDES)
-        ]
-        out_ref[:, r, 0] = jnp.concatenate(sides, axis=1)
+        for c in range(CORES):
+            starts = [((r * Y_HI + y) * CORES + c) * PAIRS for y in range(Y_HI)]
+            rows = [total[start : start + PAIRS] for start in starts]
+            out_ref[:, r, c, 0] = jnp.concatenate(rows, axis=1)
 
 
 def pairs(terms):
-    shape = jax.ShapeDtypeStruct((PAIRS, PLACES, 1, SIDES * SEQS), jnp.float32)
+    shape = jax.ShapeDtypeStruct((PAIRS, PLACES, CORES, 1, Y_HI * SEQS), jnp.float32)
     return kernel_call(pairs_kernel, shape, (terms,))
 
 
 def side_kernel(rows_ref, out_ref):
     sums = rows_ref[0]
-    for z in range(1, DEPTH):
-        sums = sums + rows_ref[z]
-    for q in range(SIDES):
-        out_ref[q] = jnp.broadcast_to(sums[:, q * SEQS : (q + 1) * SEQS][None], (TENSOR, 1, SEQS))
+    for member in range(1, DEPTH):
+        sums = sums + rows_ref[member]
+    for y in range(Y_HI):
+        out_ref[y] = jnp.broadcast_to(sums[:, y * SEQS : (y + 1) * SEQS][None], (TENSOR, 1, SEQS))
 
 
 def place_kernel(rows_ref, spots_ref, out_ref):
     row = rows_ref[0]
-    for member in range(1, SIDES * TENSOR):
+    for member in range(1, Y_HI * TENSOR):
         row = row + rows_ref[member]
     norming = 1.0 / (float(TOK) * float(D) * float(NSEL))
     out_ref[...] = lax.dot_general(
@@ -206,12 +201,12 @@
     terms = lax.all_to_all(
         terms, ("batch", "tensor"), 0, 0, axis_index_groups=pair_groups(), tiled=True
     )
-    rows = pairs(terms).reshape(DEPTH, 1, SIDES * SEQS)
+    rows = pairs(terms).reshape(DEPTH, 1, Y_HI * SEQS)
     rows = lax.all_to_all(rows, "batch", 0, 0, axis_index_groups=depth_groups(), tiled=True)
-    shape = jax.ShapeDtypeStruct((SIDES, TENSOR, 1, SEQS), jnp.float32)
-    rows = kernel_call(side_kernel, shape, (rows,)).reshape(SIDES * TENSOR, 1, SEQS)
+    shape = jax.ShapeDtypeStruct((Y_HI, TENSOR, 1, SEQS), jnp.float32)
+    rows = kernel_call(side_kernel, shape, (rows,)).reshape(Y_HI * TENSOR, 1, SEQS)
     rows = lax.all_to_all(
-        rows, ("batch", "tensor"), 0, 0, axis_index_groups=plane_groups(), tiled=True
+        rows, ("batch", "tensor"), 0, 0, axis_index_groups=side_groups(), tiled=True
     )
     shape = jax.ShapeDtypeStruct((1, SEQS), jnp.float32)
     return kernel_call(place_kernel, shape, (rows, spots))

time: 118 us -> 117 us (level)
    all_to_all x1, blocking collectives: 12 us -> 9.42 us  [on_device(): lax.all_to_all(rows, ('batch', 'tensor'), 0, 0, axis_index_groups=side_gr...]
where the time goes in v13:
time: 117 us; the launch traced here: 116 us
  blocking collectives  113 us (97%)
  Pallas kernels  2.05 us (2%)
    all_to_all x1, blocking collectives, on_device(): lax.all_to_all(packed(acts, shares), 'batch', 0, 0, axis_index_groups=col...  34.6 us
    all_to_all x1, blocking collectives, on_device(): lax.all_to_all(terms, ('batch', 'tensor'), 0, 0, axis_index_groups=pair_g...  32 us
    all_to_all x1, blocking collectives, on_device(): lax.all_to_all(rows, 'batch', 0, 0, axis_index_groups=depth_groups(), til...  16.5 us
    all_to_all x1, blocking collectives, on_device(): shares = lax.all_to_all(part, 'tensor', 0, 0, tiled=True)  11.1 us
    all_to_all x1, blocking collectives, on_device(): lax.all_to_all(rows, ('batch', 'tensor'), 0, 0, axis_index_groups=side_gr...  9.42 us
    all_to_all x1, blocking collectives, on_device(): both = lax.all_to_all(both, 'tensor', 0, 0, tiled=True)  9.22 us

profile of v13, /device:TPU:1, one launch (start us, length us, event | category | flops | bytes accessed | tf_op | source)
XLA Modules:
  0.0 116.4 jit_solution(244129014906585065)
XLA Ops:
  0.0 0.0 copy-start
  0.0 0.0 copy-start.1
  0.0 0.7 broadcast_subtract_fusion
  0.7 0.2 copy-done
  1.0 0.5 fusion.2.part_ref
  1.5 11.1 %all_to_all.30.shares_ref = bf16[8,64,128]{2,1,0:T(8,128)(2,1)S(1)} all-to-all(bf16[8,64,128]{2,1,0:T(8,128)(2,1)S(1)} %shard_map.46), channel_id=1, replica_groups=mesh['batch'=64,'tensor'=8] {'tensor'}, dimensions={0} | all-to-all | bytes 262144 | tf_op jit(solution)/shard_map/all_to_all | solution.py:195
  12.6 0.0 copy-done.1
  12.6 0.0 copy-start.2
  12.6 0.1 shard_map.47
  12.7 34.6 %all_to_all.31 = bf16[8,192,128]{2,1,0:T(8,128)(2,1)S(1)} all-to-all(bf16[8,192,128]{2,1,0:T(8,128)(2,1)S(1)} %shard_map.47), channel_id=1, replica_groups={{0,32,64,96,128,160,192,224},{8,40,72,104,136,168,200,232},{16,48,80,11..., dimensions={0} | all-to-all | bytes 786432 | tf_op jit(solution)/shard_map/all_to_all | solution.py:196
  47.3 9.2 %all_to_all.32.both_ref = bf16[8,192,128]{2,1,0:T(8,128)(2,1)S(1)} all-to-all(bf16[8,192,128]{2,1,0:T(8,128)(2,1)S(1)} %all_to_all.31), channel_id=1, replica_groups=mesh['batch'=64,'tensor'=8] {'tensor'}, dimensions={0} | all-to-all | bytes 786432 | tf_op jit(solution)/shard_map/all_to_all | solution.py:199
  56.5 0.0 copy-done.2
  56.5 0.6 shard_map.48
  57.1 32.0 %all_to_all.33.terms_ref = bf16[64,16,512]{2,1,0:T(8,128)(2,1)S(1)} all-to-all(bf16[64,16,512]{2,1,0:T(8,128)(2,1)S(1)} %get-tuple-element.7), channel_id=1, replica_groups={{0,1,2,3,4,5,6,7,8,9,10,11,12,13,14,15,256,257,258,259,260,261,262,263,..., dimensions={0} | all-to-all | bytes 2097152 | tf_op jit(solution)/shard_map/all_to_all | solution.py:201
  89.1 0.6 shard_map.49
  89.7 16.5 %all_to_all.34.rows_ref = f32[32,1,128]{2,1,0:T(1,128)S(1)} all-to-all(f32[32,1,128]{2,1,0:T(1,128)S(1)} %bitcast.6), channel_id=1, replica_groups={{0,8,16,24,32,40,48,56,64,72,80,88,96,104,112,120,128,136,144,152,160,1..., dimensions={0} | all-to-all | bytes 32768 | tf_op jit(solution)/shard_map/all_to_all | solution.py:205
  106.2 0.1 shard_map.50
  106.3 9.4 %all_to_all.35.rows_ref = f32[16,1,64]{2,1,0:T(1,128)S(1)} all-to-all(f32[16,1,64]{2,1,0:T(1,128)S(1)} %bitcast.7), channel_id=1, replica_groups={{0,1,2,3,4,5,6,7,256,257,258,259,260,261,262,263},{8,9,10,11,12,13,14,1..., dimensions={0} | all-to-all | bytes 8192 | tf_op jit(solution)/shard_map/all_to_all | solution.py:208
  115.8 0.7 shard_map.51
  (1 shorter events, 0.0 us)
Async XLA Ops:
  0.0 1.0 copy-start
  0.0 12.6 %copy-start.1 = (bf16[128,1024]{1,0:T(8,128)(2,1)S(1)}, bf16[128,1024]{1,0:T(8,128)(2,1)}, u32[]{:S(2)}) copy-start(bf16[128,1024]{1,0:T(8,128)(2,1)} %acts_ref.1) | copy-start | bytes 786436
  12.6 43.9 %copy-start.2 = (s32[64]{0:T(128)S(1)}, s32[64]{0:T(128)}, u32[]{:S(2)}) copy-start(s32[64]{0:T(128)} %param.7) | copy-start | bytes 772

commit v14 on v13

--- a/solution.py
+++ b/solution.py
@@ -23,19 +23,32 @@
 PIECE = BLOCKS * TROWS
 MEMBERS = PLACES * SIDES * TENSOR
 ROWS = WIDTH // MEMBERS
+PAIR_OF = (
+    (4, 1, 2, 7, 0, 5, 6, 3),
+    (3, 7, 1, 5, 2, 6, 0, 4),
+    (5, 0, 3, 6, 1, 4, 7, 2),
+    (2, 6, 4, 1, 7, 3, 5, 0),
+    (6, 2, 5, 0, 3, 7, 4, 1),
+    (1, 4, 7, 2, 5, 0, 3, 6),
+    (7, 3, 0, 4, 6, 2, 1, 5),
+    (0, 5, 6, 3, 4, 1, 2, 7),
+)
 
 
 def batch_index(y_hi, pair, place, core):
     return ((y_hi * PAIRS + pair) * PLACES + place) * CORES + core
 
 
-def column_groups():
-    return [
-        [batch_index(y, k, r, c) for k in range(PAIRS)]
+def to_pair(block):
+    route = [
+        (batch_index(y, k, r, c) * TENSOR + t, batch_index(y, PAIR_OF[t][k], r, c) * TENSOR + t)
         for y in range(Y_HI)
+        for k in range(PAIRS)
         for r in range(PLACES)
         for c in range(CORES)
-    ]
+        for t in range(TENSOR)
+    ]
+    return lax.ppermute(block, ("batch", "tensor"), route)
 
 
 def pair_groups():
@@ -67,54 +80,69 @@
     ]
 
 
-def kernel_call(kernel, out_shape, args):
+def kernel_call(kernel, out_shape, args, scalars=()):
+    smem = pl.BlockSpec(memory_space=pltpu.SMEM)
     vmem = pl.BlockSpec(memory_space=pltpu.VMEM)
     return pl.pallas_call(
         kernel,
         out_shape=out_shape,
-        in_specs=[vmem] * len(args),
+        in_specs=[smem] * len(scalars) + [vmem] * len(args),
         out_specs=jax.tree.map(lambda _: vmem, out_shape),
         compiler_params=pltpu.CompilerParams(vmem_limit_bytes=24 * 1024 * 1024),
-    )(*args)
-
-
-def arrange_kernel(part_ref, out_ref):
-    for y in range(Y_LO):
-        for j in range(BLOCKS):
-            lane = (y * BLOCKS + j) * LANES
-            block = part_ref[:, lane : lane + LANES].reshape(X, TROWS, LANES)
-            out_ref[y * X : (y + 1) * X, j * TROWS : (j + 1) * TROWS] = block
+    )(*scalars, *args)
+
+
+def chosen_by(number, values):
+    found = values[0]
+    for i in range(1, len(values)):
+        found = jnp.where(number == i, values[i], found)
+    return found
 
 
 def selected(chosen, grads):
     local = chosen - lax.axis_index("tensor") * WIDTH
     places = lax.broadcasted_iota(jnp.int32, (WIDTH, NSEL), 0)
     selector = (places == local[None, :]).astype(grads.dtype)
-    part = lax.dot_general(
+    return lax.dot_general(
         grads, selector, (((1,), (0,)), ((), ())), preferred_element_type=jnp.float32
     ).astype(grads.dtype)
-    shape = jax.ShapeDtypeStruct((TENSOR, PIECE, LANES), grads.dtype)
-    return kernel_call(arrange_kernel, shape, (part,))
-
-
-def pack_kernel(acts_ref, shares_ref, out_ref):
-    piece = shares_ref[0].astype(jnp.float32)
+
+
+def pack_kernel(pair_ref, acts_ref, part_ref, out_ref):
+    for t in range(TENSOR):
+        start = pl.multiple_of(chosen_by(pair_ref[0], PAIR_OF[t]) * PART, PART)
+        out_ref[t, :TOK] = acts_ref[:, pl.ds(start, PART)]
+        y, x = t // X, t % X
+        for j in range(BLOCKS):
+            lane = (y * BLOCKS + j) * LANES
+            block = part_ref[x * TROWS : (x + 1) * TROWS, lane : lane + LANES]
+            out_ref[t, TOK + j * TROWS : TOK + (j + 1) * TROWS] = block
+
+
+def packed(pair, acts, part):
+    shape = jax.ShapeDtypeStruct((TENSOR, TOK + PIECE, LANES), acts.dtype)
+    return kernel_call(pack_kernel, shape, (acts, part), (pair,))
+
+
+def split_kernel(both_ref, acts_ref, copies_ref):
+    acts_ref[...] = both_ref[:, :TOK]
+    piece = both_ref[0, TOK:].astype(jnp.float32)
     for t in range(1, TENSOR):
-        piece = piece + shares_ref[t].astype(jnp.float32)
-    piece = piece.astype(out_ref.dtype)
-    for k in range(PAIRS):
-        out_ref[k, :TOK] = acts_ref[:, k * PART : (k + 1) * PART]
-        out_ref[k, TOK:] = piece
-
-
-def packed(acts, shares):
-    shape = jax.ShapeDtypeStruct((PAIRS, TOK + PIECE, LANES), acts.dtype)
-    return kernel_call(pack_kernel, shape, (acts, shares))
-
-
-def example_grad_kernel(both_ref, assign_ref, out_ref, spots_ref):
+        piece = piece + both_ref[t, TOK:].astype(jnp.float32)
+    copies_ref[...] = jnp.broadcast_to(piece.astype(copies_ref.dtype)[None], copies_ref.shape)
+
+
+def split(both):
+    shapes = (
+        jax.ShapeDtypeStruct((TENSOR, TOK, PART), both.dtype),
+        jax.ShapeDtypeStruct((TENSOR, PIECE, LANES), both.dtype),
+    )
+    return kernel_call(split_kernel, shapes, (both,))
+
+
+def example_grad_kernel(acts_ref, picked_ref, assign_ref, out_ref, spots_ref):
     blocks = [
-        both_ref[y * X : (y + 1) * X, TOK + j * TROWS : TOK + (j + 1) * TROWS].reshape(TOK, LANES)
+        picked_ref[y * X : (y + 1) * X, j * TROWS : (j + 1) * TROWS].reshape(TOK, LANES)
         for y in range(Y_LO)
         for j in range(BLOCKS)
     ]
@@ -125,7 +153,7 @@
     count = PART // ROWS
     for t in range(TENSOR):
         grad = lax.dot_general(
-            both_ref[t, :TOK], picked, (((0,), (0,)), ((), ())), preferred_element_type=jnp.float32
+            acts_ref[t], picked, (((0,), (0,)), ((), ())), preferred_element_type=jnp.float32
         )
         noise = jnp.bitwise_and(spread + t * 7919, 65535) * 128
         grad = pltpu.stochastic_round(grad, noise.astype(jnp.uint32), target_dtype=out_ref.dtype)
@@ -141,21 +169,36 @@
     )
 
 
-def example_grad(both, assign):
+def example_grad(acts, picked, assign):
     shapes = (
-        jax.ShapeDtypeStruct((MEMBERS, ROWS, NSEL), both.dtype),
+        jax.ShapeDtypeStruct((MEMBERS, ROWS, NSEL), acts.dtype),
         jax.ShapeDtypeStruct((SEQS, SEQS), jnp.float32),
     )
-    return kernel_call(example_grad_kernel, shapes, (both, assign[None]))
-
-
-def pairs_kernel(terms_ref, out_ref):
+    return kernel_call(example_grad_kernel, shapes, (acts, picked, assign[None]))
+
+
+def pairs_kernel(pair_ref, terms_ref, out_ref):
     terms = jnp.swapaxes(terms_ref[...], 0, 1)
     total = jnp.zeros((SEQS, SEQS), jnp.float32)
     for row in range(ROWS):
         total += lax.dot_general(
             terms[row], terms[row], (((1,), (1,)), ((), ())), preferred_element_type=jnp.float32
         )
+    total = total * (1.0 / (float(TOK) * float(D) * float(NSEL)))
+    row = lax.broadcasted_iota(jnp.int32, (SEQS, SEQS), 0)
+    column = lax.broadcasted_iota(jnp.int32, (SEQS, SEQS), 1)
+    held = [chosen_by(pair_ref[0], [PAIR_OF[t].index(k) for k in range(PAIRS)]) for t in range(TENSOR)]
+    from_pair = chosen_by(column % TENSOR, held)
+    turn = (row // PAIRS == column // TENSOR) & (row % PAIRS == from_pair)
+    turn = jnp.where(turn, 1.0, 0.0)
+    for side in range(2):
+        total = lax.dot_general(
+            turn,
+            total,
+            (((1,), (1,)), ((), ())),
+            precision=lax.Precision.HIGHEST,
+            preferred_element_type=jnp.float32,
+        )
     for r in range(PLACES):
         for c in range(CORES):
             starts = [((r * Y_HI + y) * CORES + c) * PAIRS for y in range(Y_HI)]
@@ -163,9 +206,9 @@
             out_ref[:, r, c, 0] = jnp.concatenate(rows, axis=1)
 
 
-def pairs(terms):
+def pairs(pair, terms):
     shape = jax.ShapeDtypeStruct((PAIRS, PLACES, CORES, 1, Y_HI * SEQS), jnp.float32)
-    return kernel_call(pairs_kernel, shape, (terms,))
+    return kernel_call(pairs_kernel, shape, (terms,), (pair,))
 
 
 def side_kernel(rows_ref, out_ref):
@@ -180,9 +223,8 @@
     row = rows_ref[0]
     for member in range(1, Y_HI * TENSOR):
         row = row + rows_ref[member]
-    norming = 1.0 / (float(TOK) * float(D) * float(NSEL))
     out_ref[...] = lax.dot_general(
-        row * norming,
+        row,
         spots_ref[...],
         (((1,), (0,)), ((), ())),
         precision=lax.Precision.HIGHEST,
@@ -191,17 +233,17 @@
 
 
 def on_device(acts, grads, chosen, assign):
-    part = selected(chosen, grads)
-    shares = lax.all_to_all(part, "tensor", 0, 0, tiled=True)
-    both = lax.all_to_all(
-        packed(acts, shares), "batch", 0, 0, axis_index_groups=column_groups(), tiled=True
-    )
+    pair = (lax.axis_index("batch") // (PLACES * CORES) % PAIRS)[None]
+    both = packed(pair, acts, selected(chosen, grads))
     both = lax.all_to_all(both, "tensor", 0, 0, tiled=True)
-    terms, spots = example_grad(both, assign)
+    part, copies = split(both)
+    part = to_pair(part)
+    picked = to_pair(lax.all_to_all(copies, "tensor", 0, 0, tiled=True))
+    terms, spots = example_grad(part, picked, assign)
     terms = lax.all_to_all(
         terms, ("batch", "tensor"), 0, 0, axis_index_groups=pair_groups(), tiled=True
     )
-    rows = pairs(terms).reshape(DEPTH, 1, Y_HI * SEQS)
+    rows = pairs(pair, terms).reshape(DEPTH, 1, Y_HI * SEQS)
     rows = lax.all_to_all(rows, "batch", 0, 0, axis_index_groups=depth_groups(), tiled=True)
     shape = jax.ShapeDtypeStruct((Y_HI, TENSOR, 1, SEQS), jnp.float32)
     rows = kernel_call(side_kernel, shape, (rows,)).reshape(Y_HI * TENSOR, 1, SEQS)

time: 117 us -> 110 us (0.940)
  blocking collectives: 113 us -> 74.1 us
  starting transfers between devices: 0 us -> 20.6 us
  waiting for transfers between devices: 0 us -> 11 us
    all_to_all x2 -> x1, blocking collectives: 45.7 us -> 7.83 us  [on_device(): picked = to_pair(lax.all_to_all(copies, 'tensor', 0, 0, tiled=True))]
    ppermute x0 -> x2, starting transfers between devices: none -> 20.6 us  [to_pair(): return lax.ppermute(block, ('batch', 'tensor'), route)]
    ppermute x0 -> x2, waiting for transfers between devices: none -> 11 us  [to_pair(): return lax.ppermute(block, ('batch', 'tensor'), route)]
    all_to_all x1, blocking collectives: 32 us -> 27.3 us  [on_device(): lax.all_to_all(terms, ('batch', 'tensor'), 0, 0, axis_index_groups=pair_g...]
    all_to_all x1, blocking collectives: 9.22 us -> 12.5 us  [on_device(): both = lax.all_to_all(both, 'tensor', 0, 0, tiled=True)]
  transfers between devices with their start and end apart: 0 -> 2, of which waited for: 0 -> 1; matrix products, arithmetic and copies ran while one was open for 0% -> 0% of each run, Pallas kernels for 0% -> 0%
where the time goes in v14:
time: 110 us
  blocking collectives  74.1 us (67%)
  starting transfers between devices  20.6 us (19%)
  waiting for transfers between devices  11 us (10%)
  Pallas kernels  2.58 us (2%)
    all_to_all x1, blocking collectives, on_device(): lax.all_to_all(terms, ('batch', 'tensor'), 0, 0, axis_index_groups=pair_g...  27.3 us
    ppermute x2, starting transfers between devices, to_pair(): return lax.ppermute(block, ('batch', 'tensor'), route)  20.6 us
    all_to_all x1, blocking collectives, on_device(): lax.all_to_all(rows, 'batch', 0, 0, axis_index_groups=depth_groups(), til...  17 us
    all_to_all x1, blocking collectives, on_device(): both = lax.all_to_all(both, 'tensor', 0, 0, tiled=True)  12.5 us
    ppermute x2, waiting for transfers between devices, to_pair(): return lax.ppermute(block, ('batch', 'tensor'), route)  11 us
    all_to_all x1, blocking collectives, on_device(): lax.all_to_all(rows, ('batch', 'tensor'), 0, 0, axis_index_groups=side_gr...  9.42 us
    all_to_all x1, blocking collectives, on_device(): picked = to_pair(lax.all_to_all(copies, 'tensor', 0, 0, tiled=True))  7.83 us
    pallas_call x6, Pallas kernels, kernel_call(): pl.pallas_call(kernel, out_shape=out_shape, in_specs=[smem] * len(scalars...  2.58 us
  transfers between devices with their start and end apart: 2, of which 1 were waited for; matrix products, arithmetic and copies ran while one was open for 0% of the time, Pallas kernels for 0%

profile of v14, /device:TPU:1, one launch (start us, length us, event | category | flops | bytes accessed | tf_op | source)
XLA Modules:
  0.0 109.8 jit_solution(16835019100467796549)
XLA Ops:
  0.0 0.0 copy-start
  0.0 0.0 copy-start.1
  0.0 0.7 broadcast_subtract_fusion
  0.7 0.2 copy-done
  1.0 0.5 fusion.2.part_ref
  1.5 0.0 copy-done.1
  1.5 0.0 copy-start.2
  1.5 0.1 shard_map.46
  1.6 12.5 %all_to_all.25.both_ref = bf16[8,192,128]{2,1,0:T(8,128)(2,1)S(1)} all-to-all(bf16[8,192,128]{2,1,0:T(8,128)(2,1)S(1)} %shard_map.46), channel_id=1, replica_groups=mesh['batch'=64,'tensor'=8] {'tensor'}, dimensions={0} | all-to-all | bytes 786432 | tf_op jit(solution)/shard_map/all_to_all | solution.py:238
  14.1 16.6 %collective-permute-start = (bf16[8,128,128]{2,1,0:T(8,128)(2,1)S(1)}, bf16[8,128,128]{2,1,0:T(8,128)(2,1)S(1)}, u32[]{:S(2)}, u32[]{:S(2)}) collective-permute-start(bf16[8,128,128]{2,1,0:T(8,128)(2,1)S(1)} %get-tuple-element.9), channel_id=1, source_target_pairs={{0,128},{1,97},{2,162},{3,67},{4,196},{5,37},{6,230},{7,7},{8,136}... | collective-permute-start | bytes 786440 | tf_op jit(solution)/shard_map/ppermute | solution.py:51
  30.8 7.8 %all_to_all.26 = bf16[8,64,128]{2,1,0:T(8,128)(2,1)S(1)} all-to-all(bf16[8,64,128]{2,1,0:T(8,128)(2,1)S(1)} %get-tuple-element.10), channel_id=1, replica_groups=mesh['batch'=64,'tensor'=8] {'tensor'}, dimensions={0} | all-to-all | bytes 262144 | tf_op jit(solution)/shard_map/all_to_all | solution.py:241
  38.6 3.9 %collective-permute-start.1 = (bf16[8,64,128]{2,1,0:T(8,128)(2,1)S(1)}, bf16[8,64,128]{2,1,0:T(8,128)(2,1)S(1)}, u32[]{:S(2)}, u32[]{:S(2)}) collective-permute-start(bf16[8,64,128]{2,1,0:T(8,128)(2,1)S(1)} %all_to_all.26), channel_id=1, source_target_pairs={{0,128},{1,97},{2,162},{3,67},{4,196},{5,37},{6,230},{7,7},{8,136}... | collective-permute-start | bytes 393224 | tf_op jit(solution)/shard_map/ppermute | solution.py:51
  42.6 11.0 %collective-permute-done.1.picked_ref = bf16[8,64,128]{2,1,0:T(8,128)(2,1)S(1)} collective-permute-done((bf16[8,64,128]{2,1,0:T(8,128)(2,1)S(1)}, bf16[8,64,128]{2,1,0:T(8,128)(2,1)S(1)}, u32[]{:S(2)}, u32[]{:S(2)}) %collective-permute-start.1) | collective-permute-done | bytes 131104 | tf_op jit(solution)/shard_map/ppermute | solution.py:51
  53.6 0.0 collective-permute-done.acts_ref
  53.6 0.0 copy-done.2
  53.6 0.6 shard_map.48
  54.2 27.3 %all_to_all.27.terms_ref = bf16[64,16,512]{2,1,0:T(8,128)(2,1)S(1)} all-to-all(bf16[64,16,512]{2,1,0:T(8,128)(2,1)S(1)} %get-tuple-element.11), channel_id=1, replica_groups={{0,1,2,3,4,5,6,7,8,9,10,11,12,13,14,15,256,257,258,259,260,261,262,263,..., dimensions={0} | all-to-all | bytes 2097152 | tf_op jit(solution)/shard_map/all_to_all | solution.py:243
  81.5 1.1 %shard_map.49 = f32[8,2,2,1,128]{4,3,2,1,0:T(1,128)S(1)} custom-call(s32[1]{0:T(128)} %bitcast.pair_ref, bf16[64,16,512]{2,1,0:T(8,128)(2,1)S(1)} %all_to_all.27.terms_ref), custom_call_target="tpu_custom_call" | custom-call | tf_op jit(solution)/shard_map/pallas_call | solution.py:86
  82.6 17.0 %all_to_all.28.rows_ref = f32[32,1,128]{2,1,0:T(1,128)S(1)} all-to-all(f32[32,1,128]{2,1,0:T(1,128)S(1)} %bitcast.7), channel_id=1, replica_groups={{0,8,16,24,32,40,48,56,64,72,80,88,96,104,112,120,128,136,144,152,160,1..., dimensions={0} | all-to-all | bytes 32768 | tf_op jit(solution)/shard_map/all_to_all | solution.py:247
  99.6 0.1 shard_map.50
  99.7 9.4 %all_to_all.29.rows_ref = f32[16,1,64]{2,1,0:T(1,128)S(1)} all-to-all(f32[16,1,64]{2,1,0:T(1,128)S(1)} %bitcast.8), channel_id=1, replica_groups={{0,1,2,3,4,5,6,7,256,257,258,259,260,261,262,263},{8,9,10,11,12,13,14,1..., dimensions={0} | all-to-all | bytes 8192 | tf_op jit(solution)/shard_map/all_to_all | solution.py:250
  109.1 0.7 shard_map.51
  (1 shorter events, 0.0 us)
Async XLA Ops:
  0.0 1.0 copy-start
  0.0 1.5 %copy-start.1 = (bf16[128,1024]{1,0:T(8,128)(2,1)S(1)}, bf16[128,1024]{1,0:T(8,128)(2,1)}, u32[]{:S(2)}) copy-start(bf16[128,1024]{1,0:T(8,128)(2,1)} %acts_ref.1) | copy-start | bytes 786436
  1.5 52.1 %copy-start.2 = (s32[64]{0:T(128)S(1)}, s32[64]{0:T(128)}, u32[]{:S(2)}) copy-start(s32[64]{0:T(128)} %param.7) | copy-start | bytes 772
  14.1 39.5 %collective-permute-start = (bf16[8,128,128]{2,1,0:T(8,128)(2,1)S(1)}, bf16[8,128,128]{2,1,0:T(8,128)(2,1)S(1)}, u32[]{:S(2)}, u32[]{:S(2)}) collective-permute-start(bf16[8,128,128]{2,1,0:T(8,128)(2,1)S(1)} %get-tuple-element.9), channel_id=1, source_target_pairs={{0,128},{1,97},{2,162},{3,67},{4,196},{5,37},{6,230},{7,7},{8,136}... | collective-permute-start | bytes 786440 | tf_op jit(solution)/shard_map/ppermute | solution.py:51
  38.6 15.0 %collective-permute-start.1 = (bf16[8,64,128]{2,1,0:T(8,128)(2,1)S(1)}, bf16[8,64,128]{2,1,0:T(8,128)(2,1)S(1)}, u32[]{:S(2)}, u32[]{:S(2)}) collective-permute-start(bf16[8,64,128]{2,1,0:T(8,128)(2,1)S(1)} %all_to_all.26), channel_id=1, source_target_pairs={{0,128},{1,97},{2,162},{3,67},{4,196},{5,37},{6,230},{7,7},{8,136}... | collective-permute-start | bytes 393224 | tf_op jit(solution)/shard_map/ppermute | solution.py:51

commit v15 on v14

--- a/solution.py
+++ b/solution.py
@@ -185,25 +185,24 @@
             terms[row], terms[row], (((1,), (1,)), ((), ())), preferred_element_type=jnp.float32
         )
     total = total * (1.0 / (float(TOK) * float(D) * float(NSEL)))
+    held = [chosen_by(pair_ref[0], [PAIR_OF[t].index(k) for k in range(PAIRS)]) for t in range(TENSOR)]
     row = lax.broadcasted_iota(jnp.int32, (SEQS, SEQS), 0)
     column = lax.broadcasted_iota(jnp.int32, (SEQS, SEQS), 1)
-    held = [chosen_by(pair_ref[0], [PAIR_OF[t].index(k) for k in range(PAIRS)]) for t in range(TENSOR)]
-    from_pair = chosen_by(column % TENSOR, held)
-    turn = (row // PAIRS == column // TENSOR) & (row % PAIRS == from_pair)
-    turn = jnp.where(turn, 1.0, 0.0)
-    for side in range(2):
-        total = lax.dot_general(
-            turn,
-            total,
-            (((1,), (1,)), ((), ())),
-            precision=lax.Precision.HIGHEST,
-            preferred_element_type=jnp.float32,
-        )
+    tensor = jnp.bitwise_and(lax.broadcasted_iota(jnp.int32, (1, SEQS), 1), TENSOR - 1)
+    source = jnp.bitwise_and(column, ~(TENSOR - 1)) + chosen_by(tensor, held)
+    total = lax.dot_general(
+        total,
+        jnp.where(row == source, 1.0, 0.0),
+        (((1,), (1,)), ((), ())),
+        precision=lax.Precision.HIGHEST,
+        preferred_element_type=jnp.float32,
+    )
     for r in range(PLACES):
         for c in range(CORES):
-            starts = [((r * Y_HI + y) * CORES + c) * PAIRS for y in range(Y_HI)]
-            rows = [total[start : start + PAIRS] for start in starts]
-            out_ref[:, r, c, 0] = jnp.concatenate(rows, axis=1)
+            starts = [((r * Y_HI + y) * CORES + c) * TENSOR for y in range(Y_HI)]
+            rows = jnp.concatenate([total[start : start + TENSOR] for start in starts], axis=1)
+            for t in range(TENSOR):
+                out_ref[pl.ds(held[t], 1), r, c] = rows[t : t + 1][None]
 
 
 def pairs(pair, terms):

time: 110 us -> 110 us (level)
  no operation moved by 1% of the time
where the time goes in v15:
time: 110 us
  blocking collectives  74.1 us (67%)
  starting transfers between devices  20.6 us (19%)
  waiting for transfers between devices  11 us (10%)
  Pallas kernels  2.36 us (2%)
    all_to_all x1, blocking collectives, on_device(): lax.all_to_all(terms, ('batch', 'tensor'), 0, 0, axis_index_groups=pair_g...  27.3 us
    ppermute x2, starting transfers between devices, to_pair(): return lax.ppermute(block, ('batch', 'tensor'), route)  20.6 us
    all_to_all x1, blocking collectives, on_device(): lax.all_to_all(rows, 'batch', 0, 0, axis_index_groups=depth_groups(), til...  17 us
    all_to_all x1, blocking collectives, on_device(): both = lax.all_to_all(both, 'tensor', 0, 0, tiled=True)  12.5 us
    ppermute x2, waiting for transfers between devices, to_pair(): return lax.ppermute(block, ('batch', 'tensor'), route)  11 us
    all_to_all x1, blocking collectives, on_device(): lax.all_to_all(rows, ('batch', 'tensor'), 0, 0, axis_index_groups=side_gr...  9.42 us
    all_to_all x1, blocking collectives, on_device(): picked = to_pair(lax.all_to_all(copies, 'tensor', 0, 0, tiled=True))  7.83 us
    pallas_call x6, Pallas kernels, kernel_call(): pl.pallas_call(kernel, out_shape=out_shape, in_specs=[smem] * len(scalars...  2.36 us
  transfers between devices with their start and end apart: 2, of which 1 were waited for; matrix products, arithmetic and copies ran while one was open for 0% of the time, Pallas kernels for 0%

profile of v15, /device:TPU:1, one launch (start us, length us, event | category | flops | bytes accessed | tf_op | source)
XLA Modules:
  0.0 109.6 jit_solution(4261324873171445627)
XLA Ops:
  0.0 0.0 copy-start
  0.0 0.0 copy-start.1
  0.0 0.7 broadcast_subtract_fusion
  0.7 0.2 copy-done
  1.0 0.5 fusion.2.part_ref
  1.5 0.0 copy-done.1
  1.5 0.0 copy-start.2
  1.5 0.1 shard_map.46
  1.6 12.5 %all_to_all.25.both_ref = bf16[8,192,128]{2,1,0:T(8,128)(2,1)S(1)} all-to-all(bf16[8,192,128]{2,1,0:T(8,128)(2,1)S(1)} %shard_map.46), channel_id=1, replica_groups=mesh['batch'=64,'tensor'=8] {'tensor'}, dimensions={0} | all-to-all | bytes 786432 | tf_op jit(solution)/shard_map/all_to_all | solution.py:237
  14.1 16.6 %collective-permute-start = (bf16[8,128,128]{2,1,0:T(8,128)(2,1)S(1)}, bf16[8,128,128]{2,1,0:T(8,128)(2,1)S(1)}, u32[]{:S(2)}, u32[]{:S(2)}) collective-permute-start(bf16[8,128,128]{2,1,0:T(8,128)(2,1)S(1)} %get-tuple-element.9), channel_id=1, source_target_pairs={{0,128},{1,97},{2,162},{3,67},{4,196},{5,37},{6,230},{7,7},{8,136}... | collective-permute-start | bytes 786440 | tf_op jit(solution)/shard_map/ppermute | solution.py:51
  30.8 7.8 %all_to_all.26 = bf16[8,64,128]{2,1,0:T(8,128)(2,1)S(1)} all-to-all(bf16[8,64,128]{2,1,0:T(8,128)(2,1)S(1)} %get-tuple-element.10), channel_id=1, replica_groups=mesh['batch'=64,'tensor'=8] {'tensor'}, dimensions={0} | all-to-all | bytes 262144 | tf_op jit(solution)/shard_map/all_to_all | solution.py:240
  38.6 3.9 %collective-permute-start.1 = (bf16[8,64,128]{2,1,0:T(8,128)(2,1)S(1)}, bf16[8,64,128]{2,1,0:T(8,128)(2,1)S(1)}, u32[]{:S(2)}, u32[]{:S(2)}) collective-permute-start(bf16[8,64,128]{2,1,0:T(8,128)(2,1)S(1)} %all_to_all.26), channel_id=1, source_target_pairs={{0,128},{1,97},{2,162},{3,67},{4,196},{5,37},{6,230},{7,7},{8,136}... | collective-permute-start | bytes 393224 | tf_op jit(solution)/shard_map/ppermute | solution.py:51
  42.6 11.0 %collective-permute-done.1.picked_ref = bf16[8,64,128]{2,1,0:T(8,128)(2,1)S(1)} collective-permute-done((bf16[8,64,128]{2,1,0:T(8,128)(2,1)S(1)}, bf16[8,64,128]{2,1,0:T(8,128)(2,1)S(1)}, u32[]{:S(2)}, u32[]{:S(2)}) %collective-permute-start.1) | collective-permute-done | bytes 131104 | tf_op jit(solution)/shard_map/ppermute | solution.py:51
  53.6 0.0 collective-permute-done.acts_ref
  53.6 0.0 copy-done.2
  53.6 0.6 shard_map.48
  54.2 27.3 %all_to_all.27.terms_ref = bf16[64,16,512]{2,1,0:T(8,128)(2,1)S(1)} all-to-all(bf16[64,16,512]{2,1,0:T(8,128)(2,1)S(1)} %get-tuple-element.11), channel_id=1, replica_groups={{0,1,2,3,4,5,6,7,8,9,10,11,12,13,14,15,256,257,258,259,260,261,262,263,..., dimensions={0} | all-to-all | bytes 2097152 | tf_op jit(solution)/shard_map/all_to_all | solution.py:242
  81.5 0.9 shard_map.49
  82.4 17.0 %all_to_all.28.rows_ref = f32[32,1,128]{2,1,0:T(1,128)S(1)} all-to-all(f32[32,1,128]{2,1,0:T(1,128)S(1)} %bitcast.7), channel_id=1, replica_groups={{0,8,16,24,32,40,48,56,64,72,80,88,96,104,112,120,128,136,144,152,160,1..., dimensions={0} | all-to-all | bytes 32768 | tf_op jit(solution)/shard_map/all_to_all | solution.py:246
  99.4 0.1 shard_map.50
  99.5 9.4 %all_to_all.29.rows_ref = f32[16,1,64]{2,1,0:T(1,128)S(1)} all-to-all(f32[16,1,64]{2,1,0:T(1,128)S(1)} %bitcast.8), channel_id=1, replica_groups={{0,1,2,3,4,5,6,7,256,257,258,259,260,261,262,263},{8,9,10,11,12,13,14,1..., dimensions={0} | all-to-all | bytes 8192 | tf_op jit(solution)/shard_map/all_to_all | solution.py:249
  108.9 0.7 shard_map.51
  (1 shorter events, 0.0 us)
Async XLA Ops:
  0.0 1.0 copy-start
  0.0 1.5 %copy-start.1 = (bf16[128,1024]{1,0:T(8,128)(2,1)S(1)}, bf16[128,1024]{1,0:T(8,128)(2,1)}, u32[]{:S(2)}) copy-start(bf16[128,1024]{1,0:T(8,128)(2,1)} %acts_ref.1) | copy-start | bytes 786436
  1.5 52.1 %copy-start.2 = (s32[64]{0:T(128)S(1)}, s32[64]{0:T(128)}, u32[]{:S(2)}) copy-start(s32[64]{0:T(128)} %param.7) | copy-start | bytes 772
  14.1 39.5 %collective-permute-start = (bf16[8,128,128]{2,1,0:T(8,128)(2,1)S(1)}, bf16[8,128,128]{2,1,0:T(8,128)(2,1)S(1)}, u32[]{:S(2)}, u32[]{:S(2)}) collective-permute-start(bf16[8,128,128]{2,1,0:T(8,128)(2,1)S(1)} %get-tuple-element.9), channel_id=1, source_target_pairs={{0,128},{1,97},{2,162},{3,67},{4,196},{5,37},{6,230},{7,7},{8,136}... | collective-permute-start | bytes 786440 | tf_op jit(solution)/shard_map/ppermute | solution.py:51
  38.6 15.0 %collective-permute-start.1 = (bf16[8,64,128]{2,1,0:T(8,128)(2,1)S(1)}, bf16[8,64,128]{2,1,0:T(8,128)(2,1)S(1)}, u32[]{:S(2)}, u32[]{:S(2)}) collective-permute-start(bf16[8,64,128]{2,1,0:T(8,128)(2,1)S(1)} %all_to_all.26), channel_id=1, source_target_pairs={{0,128},{1,97},{2,162},{3,67},{4,196},{5,37},{6,230},{7,7},{8,136}... | collective-permute-start | bytes 393224 | tf_op jit(solution)/shard_map/ppermute | solution.py:51

commit v16 on v15

--- a/solution.py
+++ b/solution.py
@@ -236,8 +236,9 @@
     both = packed(pair, acts, selected(chosen, grads))
     both = lax.all_to_all(both, "tensor", 0, 0, tiled=True)
     part, copies = split(both)
-    part = to_pair(part)
-    picked = to_pair(lax.all_to_all(copies, "tensor", 0, 0, tiled=True))
+    picked = lax.all_to_all(copies, "tensor", 0, 0, tiled=True)
+    part, picked = lax.optimization_barrier((part, picked))
+    part, picked = to_pair(part), to_pair(picked)
     terms, spots = example_grad(part, picked, assign)
     terms = lax.all_to_all(
         terms, ("batch", "tensor"), 0, 0, axis_index_groups=pair_groups(), tiled=True

time: 110 us -> 116 us (1.055)
  blocking collectives: 74.1 us -> 80.2 us
  starting transfers between devices: 20.6 us -> 18.5 us
  waiting for transfers between devices: 11 us -> 12.6 us
    all_to_all x1, blocking collectives: 27.3 us -> 32.2 us  [on_device(): lax.all_to_all(terms, ('batch', 'tensor'), 0, 0, axis_index_groups=pair_g...]
    ppermute x2, starting transfers between devices: 20.6 us -> 18.5 us  [to_pair(): return lax.ppermute(block, ('batch', 'tensor'), route)]
    ppermute x2, waiting for transfers between devices: 11 us -> 12.6 us  [to_pair(): return lax.ppermute(block, ('batch', 'tensor'), route)]
    all_to_all x1, blocking collectives: 17 us -> 18.2 us  [on_device(): lax.all_to_all(rows, 'batch', 0, 0, axis_index_groups=depth_groups(), til...]
where the time goes in v16:
time: 116 us; the launch traced here: 115 us
  blocking collectives  80.2 us (69%)
  starting transfers between devices  18.5 us (16%)
  waiting for transfers between devices  12.6 us (11%)
  Pallas kernels  2.37 us (2%)
    all_to_all x1, blocking collectives, on_device(): lax.all_to_all(terms, ('batch', 'tensor'), 0, 0, axis_index_groups=pair_g...  32.2 us
    ppermute x2, starting transfers between devices, to_pair(): return lax.ppermute(block, ('batch', 'tensor'), route)  18.5 us
    all_to_all x1, blocking collectives, on_device(): lax.all_to_all(rows, 'batch', 0, 0, axis_index_groups=depth_groups(), til...  18.2 us
    ppermute x2, waiting for transfers between devices, to_pair(): return lax.ppermute(block, ('batch', 'tensor'), route)  12.6 us
    all_to_all x1, blocking collectives, on_device(): both = lax.all_to_all(both, 'tensor', 0, 0, tiled=True)  12.5 us
    all_to_all x1, blocking collectives, on_device(): lax.all_to_all(rows, ('batch', 'tensor'), 0, 0, axis_index_groups=side_gr...  9.42 us
    all_to_all x1, blocking collectives, on_device(): picked = lax.all_to_all(copies, 'tensor', 0, 0, tiled=True)  7.83 us
    pallas_call x6, Pallas kernels, kernel_call(): pl.pallas_call(kernel, out_shape=out_shape, in_specs=[smem] * len(scalars...  2.37 us
  transfers between devices with their start and end apart: 2, of which 1 were waited for; matrix products, arithmetic and copies ran while one was open for 0% of the time, Pallas kernels for 0%

profile of v16, /device:TPU:1, one launch (start us, length us, event | category | flops | bytes accessed | tf_op | source)
XLA Modules:
  0.0 115.3 jit_solution(2085749012415921683)
XLA Ops:
  0.0 0.0 copy-start
  0.0 0.0 copy-start.1
  0.0 0.7 broadcast_subtract_fusion
  0.7 0.2 copy-done
  1.0 0.5 fusion.2.part_ref
  1.5 0.0 copy-done.1
  1.5 0.0 copy-start.2
  1.5 0.1 shard_map.46
  1.6 12.5 %all_to_all.25.both_ref = bf16[8,192,128]{2,1,0:T(8,128)(2,1)S(1)} all-to-all(bf16[8,192,128]{2,1,0:T(8,128)(2,1)S(1)} %shard_map.46), channel_id=1, replica_groups=mesh['batch'=64,'tensor'=8] {'tensor'}, dimensions={0} | all-to-all | bytes 786432 | tf_op jit(solution)/shard_map/all_to_all | solution.py:237
  14.1 7.8 %all_to_all.26 = bf16[8,64,128]{2,1,0:T(8,128)(2,1)S(1)} all-to-all(bf16[8,64,128]{2,1,0:T(8,128)(2,1)S(1)} %get-tuple-element.12), channel_id=1, replica_groups=mesh['batch'=64,'tensor'=8] {'tensor'}, dimensions={0} | all-to-all | bytes 262144 | tf_op jit(solution)/shard_map/all_to_all | solution.py:239
  22.0 16.6 %collective-permute-start = (bf16[8,128,128]{2,1,0:T(8,128)(2,1)S(1)}, bf16[8,128,128]{2,1,0:T(8,128)(2,1)S(1)}, u32[]{:S(2)}, u32[]{:S(2)}) collective-permute-start(bf16[8,128,128]{2,1,0:T(8,128)(2,1)S(1)} %get-tuple-element.13), channel_id=1, source_target_pairs={{0,128},{1,97},{2,162},{3,67},{4,196},{5,37},{6,230},{7,7},{8,136}... | collective-permute-start | bytes 786440 | tf_op jit(solution)/shard_map/ppermute | solution.py:51
  38.6 1.9 %collective-permute-start.1 = (bf16[8,64,128]{2,1,0:T(8,128)(2,1)S(1)}, bf16[8,64,128]{2,1,0:T(8,128)(2,1)S(1)}, u32[]{:S(2)}, u32[]{:S(2)}) collective-permute-start(bf16[8,64,128]{2,1,0:T(8,128)(2,1)S(1)} %all_to_all.26), channel_id=1, source_target_pairs={{0,128},{1,97},{2,162},{3,67},{4,196},{5,37},{6,230},{7,7},{8,136}... | collective-permute-start | bytes 393224 | tf_op jit(solution)/shard_map/ppermute | solution.py:51
  40.5 12.6 %collective-permute-done.1.picked_ref = bf16[8,64,128]{2,1,0:T(8,128)(2,1)S(1)} collective-permute-done((bf16[8,64,128]{2,1,0:T(8,128)(2,1)S(1)}, bf16[8,64,128]{2,1,0:T(8,128)(2,1)S(1)}, u32[]{:S(2)}, u32[]{:S(2)}) %collective-permute-start.1) | collective-permute-done | bytes 131104 | tf_op jit(solution)/shard_map/ppermute | solution.py:51
  53.2 0.0 collective-permute-done.acts_ref
  53.2 0.0 copy-done.2
  53.2 0.6 shard_map.48
  53.8 32.2 %all_to_all.27.terms_ref = bf16[64,16,512]{2,1,0:T(8,128)(2,1)S(1)} all-to-all(bf16[64,16,512]{2,1,0:T(8,128)(2,1)S(1)} %get-tuple-element.15), channel_id=1, replica_groups={{0,1,2,3,4,5,6,7,8,9,10,11,12,13,14,15,256,257,258,259,260,261,262,263,..., dimensions={0} | all-to-all | bytes 2097152 | tf_op jit(solution)/shard_map/all_to_all | solution.py:243
  86.0 0.9 shard_map.49
  86.9 18.2 %all_to_all.28.rows_ref = f32[32,1,128]{2,1,0:T(1,128)S(1)} all-to-all(f32[32,1,128]{2,1,0:T(1,128)S(1)} %bitcast.7), channel_id=1, replica_groups={{0,8,16,24,32,40,48,56,64,72,80,88,96,104,112,120,128,136,144,152,160,1..., dimensions={0} | all-to-all | bytes 32768 | tf_op jit(solution)/shard_map/all_to_all | solution.py:247
  105.1 0.1 shard_map.50
  105.2 9.4 %all_to_all.29.rows_ref = f32[16,1,64]{2,1,0:T(1,128)S(1)} all-to-all(f32[16,1,64]{2,1,0:T(1,128)S(1)} %bitcast.8), channel_id=1, replica_groups={{0,1,2,3,4,5,6,7,256,257,258,259,260,261,262,263},{8,9,10,11,12,13,14,1..., dimensions={0} | all-to-all | bytes 8192 | tf_op jit(solution)/shard_map/all_to_all | solution.py:250
  114.6 0.7 shard_map.51
  (1 shorter events, 0.0 us)
Async XLA Ops:
  0.0 1.0 copy-start
  0.0 1.5 %copy-start.1 = (bf16[128,1024]{1,0:T(8,128)(2,1)S(1)}, bf16[128,1024]{1,0:T(8,128)(2,1)}, u32[]{:S(2)}) copy-start(bf16[128,1024]{1,0:T(8,128)(2,1)} %acts_ref.1) | copy-start | bytes 786436
  1.5 51.7 %copy-start.2 = (s32[64]{0:T(128)S(1)}, s32[64]{0:T(128)}, u32[]{:S(2)}) copy-start(s32[64]{0:T(128)} %param.7) | copy-start | bytes 772
  22.0 31.2 %collective-permute-start = (bf16[8,128,128]{2,1,0:T(8,128)(2,1)S(1)}, bf16[8,128,128]{2,1,0:T(8,128)(2,1)S(1)}, u32[]{:S(2)}, u32[]{:S(2)}) collective-permute-start(bf16[8,128,128]{2,1,0:T(8,128)(2,1)S(1)} %get-tuple-element.13), channel_id=1, source_target_pairs={{0,128},{1,97},{2,162},{3,67},{4,196},{5,37},{6,230},{7,7},{8,136}... | collective-permute-start | bytes 786440 | tf_op jit(solution)/shard_map/ppermute | solution.py:51
  38.6 14.6 %collective-permute-start.1 = (bf16[8,64,128]{2,1,0:T(8,128)(2,1)S(1)}, bf16[8,64,128]{2,1,0:T(8,128)(2,1)S(1)}, u32[]{:S(2)}, u32[]{:S(2)}) collective-permute-start(bf16[8,64,128]{2,1,0:T(8,128)(2,1)S(1)} %all_to_all.26), channel_id=1, source_target_pairs={{0,128},{1,97},{2,162},{3,67},{4,196},{5,37},{6,230},{7,7},{8,136}... | collective-permute-start | bytes 393224 | tf_op jit(solution)/shard_map/ppermute | solution.py:51

commit v17 on v15

--- a/solution.py
+++ b/solution.py
@@ -21,6 +21,7 @@
 LANES = 128
 BLOCKS = HALF // LANES
 PIECE = BLOCKS * TROWS
+REPEATS = 2
 MEMBERS = PLACES * SIDES * TENSOR
 ROWS = WIDTH // MEMBERS
 PAIR_OF = (
@@ -129,13 +130,16 @@
     piece = both_ref[0, TOK:].astype(jnp.float32)
     for t in range(1, TENSOR):
         piece = piece + both_ref[t, TOK:].astype(jnp.float32)
-    copies_ref[...] = jnp.broadcast_to(piece.astype(copies_ref.dtype)[None], copies_ref.shape)
+    piece = piece.astype(copies_ref.dtype)
+    for t in range(TENSOR):
+        for i in range(REPEATS):
+            copies_ref[t, i * PIECE : (i + 1) * PIECE] = piece
 
 
 def split(both):
     shapes = (
         jax.ShapeDtypeStruct((TENSOR, TOK, PART), both.dtype),
-        jax.ShapeDtypeStruct((TENSOR, PIECE, LANES), both.dtype),
+        jax.ShapeDtypeStruct((TENSOR, REPEATS * PIECE, LANES), both.dtype),
     )
     return kernel_call(split_kernel, shapes, (both,))
 
@@ -237,7 +241,7 @@
     both = lax.all_to_all(both, "tensor", 0, 0, tiled=True)
     part, copies = split(both)
     part = to_pair(part)
-    picked = to_pair(lax.all_to_all(copies, "tensor", 0, 0, tiled=True))
+    picked = to_pair(lax.all_to_all(copies, "tensor", 0, 0, tiled=True)[:, :PIECE])
     terms, spots = example_grad(part, picked, assign)
     terms = lax.all_to_all(
         terms, ("batch", "tensor"), 0, 0, axis_index_groups=pair_groups(), tiled=True

time: 110 us -> 113 us (1.027)
  starting transfers between devices: 20.6 us -> 26.3 us
  blocking collectives: 74.1 us -> 72.1 us
    all_to_all x1 -> x0, blocking collectives: 7.83 us -> none  [on_device(): picked = to_pair(lax.all_to_all(copies, 'tensor', 0, 0, tiled=True))]
    all_to_all x1, blocking collectives: 17 us -> 21.1 us  [on_device(): lax.all_to_all(rows, 'batch', 0, 0, axis_index_groups=depth_groups(), til...]
    all_to_all x0 -> x1, starting transfers between devices: none -> 3.41 us  [on_device(): lax.all_to_all(copies, 'tensor', 0, 0, tiled=True)[:, :PIECE]]
    ppermute x2, starting transfers between devices: 20.6 us -> 22.9 us  [to_pair(): return lax.ppermute(block, ('batch', 'tensor'), route)]
    all_to_all x1, blocking collectives: 27.3 us -> 29.1 us  [on_device(): lax.all_to_all(terms, ('batch', 'tensor'), 0, 0, axis_index_groups=pair_g...]
    ppermute x2, waiting for transfers between devices: 11 us -> 9.89 us  [to_pair(): return lax.ppermute(block, ('batch', 'tensor'), route)]
  transfers between devices with their start and end apart: 2 -> 3, of which waited for: 1 -> 1; matrix products, arithmetic and copies ran while one was open for 0% -> 0% of each run, Pallas kernels for 0% -> 0%
where the time goes in v17:
time: 113 us
  blocking collectives  72.1 us (64%)
  starting transfers between devices  26.3 us (23%)
  waiting for transfers between devices  9.89 us (9%)
  Pallas kernels  3.08 us (3%)
    all_to_all x1, blocking collectives, on_device(): lax.all_to_all(terms, ('batch', 'tensor'), 0, 0, axis_index_groups=pair_g...  29.1 us
    ppermute x2, starting transfers between devices, to_pair(): return lax.ppermute(block, ('batch', 'tensor'), route)  22.9 us
    all_to_all x1, blocking collectives, on_device(): lax.all_to_all(rows, 'batch', 0, 0, axis_index_groups=depth_groups(), til...  21.1 us
    all_to_all x1, blocking collectives, on_device(): both = lax.all_to_all(both, 'tensor', 0, 0, tiled=True)  12.5 us
    ppermute x2, waiting for transfers between devices, to_pair(): return lax.ppermute(block, ('batch', 'tensor'), route)  9.89 us
    all_to_all x1, blocking collectives, on_device(): lax.all_to_all(rows, ('batch', 'tensor'), 0, 0, axis_index_groups=side_gr...  9.42 us
    all_to_all x1, starting transfers between devices, on_device(): lax.all_to_all(copies, 'tensor', 0, 0, tiled=True)[:, :PIECE]  3.41 us
    pallas_call x6, Pallas kernels, kernel_call(): pl.pallas_call(kernel, out_shape=out_shape, in_specs=[smem] * len(scalars...  3.08 us
  transfers between devices with their start and end apart: 3, of which 1 were waited for; matrix products, arithmetic and copies ran while one was open for 0% of the time, Pallas kernels for 0%

profile of v17, /device:TPU:1, one launch (start us, length us, event | category | flops | bytes accessed | tf_op | source)
XLA Modules:
  0.0 113.0 jit_solution(6184149784616902579)
XLA Ops:
  0.0 0.0 copy-start
  0.0 0.0 copy-start.1
  0.0 0.7 broadcast_subtract_fusion
  0.7 0.2 copy-done
  1.0 0.5 fusion.2.part_ref
  1.5 0.0 copy-done.1
  1.5 0.1 shard_map.46
  1.6 0.0 copy-start.2
  1.6 12.5 %all_to_all.25.both_ref = bf16[8,192,128]{2,1,0:T(8,128)(2,1)S(1)} all-to-all(bf16[8,192,128]{2,1,0:T(8,128)(2,1)S(1)} %shard_map.46), channel_id=1, replica_groups=mesh['batch'=64,'tensor'=8] {'tensor'}, dimensions={0} | all-to-all | bytes 786432 | tf_op jit(solution)/shard_map/all_to_all | solution.py:241
  14.1 0.7 shard_map.47
  14.8 3.4 %all-to-all-start.1 = ((bf16[8,128,128]{2,1,0:T(8,128)(2,1)}), bf16[8,128,128]{2,1,0:T(8,128)(2,1)S(1)}, u32[]{:S(2)}, u32[]{:S(2)}) async-start(bf16[8,128,128]{2,1,0:T(8,128)(2,1)} %get-tuple-element.10), calls=%async_computation.1 | async-start | bytes 524288 | tf_op jit(solution)/shard_map/all_to_all | solution.py:244
  18.3 16.6 %collective-permute-start = (bf16[8,128,128]{2,1,0:T(8,128)(2,1)S(1)}, bf16[8,128,128]{2,1,0:T(8,128)(2,1)S(1)}, u32[]{:S(2)}, u32[]{:S(2)}) collective-permute-start(bf16[8,128,128]{2,1,0:T(8,128)(2,1)S(1)} %get-tuple-element.9), channel_id=1, source_target_pairs={{0,128},{1,97},{2,162},{3,67},{4,196},{5,37},{6,230},{7,7},{8,136}... | collective-permute-start | bytes 786440 | tf_op jit(solution)/shard_map/ppermute | solution.py:52
  34.9 0.0 all-to-all-done.1
  34.9 6.3 %collective-permute-start.1 = (bf16[8,64,128]{2,1,0:T(8,128)(2,1)S(1)}, bf16[8,64,128]{2,1,0:T(8,128)(2,1)S(1)}, u32[]{:S(2)}, u32[]{:S(2)}) collective-permute-start(bf16[8,64,128]{2,1,0:T(8,128)(2,1)S(1)} %slice.4), channel_id=1, source_target_pairs={{0,128},{1,97},{2,162},{3,67},{4,196},{5,37},{6,230},{7,7},{8,136}... | collective-permute-start | bytes 393224 | tf_op jit(solution)/shard_map/ppermute | solution.py:52
  41.2 0.0 collective-permute-done.acts_ref
  41.2 9.9 %collective-permute-done.1.picked_ref = bf16[8,64,128]{2,1,0:T(8,128)(2,1)S(1)} collective-permute-done((bf16[8,64,128]{2,1,0:T(8,128)(2,1)S(1)}, bf16[8,64,128]{2,1,0:T(8,128)(2,1)S(1)}, u32[]{:S(2)}, u32[]{:S(2)}) %collective-permute-start.1) | collective-permute-done | bytes 131104 | tf_op jit(solution)/shard_map/ppermute | solution.py:52
  51.1 0.0 copy-done.2
  51.1 0.6 shard_map.48
  51.7 29.1 %all_to_all.26.terms_ref = bf16[64,16,512]{2,1,0:T(8,128)(2,1)S(1)} all-to-all(bf16[64,16,512]{2,1,0:T(8,128)(2,1)S(1)} %get-tuple-element.11), channel_id=1, replica_groups={{0,1,2,3,4,5,6,7,8,9,10,11,12,13,14,15,256,257,258,259,260,261,262,263,..., dimensions={0} | all-to-all | bytes 2097152 | tf_op jit(solution)/shard_map/all_to_all | solution.py:246
  80.9 0.9 shard_map.49
  81.8 21.1 %all_to_all.27.rows_ref = f32[32,1,128]{2,1,0:T(1,128)S(1)} all-to-all(f32[32,1,128]{2,1,0:T(1,128)S(1)} %bitcast.7), channel_id=1, replica_groups={{0,8,16,24,32,40,48,56,64,72,80,88,96,104,112,120,128,136,144,152,160,1..., dimensions={0} | all-to-all | bytes 32768 | tf_op jit(solution)/shard_map/all_to_all | solution.py:250
  102.8 0.1 shard_map.50
  102.9 9.4 %all_to_all.28.rows_ref = f32[16,1,64]{2,1,0:T(1,128)S(1)} all-to-all(f32[16,1,64]{2,1,0:T(1,128)S(1)} %bitcast.8), channel_id=1, replica_groups={{0,1,2,3,4,5,6,7,256,257,258,259,260,261,262,263},{8,9,10,11,12,13,14,1..., dimensions={0} | all-to-all | bytes 8192 | tf_op jit(solution)/shard_map/all_to_all | solution.py:253
  112.3 0.7 shard_map.51
  (1 shorter events, 0.0 us)
Async XLA Ops:
  0.0 1.0 copy-start
  0.0 1.5 %copy-start.1 = (bf16[128,1024]{1,0:T(8,128)(2,1)S(1)}, bf16[128,1024]{1,0:T(8,128)(2,1)}, u32[]{:S(2)}) copy-start(bf16[128,1024]{1,0:T(8,128)(2,1)} %acts_ref.1) | copy-start | bytes 786436
  1.6 49.5 %copy-start.2 = (s32[64]{0:T(128)S(1)}, s32[64]{0:T(128)}, u32[]{:S(2)}) copy-start(s32[64]{0:T(128)} %param.7) | copy-start | bytes 772
  14.8 20.1 %all-to-all-start.1 = ((bf16[8,128,128]{2,1,0:T(8,128)(2,1)}), bf16[8,128,128]{2,1,0:T(8,128)(2,1)S(1)}, u32[]{:S(2)}, u32[]{:S(2)}) async-start(bf16[8,128,128]{2,1,0:T(8,128)(2,1)} %get-tuple-element.10), calls=%async_computation.1 | async-start | bytes 524288 | tf_op jit(solution)/shard_map/all_to_all | solution.py:244
  18.3 23.0 %collective-permute-start = (bf16[8,128,128]{2,1,0:T(8,128)(2,1)S(1)}, bf16[8,128,128]{2,1,0:T(8,128)(2,1)S(1)}, u32[]{:S(2)}, u32[]{:S(2)}) collective-permute-start(bf16[8,128,128]{2,1,0:T(8,128)(2,1)S(1)} %get-tuple-element.9), channel_id=1, source_target_pairs={{0,128},{1,97},{2,162},{3,67},{4,196},{5,37},{6,230},{7,7},{8,136}... | collective-permute-start | bytes 786440 | tf_op jit(solution)/shard_map/ppermute | solution.py:52
  34.9 16.2 %collective-permute-start.1 = (bf16[8,64,128]{2,1,0:T(8,128)(2,1)S(1)}, bf16[8,64,128]{2,1,0:T(8,128)(2,1)S(1)}, u32[]{:S(2)}, u32[]{:S(2)}) collective-permute-start(bf16[8,64,128]{2,1,0:T(8,128)(2,1)S(1)} %slice.4), channel_id=1, source_target_pairs={{0,128},{1,97},{2,162},{3,67},{4,196},{5,37},{6,230},{7,7},{8,136}... | collective-permute-start | bytes 393224 | tf_op jit(solution)/shard_map/ppermute | solution.py:52

commit v18 on v14

--- a/solution.py
+++ b/solution.py
@@ -52,15 +52,19 @@
 
 
 def pair_groups():
+    held_by = [
+        [next(t for t in range(TENSOR) if PAIR_OF[t][k] == pair) for k in range(PAIRS)]
+        for pair in range(PAIRS)
+    ]
     return [
         [
-            batch_index(y, k, r, c) * TENSOR + t
+            batch_index(y, pair, r, c) * TENSOR + held_by[pair][k]
             for r in range(PLACES)
             for y in range(Y_HI)
             for c in range(CORES)
-            for t in range(TENSOR)
+            for k in range(PAIRS)
         ]
-        for k in range(PAIRS)
+        for pair in range(PAIRS)
     ]
 
 
@@ -177,7 +181,7 @@
     return kernel_call(example_grad_kernel, shapes, (acts, picked, assign[None]))
 
 
-def pairs_kernel(pair_ref, terms_ref, out_ref):
+def pairs_kernel(terms_ref, out_ref):
     terms = jnp.swapaxes(terms_ref[...], 0, 1)
     total = jnp.zeros((SEQS, SEQS), jnp.float32)
     for row in range(ROWS):
@@ -185,20 +189,6 @@
             terms[row], terms[row], (((1,), (1,)), ((), ())), preferred_element_type=jnp.float32
         )
     total = total * (1.0 / (float(TOK) * float(D) * float(NSEL)))
-    row = lax.broadcasted_iota(jnp.int32, (SEQS, SEQS), 0)
-    column = lax.broadcasted_iota(jnp.int32, (SEQS, SEQS), 1)
-    held = [chosen_by(pair_ref[0], [PAIR_OF[t].index(k) for k in range(PAIRS)]) for t in range(TENSOR)]
-    from_pair = chosen_by(column % TENSOR, held)
-    turn = (row // PAIRS == column // TENSOR) & (row % PAIRS == from_pair)
-    turn = jnp.where(turn, 1.0, 0.0)
-    for side in range(2):
-        total = lax.dot_general(
-            turn,
-            total,
-            (((1,), (1,)), ((), ())),
-            precision=lax.Precision.HIGHEST,
-            preferred_element_type=jnp.float32,
-        )
     for r in range(PLACES):
         for c in range(CORES):
             starts = [((r * Y_HI + y) * CORES + c) * PAIRS for y in range(Y_HI)]
@@ -206,9 +196,9 @@
             out_ref[:, r, c, 0] = jnp.concatenate(rows, axis=1)
 
 
-def pairs(pair, terms):
+def pairs(terms):
     shape = jax.ShapeDtypeStruct((PAIRS, PLACES, CORES, 1, Y_HI * SEQS), jnp.float32)
-    return kernel_call(pairs_kernel, shape, (terms,), (pair,))
+    return kernel_call(pairs_kernel, shape, (terms,))
 
 
 def side_kernel(rows_ref, out_ref):
@@ -243,7 +233,7 @@
     terms = lax.all_to_all(
         terms, ("batch", "tensor"), 0, 0, axis_index_groups=pair_groups(), tiled=True
     )
-    rows = pairs(pair, terms).reshape(DEPTH, 1, Y_HI * SEQS)
+    rows = pairs(terms).reshape(DEPTH, 1, Y_HI * SEQS)
     rows = lax.all_to_all(rows, "batch", 0, 0, axis_index_groups=depth_groups(), tiled=True)
     shape = jax.ShapeDtypeStruct((Y_HI, TENSOR, 1, SEQS), jnp.float32)
     rows = kernel_call(side_kernel, shape, (rows,)).reshape(Y_HI * TENSOR, 1, SEQS)

time: 110 us -> 110 us (level)
    all_to_all x1, blocking collectives: 17 us -> 18.6 us  [on_device(): lax.all_to_all(rows, 'batch', 0, 0, axis_index_groups=depth_groups(), til...]
where the time goes in v18:
time: 110 us
  blocking collectives  74.7 us (68%)
  starting transfers between devices  20.6 us (19%)
  waiting for transfers between devices  11 us (10%)
  Pallas kernels  2.11 us (2%)
    all_to_all x1, blocking collectives, on_device(): lax.all_to_all(terms, ('batch', 'tensor'), 0, 0, axis_index_groups=pair_g...  26.4 us
    ppermute x2, starting transfers between devices, to_pair(): return lax.ppermute(block, ('batch', 'tensor'), route)  20.6 us
    all_to_all x1, blocking collectives, on_device(): lax.all_to_all(rows, 'batch', 0, 0, axis_index_groups=depth_groups(), til...  18.6 us
    all_to_all x1, blocking collectives, on_device(): both = lax.all_to_all(both, 'tensor', 0, 0, tiled=True)  12.5 us
    ppermute x2, waiting for transfers between devices, to_pair(): return lax.ppermute(block, ('batch', 'tensor'), route)  11 us
    all_to_all x1, blocking collectives, on_device(): lax.all_to_all(rows, ('batch', 'tensor'), 0, 0, axis_index_groups=side_gr...  9.35 us
    all_to_all x1, blocking collectives, on_device(): picked = to_pair(lax.all_to_all(copies, 'tensor', 0, 0, tiled=True))  7.83 us
  transfers between devices with their start and end apart: 2, of which 1 were waited for; matrix products, arithmetic and copies ran while one was open for 0% of the time, Pallas kernels for 0%

profile of v18, /device:TPU:1, one launch (start us, length us, event | category | flops | bytes accessed | tf_op | source)
XLA Modules:
  0.0 110.0 jit_solution(4947443785709460534)
XLA Ops:
  0.0 0.0 copy-start
  0.0 0.0 copy-start.1
  0.0 0.7 broadcast_subtract_fusion
  0.7 0.2 copy-done
  1.0 0.5 fusion.2.part_ref
  1.5 0.0 copy-done.1
  1.5 0.0 copy-start.2
  1.5 0.1 shard_map.46
  1.6 12.5 %all_to_all.25.both_ref = bf16[8,192,128]{2,1,0:T(8,128)(2,1)S(1)} all-to-all(bf16[8,192,128]{2,1,0:T(8,128)(2,1)S(1)} %shard_map.46), channel_id=1, replica_groups=mesh['batch'=64,'tensor'=8] {'tensor'}, dimensions={0} | all-to-all | bytes 786432 | tf_op jit(solution)/shard_map/all_to_all | solution.py:228
  14.1 16.6 %collective-permute-start = (bf16[8,128,128]{2,1,0:T(8,128)(2,1)S(1)}, bf16[8,128,128]{2,1,0:T(8,128)(2,1)S(1)}, u32[]{:S(2)}, u32[]{:S(2)}) collective-permute-start(bf16[8,128,128]{2,1,0:T(8,128)(2,1)S(1)} %get-tuple-element.9), channel_id=1, source_target_pairs={{0,128},{1,97},{2,162},{3,67},{4,196},{5,37},{6,230},{7,7},{8,136}... | collective-permute-start | bytes 786440 | tf_op jit(solution)/shard_map/ppermute | solution.py:51
  30.8 7.8 %all_to_all.26 = bf16[8,64,128]{2,1,0:T(8,128)(2,1)S(1)} all-to-all(bf16[8,64,128]{2,1,0:T(8,128)(2,1)S(1)} %get-tuple-element.10), channel_id=1, replica_groups=mesh['batch'=64,'tensor'=8] {'tensor'}, dimensions={0} | all-to-all | bytes 262144 | tf_op jit(solution)/shard_map/all_to_all | solution.py:231
  38.6 3.9 %collective-permute-start.1 = (bf16[8,64,128]{2,1,0:T(8,128)(2,1)S(1)}, bf16[8,64,128]{2,1,0:T(8,128)(2,1)S(1)}, u32[]{:S(2)}, u32[]{:S(2)}) collective-permute-start(bf16[8,64,128]{2,1,0:T(8,128)(2,1)S(1)} %all_to_all.26), channel_id=1, source_target_pairs={{0,128},{1,97},{2,162},{3,67},{4,196},{5,37},{6,230},{7,7},{8,136}... | collective-permute-start | bytes 393224 | tf_op jit(solution)/shard_map/ppermute | solution.py:51
  42.6 11.0 %collective-permute-done.1.picked_ref = bf16[8,64,128]{2,1,0:T(8,128)(2,1)S(1)} collective-permute-done((bf16[8,64,128]{2,1,0:T(8,128)(2,1)S(1)}, bf16[8,64,128]{2,1,0:T(8,128)(2,1)S(1)}, u32[]{:S(2)}, u32[]{:S(2)}) %collective-permute-start.1) | collective-permute-done | bytes 131104 | tf_op jit(solution)/shard_map/ppermute | solution.py:51
  53.6 0.0 collective-permute-done.acts_ref
  53.6 0.0 copy-done.2
  53.6 0.6 shard_map.48
  54.2 26.4 %all_to_all.27.terms_ref = bf16[64,16,512]{2,1,0:T(8,128)(2,1)S(1)} all-to-all(bf16[64,16,512]{2,1,0:T(8,128)(2,1)S(1)} %get-tuple-element.11), channel_id=1, replica_groups={{7,2,6,4,0,5,1,3,15,10,14,12,8,13,9,11,263,258,262,260,256,261,257,259,..., dimensions={0} | all-to-all | bytes 2097152 | tf_op jit(solution)/shard_map/all_to_all | solution.py:233
  80.6 0.6 shard_map.49
  81.3 18.6 %all_to_all.28.rows_ref = f32[32,1,128]{2,1,0:T(1,128)S(1)} all-to-all(f32[32,1,128]{2,1,0:T(1,128)S(1)} %bitcast.7), channel_id=1, replica_groups={{0,8,16,24,32,40,48,56,64,72,80,88,96,104,112,120,128,136,144,152,160,1..., dimensions={0} | all-to-all | bytes 32768 | tf_op jit(solution)/shard_map/all_to_all | solution.py:237
  99.8 0.1 shard_map.50
  100.0 9.3 %all_to_all.29.rows_ref = f32[16,1,64]{2,1,0:T(1,128)S(1)} all-to-all(f32[16,1,64]{2,1,0:T(1,128)S(1)} %bitcast.8), channel_id=1, replica_groups={{0,1,2,3,4,5,6,7,256,257,258,259,260,261,262,263},{8,9,10,11,12,13,14,1..., dimensions={0} | all-to-all | bytes 8192 | tf_op jit(solution)/shard_map/all_to_all | solution.py:240
  109.3 0.7 shard_map.51
  (1 shorter events, 0.0 us)
Async XLA Ops:
  0.0 1.0 copy-start
  0.0 1.5 %copy-start.1 = (bf16[128,1024]{1,0:T(8,128)(2,1)S(1)}, bf16[128,1024]{1,0:T(8,128)(2,1)}, u32[]{:S(2)}) copy-start(bf16[128,1024]{1,0:T(8,128)(2,1)} %acts_ref.1) | copy-start | bytes 786436
  1.5 52.1 %copy-start.2 = (s32[64]{0:T(128)S(1)}, s32[64]{0:T(128)}, u32[]{:S(2)}) copy-start(s32[64]{0:T(128)} %param.7) | copy-start | bytes 772
  14.1 39.5 %collective-permute-start = (bf16[8,128,128]{2,1,0:T(8,128)(2,1)S(1)}, bf16[8,128,128]{2,1,0:T(8,128)(2,1)S(1)}, u32[]{:S(2)}, u32[]{:S(2)}) collective-permute-start(bf16[8,128,128]{2,1,0:T(8,128)(2,1)S(1)} %get-tuple-element.9), channel_id=1, source_target_pairs={{0,128},{1,97},{2,162},{3,67},{4,196},{5,37},{6,230},{7,7},{8,136}... | collective-permute-start | bytes 786440 | tf_op jit(solution)/shard_map/ppermute | solution.py:51
  38.6 15.0 %collective-permute-start.1 = (bf16[8,64,128]{2,1,0:T(8,128)(2,1)S(1)}, bf16[8,64,128]{2,1,0:T(8,128)(2,1)S(1)}, u32[]{:S(2)}, u32[]{:S(2)}) collective-permute-start(bf16[8,64,128]{2,1,0:T(8,128)(2,1)S(1)} %all_to_all.26), channel_id=1, source_target_pairs={{0,128},{1,97},{2,162},{3,67},{4,196},{5,37},{6,230},{7,7},{8,136}... | collective-permute-start | bytes 393224 | tf_op jit(solution)/shard_map/ppermute | solution.py:51

commit v19 on v18

--- a/solution.py
+++ b/solution.py
@@ -39,9 +39,16 @@
     return ((y_hi * PAIRS + pair) * PLACES + place) * CORES + core
 
 
+def place_of(t, k, place):
+    return 1 - place if (PAIR_OF[t][k] - k) % PAIRS == PAIRS // 2 else place
+
+
 def to_pair(block):
     route = [
-        (batch_index(y, k, r, c) * TENSOR + t, batch_index(y, PAIR_OF[t][k], r, c) * TENSOR + t)
+        (
+            batch_index(y, k, r, c) * TENSOR + t,
+            batch_index(y, PAIR_OF[t][k], place_of(t, k, r), c) * TENSOR + t,
+        )
         for y in range(Y_HI)
         for k in range(PAIRS)
         for r in range(PLACES)
@@ -58,7 +65,7 @@
     ]
     return [
         [
-            batch_index(y, pair, r, c) * TENSOR + held_by[pair][k]
+            batch_index(y, pair, place_of(held_by[pair][k], k, r), c) * TENSOR + held_by[pair][k]
             for r in range(PLACES)
             for y in range(Y_HI)
             for c in range(CORES)

time: 110 us -> 110 us (level)
  no operation moved by 1% of the time
where the time goes in v19:
time: 110 us; the launch traced here: 109 us
  blocking collectives  74.6 us (68%)
  starting transfers between devices  20.1 us (18%)
  waiting for transfers between devices  11 us (10%)
  Pallas kernels  2.1 us (2%)
    all_to_all x1, blocking collectives, on_device(): lax.all_to_all(terms, ('batch', 'tensor'), 0, 0, axis_index_groups=pair_g...  26.2 us
    ppermute x2, starting transfers between devices, to_pair(): return lax.ppermute(block, ('batch', 'tensor'), route)  20.1 us
    all_to_all x1, blocking collectives, on_device(): lax.all_to_all(rows, 'batch', 0, 0, axis_index_groups=depth_groups(), til...  18.4 us
    all_to_all x1, blocking collectives, on_device(): both = lax.all_to_all(both, 'tensor', 0, 0, tiled=True)  12.5 us
    ppermute x2, waiting for transfers between devices, to_pair(): return lax.ppermute(block, ('batch', 'tensor'), route)  11 us
    all_to_all x1, blocking collectives, on_device(): lax.all_to_all(rows, ('batch', 'tensor'), 0, 0, axis_index_groups=side_gr...  9.66 us
    all_to_all x1, blocking collectives, on_device(): picked = to_pair(lax.all_to_all(copies, 'tensor', 0, 0, tiled=True))  7.83 us
  transfers between devices with their start and end apart: 2, of which 1 were waited for; matrix products, arithmetic and copies ran while one was open for 0% of the time, Pallas kernels for 0%

profile of v19, /device:TPU:1, one launch (start us, length us, event | category | flops | bytes accessed | tf_op | source)
XLA Modules:
  0.0 109.3 jit_solution(2544080097399221919)
XLA Ops:
  0.0 0.0 copy-start
  0.0 0.0 copy-start.1
  0.0 0.7 broadcast_subtract_fusion
  0.7 0.2 copy-done
  1.0 0.5 fusion.2.part_ref
  1.5 0.0 copy-done.1
  1.5 0.0 copy-start.2
  1.5 0.1 shard_map.46
  1.6 12.5 %all_to_all.25.both_ref = bf16[8,192,128]{2,1,0:T(8,128)(2,1)S(1)} all-to-all(bf16[8,192,128]{2,1,0:T(8,128)(2,1)S(1)} %shard_map.46), channel_id=1, replica_groups=mesh['batch'=64,'tensor'=8] {'tensor'}, dimensions={0} | all-to-all | bytes 786432 | tf_op jit(solution)/shard_map/all_to_all | solution.py:235
  14.1 16.2 %collective-permute-start = (bf16[8,128,128]{2,1,0:T(8,128)(2,1)S(1)}, bf16[8,128,128]{2,1,0:T(8,128)(2,1)S(1)}, u32[]{:S(2)}, u32[]{:S(2)}) collective-permute-start(bf16[8,128,128]{2,1,0:T(8,128)(2,1)S(1)} %get-tuple-element.9), channel_id=1, source_target_pairs={{0,144},{1,97},{2,162},{3,67},{4,196},{5,37},{6,230},{7,7},{8,152}... | collective-permute-start | bytes 786440 | tf_op jit(solution)/shard_map/ppermute | solution.py:58
  30.3 7.8 %all_to_all.26 = bf16[8,64,128]{2,1,0:T(8,128)(2,1)S(1)} all-to-all(bf16[8,64,128]{2,1,0:T(8,128)(2,1)S(1)} %get-tuple-element.10), channel_id=1, replica_groups=mesh['batch'=64,'tensor'=8] {'tensor'}, dimensions={0} | all-to-all | bytes 262144 | tf_op jit(solution)/shard_map/all_to_all | solution.py:238
  38.2 3.9 %collective-permute-start.1 = (bf16[8,64,128]{2,1,0:T(8,128)(2,1)S(1)}, bf16[8,64,128]{2,1,0:T(8,128)(2,1)S(1)}, u32[]{:S(2)}, u32[]{:S(2)}) collective-permute-start(bf16[8,64,128]{2,1,0:T(8,128)(2,1)S(1)} %all_to_all.26), channel_id=1, source_target_pairs={{0,144},{1,97},{2,162},{3,67},{4,196},{5,37},{6,230},{7,7},{8,152}... | collective-permute-start | bytes 393224 | tf_op jit(solution)/shard_map/ppermute | solution.py:58
  42.1 11.0 %collective-permute-done.1.picked_ref = bf16[8,64,128]{2,1,0:T(8,128)(2,1)S(1)} collective-permute-done((bf16[8,64,128]{2,1,0:T(8,128)(2,1)S(1)}, bf16[8,64,128]{2,1,0:T(8,128)(2,1)S(1)}, u32[]{:S(2)}, u32[]{:S(2)}) %collective-permute-start.1) | collective-permute-done | bytes 131104 | tf_op jit(solution)/shard_map/ppermute | solution.py:58
  53.1 0.0 collective-permute-done.acts_ref
  53.1 0.0 copy-done.2
  53.1 0.6 shard_map.48
  53.7 26.2 %all_to_all.27.terms_ref = bf16[64,16,512]{2,1,0:T(8,128)(2,1)S(1)} all-to-all(bf16[64,16,512]{2,1,0:T(8,128)(2,1)S(1)} %get-tuple-element.11), channel_id=1, replica_groups={{7,2,6,4,16,5,1,3,15,10,14,12,24,13,9,11,263,258,262,260,272,261,257,25..., dimensions={0} | all-to-all | bytes 2097152 | tf_op jit(solution)/shard_map/all_to_all | solution.py:240
  79.9 0.6 shard_map.49
  80.5 18.4 %all_to_all.28.rows_ref = f32[32,1,128]{2,1,0:T(1,128)S(1)} all-to-all(f32[32,1,128]{2,1,0:T(1,128)S(1)} %bitcast.7), channel_id=1, replica_groups={{0,8,16,24,32,40,48,56,64,72,80,88,96,104,112,120,128,136,144,152,160,1..., dimensions={0} | all-to-all | bytes 32768 | tf_op jit(solution)/shard_map/all_to_all | solution.py:244
  98.9 0.1 shard_map.50
  99.0 9.7 %all_to_all.29.rows_ref = f32[16,1,64]{2,1,0:T(1,128)S(1)} all-to-all(f32[16,1,64]{2,1,0:T(1,128)S(1)} %bitcast.8), channel_id=1, replica_groups={{0,1,2,3,4,5,6,7,256,257,258,259,260,261,262,263},{8,9,10,11,12,13,14,1..., dimensions={0} | all-to-all | bytes 8192 | tf_op jit(solution)/shard_map/all_to_all | solution.py:247
  108.7 0.7 shard_map.51
  (1 shorter events, 0.0 us)
Async XLA Ops:
  0.0 1.0 copy-start
  0.0 1.5 %copy-start.1 = (bf16[128,1024]{1,0:T(8,128)(2,1)S(1)}, bf16[128,1024]{1,0:T(8,128)(2,1)}, u32[]{:S(2)}) copy-start(bf16[128,1024]{1,0:T(8,128)(2,1)} %acts_ref.1) | copy-start | bytes 786436
  1.5 51.6 %copy-start.2 = (s32[64]{0:T(128)S(1)}, s32[64]{0:T(128)}, u32[]{:S(2)}) copy-start(s32[64]{0:T(128)} %param.7) | copy-start | bytes 772
  14.1 38.9 %collective-permute-start = (bf16[8,128,128]{2,1,0:T(8,128)(2,1)S(1)}, bf16[8,128,128]{2,1,0:T(8,128)(2,1)S(1)}, u32[]{:S(2)}, u32[]{:S(2)}) collective-permute-start(bf16[8,128,128]{2,1,0:T(8,128)(2,1)S(1)} %get-tuple-element.9), channel_id=1, source_target_pairs={{0,144},{1,97},{2,162},{3,67},{4,196},{5,37},{6,230},{7,7},{8,152}... | collective-permute-start | bytes 786440 | tf_op jit(solution)/shard_map/ppermute | solution.py:58
  38.2 14.9 %collective-permute-start.1 = (bf16[8,64,128]{2,1,0:T(8,128)(2,1)S(1)}, bf16[8,64,128]{2,1,0:T(8,128)(2,1)S(1)}, u32[]{:S(2)}, u32[]{:S(2)}) collective-permute-start(bf16[8,64,128]{2,1,0:T(8,128)(2,1)S(1)} %all_to_all.26), channel_id=1, source_target_pairs={{0,144},{1,97},{2,162},{3,67},{4,196},{5,37},{6,230},{7,7},{8,152}... | collective-permute-start | bytes 393224 | tf_op jit(solution)/shard_map/ppermute | solution.py:58
